TPU v7x, 32 devices: a whole 2x2x4 slice. The times are simulated.
32 devices in a mesh: wrap: 4 (over z), normal: 8 (over y, x, core).
Axes of the slice: x: 2, y: 2, z: 4, core: 2. Of those that a mesh axis runs over, the one named last changes fastest.
Arguments:
- state: float32 [5, 4, 64, 512], P(None, None, 'normal', 'wrap'), may hold values from -2 to 3, as said below
- metrics: float32 [4, 4, 64, 512], P(None, None, 'normal', 'wrap'), may hold values from 0.5 to 1.5
- time_step: float32 [4, 64, 512], P(None, 'normal', 'wrap'), may hold values from 40 to 400
- dissipation: float32 [2, 4, 64, 512], P(None, None, 'normal', 'wrap'), may hold values from 0.05 to 0.5
Outputs:
- increment: float32 [5, 4, 64, 512], P(None, None, 'normal', 'wrap')
Inputs may be any that keep to these rules, and one draw needn't show every extreme that they name: `state`: component 0 (density) lies in 0.7 to 1.4 and component 4 (energy) in 2 to 3; components 1 to 3 are momenta.
All inputs are finite; a program needn't handle non-finite values. Where the computation divides by a largest or mean magnitude, that divisor is 1e-20 or more.
Results may differ from a plain program's by a relative error of at most 0.00017.
Values sent between devices are 32-bit elements; how exact they have to be, the bound alone decides.
No kernel may reach another device: no remote copies, remote signals or barrier semaphores. Data moves between devices by JAX's collectives and lax.ppermute only.
A program may use at most 128 MiB of HBM per device.

v0:
```python
import jax
import jax.numpy as jnp
from jax import lax
from jax.sharding import PartitionSpec as P

GAMMA = 1.4


def extended_2(cells, sides, width, closed):
    for axis, dim in sides:
        count = lax.axis_size(axis)
        ends = count if closed else count - 1
        head = lax.slice_in_dim(cells, 0, width, axis=dim)
        tail = lax.slice_in_dim(cells, cells.shape[dim] - width, cells.shape[dim], axis=dim)
        cells = jnp.concatenate(
            [
                lax.ppermute(tail, axis, [(i, (i + 1) % count) for i in range(ends)]),
                cells,
                lax.ppermute(head, axis, [((i + 1) % count, i) for i in range(ends)]),
            ],
            axis=dim,
        )
    return cells


def passed_along(value, axis, steps):
    count = lax.axis_size(axis)
    pairs = [(source, (source + steps) % count) for source in range(count)]
    return lax.ppermute(value, axis, pairs)


def shifted(shard, axis, by):
    size = lax.axis_size(axis)
    pairs = [(i, i + by) for i in range(size) if 0 <= i + by < size]
    return lax.ppermute(shard, axis, pairs)


def flux_jacobian(face_state, metric_x, metric_y):
    density = face_state[0]
    vel_u = face_state[1] / density
    vel_v = face_state[2] / density
    vel_w = face_state[3] / density
    energy = face_state[4] / density
    gamma_less = GAMMA - 1.0
    contra = metric_x * vel_u + metric_y * vel_v
    kinetic = 0.5 * gamma_less * (vel_u * vel_u + vel_v * vel_v + vel_w * vel_w)
    blank = jnp.zeros_like(density)
    enthalpy = GAMMA * energy - kinetic
    entries = [
        [blank, metric_x, metric_y, blank, blank],
        [
            metric_x * kinetic - vel_u * contra,
            contra - (GAMMA - 2.0) * metric_x * vel_u,
            metric_y * vel_u - gamma_less * metric_x * vel_v,
            -gamma_less * metric_x * vel_w,
            gamma_less * metric_x,
        ],
        [
            metric_y * kinetic - vel_v * contra,
            metric_x * vel_v - gamma_less * metric_y * vel_u,
            contra - (GAMMA - 2.0) * metric_y * vel_v,
            -gamma_less * metric_y * vel_w,
            gamma_less * metric_y,
        ],
        [-vel_w * contra, metric_x * vel_w, metric_y * vel_w, contra, blank],
        [
            contra * (2.0 * kinetic - GAMMA * energy),
            metric_x * enthalpy - gamma_less * vel_u * contra,
            metric_y * enthalpy - gamma_less * vel_v * contra,
            -gamma_less * vel_w * contra,
            GAMMA * contra,
        ],
    ]
    return jnp.stack([jnp.stack(entry_row) for entry_row in entries])


def block_product(left, right):
    return jnp.sum(left[:, :, None] * right[None, :, :], axis=1)


def block_apply(matrix, vector):
    return jnp.sum(matrix * vector[None], axis=1)


def eye_like(matrix):
    trailing = len(matrix.shape) - 2
    return jnp.eye(5, dtype=jnp.float32).reshape((5, 5) + (1,) * trailing)


def invert_small(matrix):
    trailing = len(matrix.shape) - 2
    identity = jnp.broadcast_to(eye_like(matrix), matrix.shape)
    working = jnp.concatenate([matrix, identity], axis=1)
    row_ids = jnp.arange(5).reshape((5,) + (1,) * trailing)
    for column in range(5):
        magnitude = jnp.where(row_ids >= column, jnp.abs(working[:, column]), -1.0)
        chosen_row = jnp.argmax(magnitude, axis=0)
        selector = (row_ids == chosen_row[None]).astype(jnp.float32)
        chosen = jnp.sum(selector[:, None] * working, axis=0)
        current = working[column]
        working = working + selector[:, None] * (current - chosen)[None]
        pivot_row = chosen / chosen[column]
        working = working - working[:, column][:, None] * pivot_row[None]
        working = working.at[column].set(pivot_row)
    return working[:, 5:]


def face_terms(extended, metric_at, spread_at):
    state = extended[0:5]
    face_state = 0.5 * (state[:, :-1] + state[:, 1:])
    metric = extended[metric_at : metric_at + 2]
    face_metric = 0.5 * (metric[:, :-1] + metric[:, 1:])
    step_size = extended[9, :-1]
    spread = extended[spread_at, :-1]
    jacobian = flux_jacobian(face_state, face_metric[0], face_metric[1])
    row_scale = jnp.max(jnp.sum(jnp.abs(jacobian), axis=1), axis=0)
    normed = jacobian / row_scale
    flipped = jnp.swapaxes(normed, 0, 1)
    identity = eye_like(normed)
    convect = step_size * (0.5 * (normed + flipped))
    damping = step_size * spread * (0.5 * (identity + block_product(flipped, normed)))
    face_flux = block_apply(convect, face_state) - block_apply(
        damping, state[:, 1:] - state[:, :-1]
    )
    residual = -(face_flux[:, 1:] - face_flux[:, :-1])
    lower = -0.5 * convect[:, :, :-1] - damping[:, :, :-1]
    middle = identity + damping[:, :, :-1] + damping[:, :, 1:]
    upper = 0.5 * convect[:, :, 1:] - damping[:, :, 1:]
    return (residual, lower, middle, upper)


def cell_forms(lower, middle, upper, rhs):
    inverse = invert_small(middle)
    return (
        block_apply(inverse, rhs),
        -block_product(inverse, lower),
        -block_product(inverse, upper),
    )


def join_rows(left_g, left_y, left_z, right_g, right_y, right_z):
    coupling = invert_small(eye_like(left_z) - block_product(left_z, right_y))
    inner_g = block_apply(coupling, left_g + block_apply(left_z, right_g))
    inner_y = block_product(coupling, left_y)
    inner_z = block_product(coupling, block_product(left_z, right_z))
    outer_g = right_g + block_apply(right_y, inner_g)
    outer_y = block_product(right_y, inner_y)
    outer_z = right_z + block_product(right_y, inner_z)
    return ((inner_g, inner_y, inner_z), (outer_g, outer_y, outer_z))


def segment_forms(baseline, from_left, from_right):
    cell_count = baseline.shape[1]
    line_count = baseline.shape[2]
    run_length = 1
    while run_length < cell_count:
        pair_count = cell_count // (2 * run_length)

        def halves(array):
            leading = array.shape[:-2]
            shaped = array.reshape(leading + (pair_count, 2, run_length, line_count))
            return (shaped[..., 0, :, :], shaped[..., 1, :, :])

        base_left, base_right = halves(baseline)
        fromleft_l, fromleft_r = halves(from_left)
        fromright_l, fromright_r = halves(from_right)
        edge = run_length - 1
        inner, outer = join_rows(
            base_left[..., edge : edge + 1, :],
            fromleft_l[..., edge : edge + 1, :],
            fromright_l[..., edge : edge + 1, :],
            base_right[..., 0:1, :],
            fromleft_r[..., 0:1, :],
            fromright_r[..., 0:1, :],
        )
        new_base_l = base_left + block_apply(fromright_l, outer[0])
        new_left_l = fromleft_l + block_product(fromright_l, outer[1])
        new_right_l = block_product(fromright_l, outer[2])
        new_base_r = base_right + block_apply(fromleft_r, inner[0])
        new_left_r = block_product(fromleft_r, inner[1])
        new_right_r = fromright_r + block_product(fromleft_r, inner[2])

        def rejoin(left_half, right_half):
            stacked = jnp.stack([left_half, right_half], axis=-3)
            return stacked.reshape(left_half.shape[:-3] + (cell_count, line_count))

        baseline = rejoin(new_base_l, new_base_r)
        from_left = rejoin(new_left_l, new_left_r)
        from_right = rejoin(new_right_l, new_right_r)
        run_length = run_length * 2
    return (baseline, from_left, from_right)


def pack_ends(baseline, from_left, from_right):
    line_count = baseline.shape[-1]
    return jnp.concatenate(
        [
            baseline[:, 0],
            from_left[:, :, 0].reshape(25, line_count),
            from_right[:, :, 0].reshape(25, line_count),
            baseline[:, -1],
            from_left[:, :, -1].reshape(25, line_count),
            from_right[:, :, -1].reshape(25, line_count),
        ],
        axis=0,
    )


def unpack_ends(packed):
    line_count = packed.shape[-1]
    return (
        packed[0:5],
        packed[5:30].reshape(5, 5, line_count),
        packed[30:55].reshape(5, 5, line_count),
        packed[55:60],
        packed[60:85].reshape(5, 5, line_count),
        packed[85:110].reshape(5, 5, line_count),
    )


def merge_full(left, right):
    lf_base, lf_left, lf_right, ll_base, ll_left, ll_right = unpack_ends(left)
    rf_base, rf_left, rf_right, rl_base, rl_left, rl_right = unpack_ends(right)
    inner, outer = join_rows(ll_base, ll_left, ll_right, rf_base, rf_left, rf_right)
    packed = jnp.concatenate(
        [
            lf_base + block_apply(lf_right, outer[0]),
            (lf_left + block_product(lf_right, outer[1])).reshape(25, -1),
            block_product(lf_right, outer[2]).reshape(25, -1),
            rl_base + block_apply(rl_left, inner[0]),
            block_product(rl_left, inner[1]).reshape(25, -1),
            (rl_right + block_product(rl_left, inner[2])).reshape(25, -1),
        ],
        axis=0,
    )
    return (packed, inner, outer)


def merge_ends(left, right):
    return merge_full(left, right)[0]


def cycle_close(own, rest):
    composite, inner, outer = merge_full(own, rest)
    cf_base, cf_left, cf_right, cl_base, cl_left, cl_right = unpack_ends(composite)
    identity = eye_like(cl_left)
    back_inverse = invert_small(identity - cl_left)
    reduced = identity - cf_right - block_product(cf_left, block_product(back_inverse, cl_right))
    first_val = block_apply(
        invert_small(reduced), cf_base + block_apply(cf_left, block_apply(back_inverse, cl_base))
    )
    left_val = block_apply(back_inverse, cl_base + block_apply(cl_right, first_val))
    right_val = outer[0] + block_apply(outer[1], left_val) + block_apply(outer[2], first_val)
    return (left_val, right_val)


def open_close(below, own, above):
    joined, inner_a, outer_a = merge_full(below, own)
    whole, inner_b, outer_b = merge_full(joined, above)
    right_val = outer_b[0]
    left_val = inner_a[0] + block_apply(inner_a[2], right_val)
    return (left_val, right_val)


def substitute(baseline, from_left, from_right, left_val, right_val):
    return (
        baseline
        + block_apply(from_left, left_val[:, None])
        + block_apply(from_right, right_val[:, None])
    )


def swap_layout(array, span_count):
    first_len = array.shape[1]
    other_len = array.shape[2] // span_count
    shaped = array.reshape(array.shape[0], first_len, span_count, other_len)
    return jnp.transpose(shaped, (0, 3, 2, 1)).reshape(
        array.shape[0], other_len, span_count * first_len
    )


def on_device(state, metrics, time_step, dissipation):
    span_count = state.shape[1]
    eta_count = state.shape[2]
    xi_count = state.shape[3]
    cells = jnp.concatenate([state, metrics, time_step[None], dissipation], axis=0)
    wrapped = extended_2(cells, (("wrap", 3),), 1, True)
    walled = extended_2(cells, (("normal", 2),), 1, False)
    cycle_ext = jnp.transpose(wrapped, (0, 3, 1, 2)).reshape(
        12, xi_count + 2, span_count * eta_count
    )
    wall_ext = jnp.transpose(walled, (0, 2, 1, 3)).reshape(12, eta_count + 2, span_count * xi_count)
    wall_res, wall_low, wall_mid, wall_upp = face_terms(wall_ext, 7, 11)
    cycle_res, cycle_low, cycle_mid, cycle_upp = face_terms(cycle_ext, 5, 10)
    total = cycle_res + swap_layout(wall_res, span_count)
    baseline, from_left, from_right = cell_forms(cycle_low, cycle_mid, cycle_upp, total)
    baseline, from_left, from_right = segment_forms(baseline, from_left, from_right)
    own = pack_ends(baseline, from_left, from_right)

    def cycle_step(step_index, carry):
        held, moved = carry
        moved = passed_along(held, "wrap", 1)
        return (merge_ends(moved, own), moved)

    unused, rest = lax.fori_loop(0, lax.axis_size("wrap") - 1, cycle_step, (own, own))
    left_val, right_val = cycle_close(own, rest)
    swept = substitute(baseline, from_left, from_right, left_val, right_val)
    swept_eta = swap_layout(swept, span_count)
    baseline, from_left, from_right = cell_forms(wall_low, wall_mid, wall_upp, swept_eta)
    baseline, from_left, from_right = segment_forms(baseline, from_left, from_right)
    own_eta = pack_ends(baseline, from_left, from_right)

    def rise_step(step_index, carry):
        held, moved = carry
        moved = shifted(held, "normal", 1)
        return (merge_ends(moved, own_eta), moved)

    def fall_step(step_index, carry):
        held, moved = carry
        moved = shifted(held, "normal", -1)
        return (merge_ends(own_eta, moved), moved)

    unused_rise, below = lax.fori_loop(
        0, lax.axis_size("normal") - 1, rise_step, (own_eta, own_eta)
    )
    unused_fall, above = lax.fori_loop(
        0, lax.axis_size("normal") - 1, fall_step, (own_eta, own_eta)
    )
    left_val, right_val = open_close(below, own_eta, above)
    field = substitute(baseline, from_left, from_right, left_val, right_val)
    return jnp.transpose(field.reshape(5, eta_count, span_count, xi_count), (0, 2, 1, 3))


def solution(mesh):
    placed = (
        P(None, None, "normal", "wrap"),
        P(None, None, "normal", "wrap"),
        P(None, "normal", "wrap"),
        P(None, None, "normal", "wrap"),
    )
    return jax.shard_map(
        on_device,
        mesh=mesh,
        in_specs=placed,
        out_specs=P(None, None, "normal", "wrap"),
        check_vma=False,
    )
```

profile of v0, /device:TPU:3, one launch (start us, length us, event | category | flops | bytes accessed | tf_op | source)
XLA Modules:
  0.0 583.8 jit_solution(11757585280860126103)
XLA Ops:
  198.1 31.1 %while.148 = (s32[]{:T(128)}, f32[110,32]{0,1:T(8,128)S(1)}, f32[110,32]{1,0:T(8,128)}, f32[5,5,1,32]{3,1,0,2:T(8,128)S(1)}, f32[5,1,32]{2,0,1:T(8,128)S(1)}, /*...) while((s32[]{:T(128)}, f32[110,32]{0,1:T(8,128)S(1)}, ...), condition=%wide.wide.region_231.232_spmd, body=%wide.wide.region_205.231_spmd.sunk | while | flops 164232 | bytes 755405 | solution.py:305
  306.8 151.6 %while.149 = (s32[]{:T(128)}, f32[110,512]{1,0:T(8,128)}, f32[110,512]{1,0:T(8,128)}, f32[5,5,1,512]{3,1,0,2:T(8,128)S(1)}, f32[5,1,512]{2,0,1:T(8,128)S(1)}, /*...) while((s32[]{:T(128)}, f32[110,512]{1,0:T(8,128)}, ...), condition=%wide.wide.region_389.390_spmd, body=%wide.wide.region_363.389_spmd.sunk | while | flops 2626632 | bytes 10163725 | solution.py:323
  306.8 6.7 %collective-permute-start.1 = (f32[110,512]{1,0:T(8,128)}, f32[110,512]{1,0:T(8,128)S(1)}, u32[]{:S(2)}, u32[]{:S(2)}) collective-permute-start(f32[110,512]{1,0:T(8,128)} %get-tuple-element.3490), channel_id=1, source_target_pairs={{0,1},{1,2},{2,3},{3,4},{4,5},{5,6},{6,7},{8,9},{9,10},{10,11},{11... | collective-permute-start | bytes 675848 | tf_op jit(solution)/shard_map/while/body/eval_jaxpr/ppermute | solution.py:35
  322.1 7.7 %concatenate.659 = f32[110,512]{1,0:T(8,128)} concatenate(f32[5,512]{1,0:T(8,128)S(1)} %slice_add_fusion.50, f32[25,512]{1,0:T(8,128)S(1)} %slice_add_fusion.51, f32[25,512]{1,0:T(8,128)S(1)} %reshape.13054, f32[5,512]{1,0:T(8,128)S(1)} %add.2246, f32[25,512]{1,0:T(8,128)S(1)} %reshape.13055, f32[25,512]{1,0:T(8,128)S(1)} %add.2247), dimensions={0} | concatenate | bytes 450560 | tf_op jit(solution)/shard_map/while/body/eval_jaxpr/concatenate | solution.py:225
  329.7 5.2 collective-permute-start.1
  343.5 7.7 %concatenate.659 = f32[110,512]{1,0:T(8,128)} concatenate(f32[5,512]{1,0:T(8,128)S(1)} %slice_add_fusion.50, f32[25,512]{1,0:T(8,128)S(1)} %slice_add_fusion.51, f32[25,512]{1,0:T(8,128)S(1)} %reshape.13054, f32[5,512]{1,0:T(8,128)S(1)} %add.2246, f32[25,512]{1,0:T(8,128)S(1)} %reshape.13055, f32[25,512]{1,0:T(8,128)S(1)} %add.2247), dimensions={0} | concatenate | bytes 450560 | tf_op jit(solution)/shard_map/while/body/eval_jaxpr/concatenate | solution.py:225
  351.2 5.2 collective-permute-start.1
  364.9 7.7 %concatenate.659 = f32[110,512]{1,0:T(8,128)} concatenate(f32[5,512]{1,0:T(8,128)S(1)} %slice_add_fusion.50, f32[25,512]{1,0:T(8,128)S(1)} %slice_add_fusion.51, f32[25,512]{1,0:T(8,128)S(1)} %reshape.13054, f32[5,512]{1,0:T(8,128)S(1)} %add.2246, f32[25,512]{1,0:T(8,128)S(1)} %reshape.13055, f32[25,512]{1,0:T(8,128)S(1)} %add.2247), dimensions={0} | concatenate | bytes 450560 | tf_op jit(solution)/shard_map/while/body/eval_jaxpr/concatenate | solution.py:225
  372.6 5.2 collective-permute-start.1
  386.4 7.7 %concatenate.659 = f32[110,512]{1,0:T(8,128)} concatenate(f32[5,512]{1,0:T(8,128)S(1)} %slice_add_fusion.50, f32[25,512]{1,0:T(8,128)S(1)} %slice_add_fusion.51, f32[25,512]{1,0:T(8,128)S(1)} %reshape.13054, f32[5,512]{1,0:T(8,128)S(1)} %add.2246, f32[25,512]{1,0:T(8,128)S(1)} %reshape.13055, f32[25,512]{1,0:T(8,128)S(1)} %add.2247), dimensions={0} | concatenate | bytes 450560 | tf_op jit(solution)/shard_map/while/body/eval_jaxpr/concatenate | solution.py:225
  394.0 5.2 collective-permute-start.1
  407.8 7.7 %concatenate.659 = f32[110,512]{1,0:T(8,128)} concatenate(f32[5,512]{1,0:T(8,128)S(1)} %slice_add_fusion.50, f32[25,512]{1,0:T(8,128)S(1)} %slice_add_fusion.51, f32[25,512]{1,0:T(8,128)S(1)} %reshape.13054, f32[5,512]{1,0:T(8,128)S(1)} %add.2246, f32[25,512]{1,0:T(8,128)S(1)} %reshape.13055, f32[25,512]{1,0:T(8,128)S(1)} %add.2247), dimensions={0} | concatenate | bytes 450560 | tf_op jit(solution)/shard_map/while/body/eval_jaxpr/concatenate | solution.py:225
  415.5 5.2 collective-permute-start.1
  429.3 7.7 %concatenate.659 = f32[110,512]{1,0:T(8,128)} concatenate(f32[5,512]{1,0:T(8,128)S(1)} %slice_add_fusion.50, f32[25,512]{1,0:T(8,128)S(1)} %slice_add_fusion.51, f32[25,512]{1,0:T(8,128)S(1)} %reshape.13054, f32[5,512]{1,0:T(8,128)S(1)} %add.2246, f32[25,512]{1,0:T(8,128)S(1)} %reshape.13055, f32[25,512]{1,0:T(8,128)S(1)} %add.2247), dimensions={0} | concatenate | bytes 450560 | tf_op jit(solution)/shard_map/while/body/eval_jaxpr/concatenate | solution.py:225
  436.9 5.2 collective-permute-start.1
  450.7 7.7 %concatenate.659 = f32[110,512]{1,0:T(8,128)} concatenate(f32[5,512]{1,0:T(8,128)S(1)} %slice_add_fusion.50, f32[25,512]{1,0:T(8,128)S(1)} %slice_add_fusion.51, f32[25,512]{1,0:T(8,128)S(1)} %reshape.13054, f32[5,512]{1,0:T(8,128)S(1)} %add.2246, f32[25,512]{1,0:T(8,128)S(1)} %reshape.13055, f32[25,512]{1,0:T(8,128)S(1)} %add.2247), dimensions={0} | concatenate | bytes 450560 | tf_op jit(solution)/shard_map/while/body/eval_jaxpr/concatenate | solution.py:225
  469.9 101.8 %while.150 = (s32[]{:T(128)}, f32[110,512]{1,0:T(8,128)S(1)}, f32[110,512]{1,0:T(8,128)}, f32[5,5,1,512]{3,1,0,2:T(8,128)S(1)}, f32[5,5,1,512]{3,1,0,2:T(8,128)S...) while((s32[]{:T(128)}, f32[110,512]{1,0:T(8,128)S(1)}, ...), condition=%wide.wide.region_431.432_spmd, body=%wide.wide.region_405.431_spmd.sunk | while | flops 2626632 | bytes 10184197 | solution.py:326
  471.8 6.9 %collective-permute-done.2 = f32[110,512]{1,0:T(8,128)S(1)} collective-permute-done((f32[110,512]{1,0:T(8,128)S(1)}, f32[110,512]{1,0:T(8,128)S(1)}, u32[]{:S(2)}, u32[]{:S(2)}) %collective-permute-start.2) | collective-permute-done | bytes 225312 | tf_op jit(solution)/shard_map/while/body/eval_jaxpr/ppermute | solution.py:35
  486.9 6.3 %collective-permute-done.2 = f32[110,512]{1,0:T(8,128)S(1)} collective-permute-done((f32[110,512]{1,0:T(8,128)S(1)}, f32[110,512]{1,0:T(8,128)S(1)}, u32[]{:S(2)}, u32[]{:S(2)}) %collective-permute-start.2) | collective-permute-done | bytes 225312 | tf_op jit(solution)/shard_map/while/body/eval_jaxpr/ppermute | solution.py:35
  501.4 6.3 %collective-permute-done.2 = f32[110,512]{1,0:T(8,128)S(1)} collective-permute-done((f32[110,512]{1,0:T(8,128)S(1)}, f32[110,512]{1,0:T(8,128)S(1)}, u32[]{:S(2)}, u32[]{:S(2)}) %collective-permute-start.2) | collective-permute-done | bytes 225312 | tf_op jit(solution)/shard_map/while/body/eval_jaxpr/ppermute | solution.py:35
  515.9 6.3 %collective-permute-done.2 = f32[110,512]{1,0:T(8,128)S(1)} collective-permute-done((f32[110,512]{1,0:T(8,128)S(1)}, f32[110,512]{1,0:T(8,128)S(1)}, u32[]{:S(2)}, u32[]{:S(2)}) %collective-permute-start.2) | collective-permute-done | bytes 225312 | tf_op jit(solution)/shard_map/while/body/eval_jaxpr/ppermute | solution.py:35
  530.3 6.3 %collective-permute-done.2 = f32[110,512]{1,0:T(8,128)S(1)} collective-permute-done((f32[110,512]{1,0:T(8,128)S(1)}, f32[110,512]{1,0:T(8,128)S(1)}, u32[]{:S(2)}, u32[]{:S(2)}) %collective-permute-start.2) | collective-permute-done | bytes 225312 | tf_op jit(solution)/shard_map/while/body/eval_jaxpr/ppermute | solution.py:35
  544.8 6.3 %collective-permute-done.2 = f32[110,512]{1,0:T(8,128)S(1)} collective-permute-done((f32[110,512]{1,0:T(8,128)S(1)}, f32[110,512]{1,0:T(8,128)S(1)}, u32[]{:S(2)}, u32[]{:S(2)}) %collective-permute-start.2) | collective-permute-done | bytes 225312 | tf_op jit(solution)/shard_map/while/body/eval_jaxpr/ppermute | solution.py:35
  559.2 6.3 %collective-permute-done.2 = f32[110,512]{1,0:T(8,128)S(1)} collective-permute-done((f32[110,512]{1,0:T(8,128)S(1)}, f32[110,512]{1,0:T(8,128)S(1)}, u32[]{:S(2)}, u32[]{:S(2)}) %collective-permute-start.2) | collective-permute-done | bytes 225312 | tf_op jit(solution)/shard_map/while/body/eval_jaxpr/ppermute | solution.py:35
  (3258 shorter events, 429.9 us)
Async XLA Ops:
  1.1 30.8 %collective-permute-start.4 = (f32[12,4,1,128]{3,2,1,0:T(1,128)S(1)}, f32[12,4,1,128]{3,2,1,0:T(1,128)S(1)}, u32[]{:S(2)}, u32[]{:S(2)}) collective-permute-start(f32[12,4,1,128]{3,2,1,0:T(1,128)S(1)} %get-tuple-element.2785), channel_id=1, source_target_pairs={{1,0},{2,1},{3,2},{4,3},{5,4},{6,5},{7,6},{9,8},{10,9},{11,10},{12... | collective-permute-start | bytes 73736 | tf_op jit(solution)/shard_map/ppermute | solution.py:19
  3.7 28.3 %collective-permute-start.3 = (f32[12,4,1,128]{3,2,1,0:T(1,128)S(1)}, f32[12,4,1,128]{3,2,1,0:T(1,128)S(1)}, u32[]{:S(2)}, u32[]{:S(2)}) collective-permute-start(f32[12,4,1,128]{3,2,1,0:T(1,128)S(1)} %get-tuple-element.2784), channel_id=1, source_target_pairs={{0,1},{1,2},{2,3},{3,4},{4,5},{5,6},{6,7},{8,9},{9,10},{10,11},{11... | collective-permute-start | bytes 73736 | tf_op jit(solution)/shard_map/ppermute | solution.py:17
  8.7 8.1 %collective-permute-start.6 = (f32[12,4,8,1]{3,2,1,0:T(8,128)S(1)}, f32[12,4,8,1]{3,2,1,0:T(8,128)S(1)}, u32[]{:S(2)}, u32[]{:S(2)}) collective-permute-start(f32[12,4,8,1]{3,2,1,0:T(8,128)S(1)} %get-tuple-element.2783), channel_id=1, source_target_pairs={{8,0},{16,8},{24,16},{0,24},{9,1},{17,9},{25,17},{1,25},{10,2},{18... | collective-permute-start | bytes 4616 | tf_op jit(solution)/shard_map/ppermute | solution.py:19
  12.1 8.5 %collective-permute-start.5 = (f32[12,4,8,1]{3,2,1,0:T(8,128)S(1)}, f32[12,4,8,1]{3,2,1,0:T(8,128)S(1)}, u32[]{:S(2)}, u32[]{:S(2)}) collective-permute-start(f32[12,4,8,1]{3,2,1,0:T(8,128)S(1)} %get-tuple-element.2782), channel_id=1, source_target_pairs={{0,8},{8,16},{16,24},{24,0},{1,9},{9,17},{17,25},{25,1},{2,10},{10... | collective-permute-start | bytes 4616 | tf_op jit(solution)/shard_map/ppermute | solution.py:17
  12.1 231.0 %copy-start.59 = (pred[5]{0:T(512)(128)(4,1)}, pred[5]{0:T(512)(128)(4,1)S(1)}, u32[]{:S(2)}) copy-start(pred[5]{0:T(512)(128)(4,1)S(1)} %iota_compare_fusion.109) | copy-start | bytes 19
  12.1 231.8 %copy-start.55 = (pred[5]{0:T(512)(128)(4,1)}, pred[5]{0:T(512)(128)(4,1)S(1)}, u32[]{:S(2)}) copy-start(pred[5]{0:T(512)(128)(4,1)S(1)} %iota_compare_fusion.108) | copy-start | bytes 19
  192.0 49.7 %copy-start.45 = (f32[5,5,32]{2,1,0:T(8,128)}, f32[5,5,32]{2,1,0:T(8,128)S(1)}, u32[]{:S(2)}) copy-start(f32[5,5,32]{2,1,0:T(8,128)S(1)} %get-tuple-element.2459) | copy-start | bytes 9604
  198.2 5.5 collective-permute-start
  209.0 4.9 collective-permute-start
  219.2 4.9 collective-permute-start
  306.8 9.9 %collective-permute-start.1 = (f32[110,512]{1,0:T(8,128)}, f32[110,512]{1,0:T(8,128)S(1)}, u32[]{:S(2)}, u32[]{:S(2)}) collective-permute-start(f32[110,512]{1,0:T(8,128)} %get-tuple-element.3490), channel_id=1, source_target_pairs={{0,1},{1,2},{2,3},{3,4},{4,5},{5,6},{6,7},{8,9},{9,10},{10,11},{11... | collective-permute-start | bytes 675848 | tf_op jit(solution)/shard_map/while/body/eval_jaxpr/ppermute | solution.py:35
  329.7 8.4 %collective-permute-start.1 = (f32[110,512]{1,0:T(8,128)}, f32[110,512]{1,0:T(8,128)S(1)}, u32[]{:S(2)}, u32[]{:S(2)}) collective-permute-start(f32[110,512]{1,0:T(8,128)} %get-tuple-element.3490), channel_id=1, source_target_pairs={{0,1},{1,2},{2,3},{3,4},{4,5},{5,6},{6,7},{8,9},{9,10},{10,11},{11... | collective-permute-start | bytes 675848 | tf_op jit(solution)/shard_map/while/body/eval_jaxpr/ppermute | solution.py:35
  351.2 8.4 %collective-permute-start.1 = (f32[110,512]{1,0:T(8,128)}, f32[110,512]{1,0:T(8,128)S(1)}, u32[]{:S(2)}, u32[]{:S(2)}) collective-permute-start(f32[110,512]{1,0:T(8,128)} %get-tuple-element.3490), channel_id=1, source_target_pairs={{0,1},{1,2},{2,3},{3,4},{4,5},{5,6},{6,7},{8,9},{9,10},{10,11},{11... | collective-permute-start | bytes 675848 | tf_op jit(solution)/shard_map/while/body/eval_jaxpr/ppermute | solution.py:35
  372.6 8.4 %collective-permute-start.1 = (f32[110,512]{1,0:T(8,128)}, f32[110,512]{1,0:T(8,128)S(1)}, u32[]{:S(2)}, u32[]{:S(2)}) collective-permute-start(f32[110,512]{1,0:T(8,128)} %get-tuple-element.3490), channel_id=1, source_target_pairs={{0,1},{1,2},{2,3},{3,4},{4,5},{5,6},{6,7},{8,9},{9,10},{10,11},{11... | collective-permute-start | bytes 675848 | tf_op jit(solution)/shard_map/while/body/eval_jaxpr/ppermute | solution.py:35
  394.0 8.4 %collective-permute-start.1 = (f32[110,512]{1,0:T(8,128)}, f32[110,512]{1,0:T(8,128)S(1)}, u32[]{:S(2)}, u32[]{:S(2)}) collective-permute-start(f32[110,512]{1,0:T(8,128)} %get-tuple-element.3490), channel_id=1, source_target_pairs={{0,1},{1,2},{2,3},{3,4},{4,5},{5,6},{6,7},{8,9},{9,10},{10,11},{11... | collective-permute-start | bytes 675848 | tf_op jit(solution)/shard_map/while/body/eval_jaxpr/ppermute | solution.py:35
  415.5 8.4 %collective-permute-start.1 = (f32[110,512]{1,0:T(8,128)}, f32[110,512]{1,0:T(8,128)S(1)}, u32[]{:S(2)}, u32[]{:S(2)}) collective-permute-start(f32[110,512]{1,0:T(8,128)} %get-tuple-element.3490), channel_id=1, source_target_pairs={{0,1},{1,2},{2,3},{3,4},{4,5},{5,6},{6,7},{8,9},{9,10},{10,11},{11... | collective-permute-start | bytes 675848 | tf_op jit(solution)/shard_map/while/body/eval_jaxpr/ppermute | solution.py:35
  436.9 8.4 %collective-permute-start.1 = (f32[110,512]{1,0:T(8,128)}, f32[110,512]{1,0:T(8,128)S(1)}, u32[]{:S(2)}, u32[]{:S(2)}) collective-permute-start(f32[110,512]{1,0:T(8,128)} %get-tuple-element.3490), channel_id=1, source_target_pairs={{0,1},{1,2},{2,3},{3,4},{4,5},{5,6},{6,7},{8,9},{9,10},{10,11},{11... | collective-permute-start | bytes 675848 | tf_op jit(solution)/shard_map/while/body/eval_jaxpr/ppermute | solution.py:35
  469.9 8.9 %collective-permute-start.2 = (f32[110,512]{1,0:T(8,128)S(1)}, f32[110,512]{1,0:T(8,128)S(1)}, u32[]{:S(2)}, u32[]{:S(2)}) collective-permute-start(f32[110,512]{1,0:T(8,128)S(1)} %get-tuple-element.3456), channel_id=1, source_target_pairs={{1,0},{2,1},{3,2},{4,3},{5,4},{6,5},{7,6},{9,8},{10,9},{11,10},{12... | collective-permute-start | bytes 675848 | tf_op jit(solution)/shard_map/while/body/eval_jaxpr/ppermute | solution.py:35
  485.0 8.2 %collective-permute-start.2 = (f32[110,512]{1,0:T(8,128)S(1)}, f32[110,512]{1,0:T(8,128)S(1)}, u32[]{:S(2)}, u32[]{:S(2)}) collective-permute-start(f32[110,512]{1,0:T(8,128)S(1)} %get-tuple-element.3456), channel_id=1, source_target_pairs={{1,0},{2,1},{3,2},{4,3},{5,4},{6,5},{7,6},{9,8},{10,9},{11,10},{12... | collective-permute-start | bytes 675848 | tf_op jit(solution)/shard_map/while/body/eval_jaxpr/ppermute | solution.py:35
  499.4 8.2 %collective-permute-start.2 = (f32[110,512]{1,0:T(8,128)S(1)}, f32[110,512]{1,0:T(8,128)S(1)}, u32[]{:S(2)}, u32[]{:S(2)}) collective-permute-start(f32[110,512]{1,0:T(8,128)S(1)} %get-tuple-element.3456), channel_id=1, source_target_pairs={{1,0},{2,1},{3,2},{4,3},{5,4},{6,5},{7,6},{9,8},{10,9},{11,10},{12... | collective-permute-start | bytes 675848 | tf_op jit(solution)/shard_map/while/body/eval_jaxpr/ppermute | solution.py:35
  513.9 8.2 %collective-permute-start.2 = (f32[110,512]{1,0:T(8,128)S(1)}, f32[110,512]{1,0:T(8,128)S(1)}, u32[]{:S(2)}, u32[]{:S(2)}) collective-permute-start(f32[110,512]{1,0:T(8,128)S(1)} %get-tuple-element.3456), channel_id=1, source_target_pairs={{1,0},{2,1},{3,2},{4,3},{5,4},{6,5},{7,6},{9,8},{10,9},{11,10},{12... | collective-permute-start | bytes 675848 | tf_op jit(solution)/shard_map/while/body/eval_jaxpr/ppermute | solution.py:35
  528.3 8.2 %collective-permute-start.2 = (f32[110,512]{1,0:T(8,128)S(1)}, f32[110,512]{1,0:T(8,128)S(1)}, u32[]{:S(2)}, u32[]{:S(2)}) collective-permute-start(f32[110,512]{1,0:T(8,128)S(1)} %get-tuple-element.3456), channel_id=1, source_target_pairs={{1,0},{2,1},{3,2},{4,3},{5,4},{6,5},{7,6},{9,8},{10,9},{11,10},{12... | collective-permute-start | bytes 675848 | tf_op jit(solution)/shard_map/while/body/eval_jaxpr/ppermute | solution.py:35
  542.8 8.2 %collective-permute-start.2 = (f32[110,512]{1,0:T(8,128)S(1)}, f32[110,512]{1,0:T(8,128)S(1)}, u32[]{:S(2)}, u32[]{:S(2)}) collective-permute-start(f32[110,512]{1,0:T(8,128)S(1)} %get-tuple-element.3456), channel_id=1, source_target_pairs={{1,0},{2,1},{3,2},{4,3},{5,4},{6,5},{7,6},{9,8},{10,9},{11,10},{12... | collective-permute-start | bytes 675848 | tf_op jit(solution)/shard_map/while/body/eval_jaxpr/ppermute | solution.py:35
  557.2 8.2 %collective-permute-start.2 = (f32[110,512]{1,0:T(8,128)S(1)}, f32[110,512]{1,0:T(8,128)S(1)}, u32[]{:S(2)}, u32[]{:S(2)}) collective-permute-start(f32[110,512]{1,0:T(8,128)S(1)} %get-tuple-element.3456), channel_id=1, source_target_pairs={{1,0},{2,1},{3,2},{4,3},{5,4},{6,5},{7,6},{9,8},{10,9},{11,10},{12... | collective-permute-start | bytes 675848 | tf_op jit(solution)/shard_map/while/body/eval_jaxpr/ppermute | solution.py:35
  (83 other events, 292.1 us)
where the time goes:
time: 595 us; the launch traced here: 584 us
  other arithmetic  245 us (41%)
  local copies, waits for them, and re-layouts  170 us (29%)
  waiting for transfers between devices  88.1 us (15%)
  starting transfers between devices  62.4 us (10%)
  loops' own time  9.21 us (2%)
  between operations  9.07 us (2%)
    another operation x170, other arithmetic, invert_small(): chosen_row = jnp.argmax(magnitude, axis=0)  116 us
    ppermute x14, waiting for transfers between devices, shifted(): return lax.ppermute(shard, axis, pairs)  66.8 us
    concatenate x17, local copies, waits for them, and re-layouts, merge_full(): jnp.concatenate([lf_base + block_apply(lf_right, outer[0]), (lf_left + bl...  58.7 us
    ppermute x14, starting transfers between devices, shifted(): return lax.ppermute(shard, axis, pairs)  51.1 us
    reduce_sum x130, other arithmetic, block_product(): return jnp.sum(left[:, :, None] * right[None, :, :], axis=1)  43.4 us
    unnamed x235, local copies, waits for them, and re-layouts  21.2 us
    reduce_sum x123, other arithmetic, block_apply(): return jnp.sum(matrix * vector[None], axis=1)  18.6 us
    ppermute x3, waiting for transfers between devices, passed_along(): return lax.ppermute(value, axis, pairs)  13.6 us
  transfers between devices with their start and end apart: 21, of which 19 were waited for; matrix products, arithmetic and copies ran while one was open for 2% of the time, Pallas kernels for 0%

commit v1 on v0

v1 whole, which is shorter than its diff:
```python
import jax
import jax.numpy as jnp
from jax import lax
from jax.experimental import pallas as pl
from jax.experimental.pallas import tpu as pltpu
from jax.sharding import PartitionSpec as P

GAMMA = 1.4
LESS = GAMMA - 1.0
VMEM_LIMIT = 16 * 1024 * 1024
TILE = (8, 128)
LANES = 128


def mat_mul(a, b):
    out = []
    for i in range(5):
        row = []
        for j in range(5):
            total = a[i][0] * b[0][j]
            for k in range(1, 5):
                total = total + a[i][k] * b[k][j]
            row.append(total)
        out.append(row)
    return out


def mat_vec(a, x):
    out = []
    for i in range(5):
        total = a[i][0] * x[0]
        for k in range(1, 5):
            total = total + a[i][k] * x[k]
        out.append(total)
    return out


def mat_map(fn, *mats):
    return [[fn(*(m[i][j] for m in mats)) for j in range(5)] for i in range(5)]


def vec_map(fn, *vecs):
    return [fn(*(v[i] for v in vecs)) for i in range(5)]


def mat_add(a, b):
    return mat_map(lambda x, y: x + y, a, b)


def mat_sub(a, b):
    return mat_map(lambda x, y: x - y, a, b)


def mat_neg(a):
    return mat_map(lambda x: -x, a)


def vec_add(a, b):
    return vec_map(lambda x, y: x + y, a, b)


def vec_sub(a, b):
    return vec_map(lambda x, y: x - y, a, b)


def plus_eye(a):
    return [[a[i][j] + 1.0 if i == j else a[i][j] for j in range(5)] for i in range(5)]


def mat_inv(matrix):
    a = [list(row) for row in matrix]
    for k in range(5):
        pivot = 1.0 / a[k][k]
        row = [a[k][j] * pivot if j != k else pivot for j in range(5)]
        for i in range(5):
            if i == k:
                continue
            factor = a[i][k]
            for j in range(5):
                a[i][j] = -(factor * pivot) if j == k else a[i][j] - factor * row[j]
        a[k] = row
    return a


def face_values(left, right):
    state = [0.5 * (left[i] + right[i]) for i in range(5)]
    m1 = 0.5 * (left[5] + right[5])
    m2 = 0.5 * (left[6] + right[6])
    step, spread = left[7], left[8]
    over = 1.0 / state[0]
    u, v, w, e = (state[i] * over for i in range(1, 5))
    t = m1 * u + m2 * v
    f = (0.5 * LESS) * (u * u + v * v + w * w)
    h = GAMMA * e - f
    jac = [
        [None, m1, m2, None, None],
        [
            m1 * f - u * t,
            t - (GAMMA - 2.0) * m1 * u,
            m2 * u - LESS * m1 * v,
            -LESS * m1 * w,
            LESS * m1,
        ],
        [
            m2 * f - v * t,
            m1 * v - LESS * m2 * u,
            t - (GAMMA - 2.0) * m2 * v,
            -LESS * m2 * w,
            LESS * m2,
        ],
        [-w * t, m1 * w, m2 * w, t, None],
        [
            t * (2.0 * f - GAMMA * e),
            m1 * h - LESS * u * t,
            m2 * h - LESS * v * t,
            -LESS * w * t,
            GAMMA * t,
        ],
    ]
    widest = None
    for row in jac:
        total = None
        for x in row:
            if x is not None:
                total = jnp.abs(x) if total is None else total + jnp.abs(x)
        widest = total if widest is None else jnp.maximum(widest, total)
    scale = 1.0 / widest
    norm = [[None if x is None else x * scale for x in row] for row in jac]
    half_step = 0.5 * step
    weight = half_step * spread
    convect = [[None] * 5 for _ in range(5)]
    damping = [[None] * 5 for _ in range(5)]
    for i in range(5):
        for j in range(i, 5):
            parts = [x for x in (norm[i][j], norm[j][i]) if x is not None]
            if parts:
                c = half_step * (parts[0] + parts[1] if len(parts) == 2 else parts[0])
            else:
                c = jnp.zeros_like(step)
            total = None
            for k in range(5):
                if norm[k][i] is None or norm[k][j] is None:
                    continue
                term = norm[k][i] * norm[k][j]
                total = term if total is None else total + term
            if i == j:
                total = total + 1.0
            d = weight * total
            convect[i][j] = convect[j][i] = c
            damping[i][j] = damping[j][i] = d
    jump = [right[i] - left[i] for i in range(5)]
    flux = vec_sub(mat_vec(convect, state), mat_vec(damping, jump))
    lower = mat_map(lambda c, d: -0.5 * c - d, convect, damping)
    upper = mat_map(lambda c, d: 0.5 * c - d, convect, damping)
    for i in range(5):
        for j in range(i):
            lower[i][j] = lower[j][i]
            upper[i][j] = upper[j][i]
    return damping, lower, upper, flux


def put_mat(ref, at, a, lead=()):
    for i in range(5):
        for j in range(5):
            ref[lead + (at + 5 * i + j,)] = a[i][j]


def get_mat(ref, at, lead=()):
    return [[ref[lead + (at + 5 * i + j,)] for j in range(5)] for i in range(5)]


def put_vec(ref, at, x, lead=()):
    for i in range(5):
        ref[lead + (at + i,)] = x[i]


def get_vec(ref, at, lead=()):
    return [ref[lead + (at + i,)] for i in range(5)]


class Line:
    def __init__(self, dim):
        self.dim = dim
        self.n = TILE[dim]
        self.count = self.n // 4
        self.at = lax.broadcasted_iota(jnp.int32, TILE, dim)
        self.even1 = (self.at & 1) == 0
        self.even2 = (self.at & 2) == 0
        self.inner = self.at < self.n - 2
        self.group = self.at >> 2

    def roll(self, x, by):
        if isinstance(by, int):
            by = by % self.n
            if by == 0:
                return x
        return pltpu.roll(x, by, self.dim)

    def vroll(self, v, by):
        return [self.roll(x, by) for x in v]

    def mroll(self, m, by):
        return [self.vroll(row, by) for row in m]

    def pack1(self, a, b):
        first = jnp.where(self.even1, a, self.roll(b, 1))
        second = jnp.where(self.even1, self.roll(a, -1), b)
        return first, second

    def unpack1(self, first, second):
        a = jnp.where(self.even1, first, self.roll(second, 1))
        b = jnp.where(self.even1, self.roll(first, -1), second)
        return a, b

    def pack2(self, a, b):
        first = jnp.where(self.even2, a, self.roll(b, 2))
        second = jnp.where(self.even2, self.roll(a, -2), b)
        return first, second

    def unpack2(self, first, second):
        a = jnp.where(self.even2, first, self.roll(second, 2))
        b = jnp.where(self.even2, self.roll(first, -2), second)
        return a, b


def line_faces(line, cells_e, cells_o):
    after_e = face_values(cells_e, cells_o)
    nexts = [line.roll(x, -2) for x in cells_e[:7]]
    after_o = face_values(cells_o, nexts)
    return after_e, after_o


def first_level(line, after_e, after_o, keep_ref, t):
    damp_e, low_e, upp_e, _ = after_e
    damp_o, low_o, upp_o, _ = after_o
    inverse = mat_inv(plus_eye(mat_add(damp_e, damp_o)))
    w_low = mat_mul(inverse, low_e)
    w_upp = mat_mul(inverse, upp_o)
    put_mat(keep_ref, 0, inverse, (t,))
    put_mat(keep_ref, 25, upp_e, (t,))
    put_mat(keep_ref, 50, low_o, (t,))
    put_mat(keep_ref, 75, w_low, (t,))
    put_mat(keep_ref, 100, w_upp, (t,))
    inner = line.inner
    low = mat_map(lambda x, y: jnp.where(inner, -x, y), mat_mul(low_o, w_low), low_e)
    mid_l = mat_map(
        lambda x, y, z: jnp.where(inner, y - x, z), mat_mul(low_o, w_upp), damp_o, damp_e
    )
    upp = mat_map(lambda x, y: jnp.where(inner, -x, y), mat_mul(upp_e, w_upp), upp_e)
    mid_r = mat_map(
        lambda x, y: jnp.where(inner, y - x, y), mat_mul(upp_e, w_low), plus_eye(damp_e)
    )
    return line.mroll(low, 2), line.mroll(mid_l, 2), mid_r, upp


def second_level(line, level_a, level_b, keep_ref):
    packed = [
        [[line.pack2(x, y) for x, y in zip(ra, rb)] for ra, rb in zip(ma, mb)]
        for ma, mb in zip(level_a, level_b)
    ]
    evens = [mat_map(lambda p: p[0], m) for m in packed]
    odds = [mat_map(lambda p: p[1], m) for m in packed]
    inverse = mat_inv(mat_add(odds[1], odds[2]))
    w_low = mat_mul(inverse, odds[0])
    w_upp = mat_mul(inverse, odds[3])
    put_mat(keep_ref, 0, inverse)
    put_mat(keep_ref, 25, evens[3])
    put_mat(keep_ref, 50, evens[0])
    put_mat(keep_ref, 75, w_low)
    put_mat(keep_ref, 100, w_upp)
    left_low = line.mroll(w_low, 4)
    left_upp = line.mroll(w_upp, 4)
    low = mat_neg(mat_mul(evens[0], left_low))
    mid_l = mat_sub(evens[1], mat_mul(evens[0], left_upp))
    mid_r = mat_sub(evens[2], mat_mul(evens[3], w_low))
    upp = mat_neg(mat_mul(evens[3], w_upp))
    return low, mid_l, mid_r, upp


def later_level(line, low, mid_l, mid_r, upp, reach, keep_ref, level):
    left_ok = (line.group > reach) | (line.group == 0)
    right_ok = line.group + reach < line.count
    inverse = mat_inv(mat_add(mid_l, mid_r))
    w_low = mat_mul(inverse, low)
    w_upp = mat_mul(inverse, upp)
    low_in = mat_map(lambda x: jnp.where(left_ok, x, 0.0), low)
    upp_in = mat_map(lambda x: jnp.where(right_ok, x, 0.0), upp)
    put_mat(keep_ref, 0, inverse, (level,))
    put_mat(keep_ref, 25, low_in, (level,))
    put_mat(keep_ref, 50, upp_in, (level,))
    back = 4 * reach
    ahead = line.n - 4 * reach
    left_low, left_upp = line.mroll(w_low, back), line.mroll(w_upp, back)
    right_low, right_upp = line.mroll(w_low, ahead), line.mroll(w_upp, ahead)
    new_low = mat_map(
        lambda x, y: jnp.where(left_ok, -x, y), mat_mul(low_in, left_low), low
    )
    new_mid_l = mat_sub(mid_l, mat_mul(low_in, left_upp))
    new_upp = mat_map(
        lambda x, y: jnp.where(right_ok, -x, y), mat_mul(upp_in, right_upp), upp
    )
    new_mid_r = mat_sub(mid_r, mat_mul(upp_in, right_low))
    return new_low, new_mid_l, new_mid_r, new_upp


def line_levels(line, states, keep1, keep2, keep3, ends, work):
    low, mid_l, mid_r, upp = second_level(line, states[0], states[1], keep2)
    steps = line.count.bit_length() - 1
    if steps == 1:
        low, mid_l, mid_r, upp = later_level(line, low, mid_l, mid_r, upp, 1, keep3, 0)
    else:
        for at, m in enumerate((low, mid_l, mid_r, upp)):
            put_mat(work, 25 * at, m)

        def body(level, carry):
            now = [get_mat(work, 25 * at) for at in range(4)]
            reach = lax.shift_left(jnp.int32(1), level)
            new = later_level(line, *now, reach, keep3, level)
            for at, m in enumerate(new):
                put_mat(work, 25 * at, m)
            return carry

        lax.fori_loop(0, steps, body, 0)
        low, mid_l, mid_r, upp = (get_mat(work, 25 * at) for at in range(4))
    for at, m in enumerate((low, mid_l, mid_r, upp)):
        put_mat(ends, 25 * at, m)
    inverse = mat_inv(mat_add(mid_l, mid_r))
    put_mat(keep3, 0, inverse, (steps,))
    put_mat(keep3, 25, mat_mul(inverse, low), (steps,))
    put_mat(keep3, 50, mat_mul(inverse, upp), (steps,))


def line_forward(line, rhs_e, rhs_o, keep1, keep2, keep3, zs):
    right, left = [], []
    for t in range(2):
        z = mat_vec(get_mat(keep1, 0, (t,)), rhs_o[t])
        put_vec(zs, 5 * t, z)
        from_r = mat_vec(get_mat(keep1, 25, (t,)), z)
        from_l = mat_vec(get_mat(keep1, 50, (t,)), z)
        right.append(
            vec_map(lambda r, x: jnp.where(line.inner, r - x, r), rhs_e[t], from_r)
        )
        left.append(
            line.vroll(vec_map(lambda r, x: jnp.where(line.inner, -x, r), rhs_o[t], from_l), 2)
        )
    pair_r = [line.pack2(x, y) for x, y in zip(right[0], right[1])]
    pair_l = [line.pack2(x, y) for x, y in zip(left[0], left[1])]
    odd = [x[1] + y[1] for x, y in zip(pair_r, pair_l)]
    z = mat_vec(get_mat(keep2, 0), odd)
    put_vec(zs, 10, z)
    r_r = vec_sub([x[0] for x in pair_r], mat_vec(get_mat(keep2, 25), z))
    r_l = vec_sub([x[0] for x in pair_l], mat_vec(get_mat(keep2, 50), line.vroll(z, 4)))
    steps = line.count.bit_length() - 1
    for level in range(steps):
        z = mat_vec(get_mat(keep3, 0, (level,)), vec_add(r_l, r_r))
        back = 4 << level
        r_l = vec_sub(r_l, mat_vec(get_mat(keep3, 25, (level,)), line.vroll(z, back)))
        r_r = vec_sub(r_r, mat_vec(get_mat(keep3, 50, (level,)), line.vroll(z, -back)))
    put_vec(zs, 15, mat_vec(get_mat(keep3, 0, (steps,)), vec_add(r_l, r_r)))
    return r_r, r_l


def line_backward(line, first, last, keep1, keep2, keep3, zs):
    steps = line.count.bit_length() - 1
    inner = vec_sub(
        get_vec(zs, 15),
        vec_add(
            mat_vec(get_mat(keep3, 25, (steps,)), first),
            mat_vec(get_mat(keep3, 50, (steps,)), last),
        ),
    )
    even = vec_map(lambda x, y: jnp.where(line.group == 0, y, x), inner, first)
    ahead = vec_map(
        lambda x, y: jnp.where(line.at >= line.n - 4, y, x), line.vroll(even, -4), last
    )
    odd = vec_sub(
        get_vec(zs, 10),
        vec_add(
            mat_vec(get_mat(keep2, 75), even), mat_vec(get_mat(keep2, 100), ahead)
        ),
    )
    pairs = [line.unpack2(x, y) for x, y in zip(even, odd)]
    out = []
    for t in range(2):
        even = [p[t] for p in pairs]
        ends = line.vroll(last, 2) if t == 0 else last
        ahead = line.vroll(even, -2)
        odd = vec_sub(
            get_vec(zs, 5 * t),
            vec_add(
                mat_vec(get_mat(keep1, 75, (t,)), even),
                mat_vec(get_mat(keep1, 100, (t,)), ahead),
            ),
        )
        odd = vec_map(lambda x, y: jnp.where(line.inner, x, y), odd, ends)
        spans = [line.unpack1(x, y) for x, y in zip(even, odd)]
        out.append([s[0] for s in spans])
        out.append([s[1] for s in spans])
    return out


def halo_kernel(state, metrics, step, spread, up, down):
    for s in range(4):
        for c in range(5):
            up[c, s : s + 1, :] = state[c, s, 7:8, :]
            down[c, s : s + 1, :] = state[c, s, 0:1, :]
        for c in range(2):
            up[5 + c, s : s + 1, :] = metrics[2 + c, s, 7:8, :]
            down[5 + c, s : s + 1, :] = metrics[2 + c, s, 0:1, :]
        up[7, s : s + 1, :] = step[s, 7:8, :]
        up[8, s : s + 1, :] = spread[1, s, 7:8, :]


def load_cells(line, state, metrics, step, spread, t, metric_at, spread_at):
    first, second = 2 * t, 2 * t + 1
    pairs = [(state[c, first], state[c, second]) for c in range(5)]
    pairs += [(metrics[metric_at + c, first], metrics[metric_at + c, second]) for c in range(2)]
    pairs += [(step[first], step[second]), (spread[spread_at, first], spread[spread_at, second])]
    packed = [line.pack1(a, b) for a, b in pairs]
    return [p[0] for p in packed], [p[1] for p in packed]


def line_residual(line, after_e, after_o):
    flux_e, flux_o = after_e[3], after_o[3]
    flux_o = vec_map(lambda x: jnp.where(line.inner, x, 0.0), flux_o)
    return vec_sub(line.vroll(flux_o, 2), flux_e), vec_sub(flux_e, flux_o)


def wrap_kernel(state, metrics, step, spread, keep1, keep2, keep3, rhs, note, ends, work):
    line = Line(1)
    states = []
    note[...] = jnp.zeros_like(note)
    packed = [jnp.zeros(TILE, jnp.float32) for _ in range(4)]
    lane_group = line.group
    for t in range(2):
        cells_e, cells_o = load_cells(line, state, metrics, step, spread, t, 0, 0)
        pick = line.at & 3
        mine = (pick >> 1) == t
        for c in range(9):
            k, g = divmod(100 + c, 32)
            moved = line.roll(cells_o[c], 4 * g + 2 * t - (line.n - 2))
            packed[k] = jnp.where((lane_group == g) & mine, moved, packed[k])
        for c in range(7):
            k, g = divmod(109 + c, 32)
            moved = line.roll(cells_e[c], 4 * g + 2 * t)
            packed[k] = jnp.where((lane_group == g) & mine, moved, packed[k])
        after_e, after_o = line_faces(line, cells_e, cells_o)
        rhs_e, rhs_o = line_residual(line, after_e, after_o)
        put_vec(rhs, 0, rhs_e, (t,))
        put_vec(rhs, 5, rhs_o, (t,))
        states.append(first_level(line, after_e, after_o, keep1, t))
    line_levels(line, states, keep1, keep2, keep3, ends, work)
    for place, at in enumerate((50, 75, 0, 25)):
        for c in range(25):
            k, g = divmod(25 * place + c, 32)
            packed[k] = jnp.where(lane_group == g, line.roll(ends[at + c], 4 * g), packed[k])
    for k in range(4):
        note[k] = packed[k]


def wall_faces_kernel(state, metrics, step, spread, coefs, rhs):
    line = Line(0)
    for t in range(2):
        cells_e, cells_o = load_cells(line, state, metrics, step, spread, t, 2, 1)
        after_e, after_o = line_faces(line, cells_e, cells_o)
        rhs_e, rhs_o = line_residual(line, after_e, after_o)
        for c in range(5):
            a, b = line.unpack1(rhs_e[c], rhs_o[c])
            rhs[2 * t, c] = a
            rhs[2 * t + 1, c] = b
        for half, face in enumerate((after_e, after_o)):
            for which in range(3):
                at = 0
                for i in range(5):
                    for j in range(i, 5):
                        coefs[t, half, 15 * which + at] = face[which][i][j]
                        at += 1


def get_face(ref, lead):
    out = []
    for which in range(3):
        m = [[None] * 5 for _ in range(5)]
        at = 0
        for i in range(5):
            for j in range(i, 5):
                m[i][j] = m[j][i] = ref[lead + (15 * which + at,)]
                at += 1
        out.append(m)
    return out + [None]


def wrap_rhs_kernel(
    below, above, up, down, rhs_wall, rhs_wrap, note, keep1, keep2, keep3, zs, sent, edge
):
    line, wall = Line(1), Line(0)
    left = [jnp.concatenate([below[c], up[c]], axis=0) for c in range(9)]
    right = [jnp.concatenate([down[c], above[c]], axis=0) for c in range(7)]
    face = face_values(left, right)
    for which in range(3):
        at = 0
        for i in range(5):
            for j in range(i, 5):
                edge[15 * which + at] = wall.roll(face[which][i][j], 4)
                at += 1
    flux = face[3]
    rhs_e, rhs_o = [], []
    for t in range(2):
        spans = []
        for s in (2 * t, 2 * t + 1):
            values = []
            for c in range(5):
                x = rhs_wall[s, c]
                x = jnp.where(wall.at == 0, x + wall.roll(flux[c], -s), x)
                x = jnp.where(wall.at == 7, x - wall.roll(flux[c], 3 - s), x)
                values.append(x)
            spans.append(values)
        packed = [line.pack1(a, b) for a, b in zip(*spans)]
        rhs_e.append([packed[c][0] + rhs_wrap[t, c] for c in range(5)])
        rhs_o.append([packed[c][1] + rhs_wrap[t, 5 + c] for c in range(5)])
    r_r, r_l = line_forward(line, rhs_e, rhs_o, keep1, keep2, keep3, zs)
    for k in range(3):
        sent[k] = note[k]
    tail = note[3]
    for c in range(10):
        g = 116 + c - 96
        value = r_r[c] if c < 5 else r_l[c - 5]
        tail = jnp.where(line.group == g, line.roll(value, 4 * g), tail)
    sent[3] = tail


def transpose_blocks(rows, count):
    width = LANES // count
    at = lax.broadcasted_iota(jnp.int32, rows[0].shape, 1)
    block = at // width
    bit = 1
    while bit < count:
        clear = (block & bit) == 0
        new = [None] * count
        for m in range(count):
            if m & bit:
                continue
            a, b = rows[m], rows[m | bit]
            new[m] = jnp.where(clear, a, pltpu.roll(b, bit * width, 1))
            new[m | bit] = jnp.where(clear, pltpu.roll(a, LANES - bit * width, 1), b)
        rows = new
        bit *= 2
    return rows


def wall_kernel(coefs, edge, keep1, keep2, keep3, close, parcel, ends, *, count):
    line = Line(0)
    states = []
    for t in range(2):
        after_e = get_face(coefs, (t, 0))
        after_o = get_face(coefs, (t, 1))
        states.append(first_level(line, after_e, after_o, keep1, t))
    line_levels(line, states, keep1, keep2, keep3, ends, None)
    low, mid_l, mid_r, upp = (get_mat(ends, 25 * at) for at in range(4))
    damp_f, low_f, upp_f, _ = get_face(edge, ())
    inverse = mat_inv(plus_eye(mat_add(mid_l, damp_f)))
    w_low = mat_mul(inverse, low)
    w_upp = mat_mul(inverse, upp_f)
    put_mat(close, 0, inverse)
    put_mat(close, 25, upp)
    put_mat(close, 50, low_f)
    put_mat(close, 75, w_low)
    put_mat(close, 100, w_upp)
    final = [
        mat_sub(mid_r, mat_mul(upp, w_low)),
        mat_neg(mat_mul(upp, w_upp)),
        mat_neg(mat_mul(low_f, w_low)),
        mat_sub(damp_f, mat_mul(low_f, w_upp)),
    ]
    rows = [x[0:4] for m in final for r in m for x in r]
    zero = jnp.zeros((4, LANES), jnp.float32)
    rows += [zero] * (-len(rows) % count)
    for k in range(len(rows) // count):
        out = transpose_blocks(rows[k * count : (k + 1) * count], count)
        for d in range(count):
            parcel[d, k] = out[d]


def cycle_kernel(
    *refs, count, wall_count
):
    notes = refs[:count]
    (keep1, keep2, keep3, zs, wkeep1, wkeep2, wkeep3, close, parcel) = refs[count : count + 9]
    sent, wzs, closed = refs[count + 9 :]
    line = Line(1)
    period = 4 * count
    repeat = line.at % period
    channels = [None] * 126
    for k in range(4):
        rolled = [line.roll(notes[q][k], 4 * q) for q in range(count)]
        for a in range(count):
            which = (line.group - a) % count
            mixed = rolled[0]
            for q in range(1, count):
                mixed = jnp.where(which == q, rolled[q], mixed)
            for c in range(a, 32, count):
                if 32 * k + c < 126:
                    index = (repeat + 4 * c) & (LANES - 1)
                    channels[32 * k + c] = jnp.take_along_axis(mixed, index, axis=1)

    def mat_at(at):
        return [[channels[at + 5 * i + j] for j in range(5)] for i in range(5)]

    mid_r, upp, low, mid_l = (mat_at(25 * i) for i in range(4))
    left = channels[100:109]
    right = line.vroll(channels[109:116], -4)
    r_r, r_l = channels[116:121], channels[121:126]
    damp_f, low_f, upp_f, flux = face_values(left, right)
    inverse = mat_inv(plus_eye(mat_add(mid_l, damp_f)))
    w_low = mat_mul(inverse, low)
    w_upp = mat_mul(inverse, upp_f)
    zb = mat_vec(inverse, vec_sub(r_l, flux))
    mid = mat_add(
        mat_sub(mid_r, mat_mul(upp, w_low)),
        line.mroll(mat_sub(damp_f, mat_mul(low_f, w_upp)), 4),
    )
    ahead = mat_neg(mat_mul(upp, w_upp))
    back = mat_neg(line.mroll(mat_mul(low_f, w_low), 4))
    load = vec_add(
        vec_sub(r_r, mat_vec(upp, zb)), line.vroll(vec_sub(flux, mat_vec(low_f, zb)), 4)
    )
    reach = 1
    while 2 * reach < count:
        inverse = mat_inv(mid)
        wb, wa, z = mat_mul(inverse, back), mat_mul(inverse, ahead), mat_vec(inverse, load)
        by = 4 * reach
        mid = mat_sub(
            mid,
            mat_add(
                mat_mul(back, line.mroll(wa, by)), mat_mul(ahead, line.mroll(wb, -by))
            ),
        )
        load = vec_sub(
            load,
            vec_add(mat_vec(back, line.vroll(z, by)), mat_vec(ahead, line.vroll(z, -by))),
        )
        back, ahead = (
            mat_neg(mat_mul(back, line.mroll(wb, by))),
            mat_neg(mat_mul(ahead, line.mroll(wa, -by))),
        )
        reach *= 2
    both = mat_add(back, ahead)
    inverse = mat_inv(mid)
    w, z = mat_mul(inverse, both), mat_vec(inverse, load)
    by = 4 * reach
    mid = mat_sub(mid, mat_mul(both, line.mroll(w, by)))
    load = vec_sub(load, mat_vec(both, line.vroll(z, by)))
    x = mat_vec(mat_inv(mid), load)
    b = vec_sub(zb, vec_add(mat_vec(w_low, x), mat_vec(w_upp, line.vroll(x, -4))))
    spread = line.at & 3
    first = [jnp.take_along_axis(y, spread, axis=1) for y in x]
    last = [jnp.take_along_axis(y, spread, axis=1) for y in b]
    swept = line_backward(line, first, last, keep1, keep2, keep3, zs)

    wall = Line(0)
    rhs_e, rhs_o = [], []
    for t in range(2):
        packed = [wall.pack1(p, q) for p, q in zip(swept[2 * t], swept[2 * t + 1])]
        rhs_e.append([p[0] for p in packed])
        rhs_o.append([p[1] for p in packed])
    r_r, r_l = line_forward_wall(wall, rhs_e, rhs_o, wkeep1, wkeep2, wkeep3, wzs)
    zb = mat_vec(get_mat(close, 0), r_l)
    put_vec(closed, 0, zb)
    out_r = vec_sub(r_r, mat_vec(get_mat(close, 25), zb))
    out_l = vec_map(lambda y: -y, mat_vec(get_mat(close, 50), zb))
    rows = [y[0:4] for y in out_r + out_l]
    zero = jnp.zeros((4, LANES), jnp.float32)
    rows += [zero] * (-len(rows) % wall_count)
    base = parcel.shape[1]
    for k in range(base):
        for d in range(wall_count):
            sent[d, k] = parcel[d, k]
    for k in range(len(rows) // wall_count):
        out = transpose_blocks(rows[k * wall_count : (k + 1) * wall_count], wall_count)
        for d in range(wall_count):
            sent[d, base + k] = out[d]


def line_forward_wall(wall, rhs_e, rhs_o, keep1, keep2, keep3, zs):
    return line_forward(wall, rhs_e, rhs_o, keep1, keep2, keep3, zs)


def open_kernel(got, reply, *, count):
    width = LANES // count
    base = -(-100 // count)

    def unpack(k):
        return transpose_blocks([got[q, k] for q in range(count)], count)

    flat = [x for k in range(base) for x in unpack(k)][:100]
    tail = [x for k in range(base, got.shape[1]) for x in unpack(k)][:10]

    def mat_at(at):
        return [[flat[at + 5 * i + j] for j in range(5)] for i in range(5)]

    mid_r, upp, low, mid_l = (mat_at(25 * i) for i in range(4))
    at = lax.broadcasted_iota(jnp.int32, (4, LANES), 1)
    not_first = at >= width
    not_last = at < LANES - width

    def shift(x, by):
        return pltpu.roll(x, by % LANES, 1)

    def from_back(x):
        return jnp.where(not_first, shift(x, width), 0.0)

    mid = mat_add(mid_r, mat_map(from_back, mid_l))
    back = mat_map(from_back, low)
    ahead = mat_map(lambda x: jnp.where(not_last, x, 0.0), upp)
    load = vec_add(tail[0:5], vec_map(from_back, tail[5:10]))
    reach = 1
    while reach < count:
        by = width * reach
        inverse = mat_inv(mid)
        wb, wa, z = mat_mul(inverse, back), mat_mul(inverse, ahead), mat_vec(inverse, load)
        behind = lambda m: mat_map(lambda x: shift(x, by), m)
        beyond = lambda m: mat_map(lambda x: shift(x, -by), m)
        mid = mat_sub(mid, mat_add(mat_mul(back, behind(wa)), mat_mul(ahead, beyond(wb))))
        load = vec_sub(
            load,
            vec_add(
                mat_vec(back, [shift(x, by) for x in z]),
                mat_vec(ahead, [shift(x, -by) for x in z]),
            ),
        )
        if 2 * reach < count:
            back, ahead = (
                mat_neg(mat_mul(back, behind(wb))),
                mat_neg(mat_mul(ahead, beyond(wa))),
            )
        reach *= 2
    x = mat_vec(mat_inv(mid), load)
    nexts = [jnp.where(not_last, shift(y, -width), 0.0) for y in x]
    rows = x + nexts
    rows += [jnp.zeros((4, LANES), jnp.float32)] * (-len(rows) % count)
    for k in range(len(rows) // count):
        out = transpose_blocks(rows[k * count : (k + 1) * count], count)
        for d in range(count):
            reply[d, k] = out[d]


def finish_kernel(got, keep1, keep2, keep3, close, closed, zs, field, *, count):
    line = Line(0)
    rows = [
        x
        for k in range(got.shape[1])
        for x in transpose_blocks([got[q, k] for q in range(count)], count)
    ]
    twice = [jnp.concatenate([x, x], axis=0) for x in rows[:10]]
    first, nexts = twice[0:5], twice[5:10]
    last = vec_sub(
        get_vec(closed, 0),
        vec_add(mat_vec(get_mat(close, 75), first), mat_vec(get_mat(close, 100), nexts)),
    )
    last = [jnp.where(line.at < 4, x, line.roll(x, 4)) for x in last]
    out = line_backward(line, first, last, keep1, keep2, keep3, zs)
    for s in range(4):
        for c in range(5):
            field[c, s] = out[s][c]


def call(kernel, name, shapes, flops, *args, scratch=()):
    spec = pl.BlockSpec(memory_space=pltpu.VMEM)
    return pl.pallas_call(
        kernel,
        name=name,
        out_shape=[jax.ShapeDtypeStruct(s, jnp.float32) for s in shapes],
        in_specs=[spec] * len(args),
        out_specs=[spec] * len(shapes),
        scratch_shapes=[pltpu.VMEM(s, jnp.float32) for s in scratch],
        compiler_params=pltpu.CompilerParams(vmem_limit_bytes=VMEM_LIMIT),
        cost_estimate=pl.CostEstimate(flops=flops, bytes_accessed=1 << 20, transcendentals=0),
    )(*args)


def on_device(state, metrics, time_step, dissipation, *, wrap_count, wall_count):
    inputs = (state, metrics, time_step, dissipation)
    up, down = call(
        halo_kernel, "halo", [(9, 4, LANES), (7, 4, LANES)], 1 << 12, *inputs
    )
    rises = [(i, i + 1) for i in range(wall_count - 1)]
    falls = [(i + 1, i) for i in range(wall_count - 1)]
    below = lax.ppermute(up, "normal", rises)
    above = lax.ppermute(down, "normal", falls)
    keep1, keep2, keep3, rhs_wrap, note = call(
        wrap_kernel,
        "wrap",
        [(2, 125) + TILE, (125,) + TILE, (6, 75) + TILE, (2, 10) + TILE, (4,) + TILE],
        40 << 20,
        *inputs,
        scratch=[(100,) + TILE, (100,) + TILE],
    )
    coefs, rhs_wall = call(
        wall_faces_kernel,
        "wall_faces",
        [(2, 2, 45) + TILE, (4, 5) + TILE],
        8 << 20,
        *inputs,
    )
    zs, own, edge = call(
        wrap_rhs_kernel,
        "wrap_rhs",
        [(20,) + TILE, (4,) + TILE, (45,) + TILE],
        8 << 20,
        below,
        above,
        up,
        down,
        rhs_wall,
        rhs_wrap,
        note,
        keep1,
        keep2,
        keep3,
    )
    notes = [own]
    for by in range(1, wrap_count):
        pairs = [((i + by) % wrap_count, i) for i in range(wrap_count)]
        notes.append(lax.ppermute(own, "wrap", pairs))
    groups = -(-100 // wall_count)
    tails = -(-10 // wall_count)
    wkeep1, wkeep2, wkeep3, close, parcel = call(
        lambda *refs: wall_kernel(*refs, count=wall_count),
        "wall",
        [
            (2, 125) + TILE,
            (125,) + TILE,
            (2, 75) + TILE,
            (125,) + TILE,
            (wall_count, groups, 4, LANES),
        ],
        20 << 20,
        coefs,
        edge,
        scratch=[(100,) + TILE],
    )
    sent, wzs, closed = call(
        lambda *refs: cycle_kernel(*refs, count=wrap_count, wall_count=wall_count),
        "cycle",
        [(wall_count, groups + tails, 4, LANES), (20,) + TILE, (5,) + TILE],
        10 << 20,
        *notes,
        keep1,
        keep2,
        keep3,
        zs,
        wkeep1,
        wkeep2,
        wkeep3,
        close,
        parcel,
    )
    got = lax.all_to_all(sent, "normal", 0, 0)
    (reply,) = call(
        lambda *refs: open_kernel(*refs, count=wall_count),
        "open",
        [(wall_count, tails, 4, LANES)],
        10 << 20,
        got,
    )
    answer = lax.all_to_all(reply, "normal", 0, 0)
    (field,) = call(
        lambda *refs: finish_kernel(*refs, count=wall_count),
        "finish",
        [(5, 4) + TILE],
        4 << 20,
        answer,
        wkeep1,
        wkeep2,
        wkeep3,
        close,
        closed,
        wzs,
    )
    return field


def solution(mesh):
    placed = (
        P(None, None, "normal", "wrap"),
        P(None, None, "normal", "wrap"),
        P(None, "normal", "wrap"),
        P(None, None, "normal", "wrap"),
    )

    def body(state, metrics, time_step, dissipation):
        return on_device(
            state,
            metrics,
            time_step,
            dissipation,
            wrap_count=mesh.shape["wrap"],
            wall_count=mesh.shape["normal"],
        )

    return jax.shard_map(
        body,
        mesh=mesh,
        in_specs=placed,
        out_specs=P(None, None, "normal", "wrap"),
        check_vma=False,
    )
```

time: 595 us -> 46.1 us (0.08)
  the two profiles are of different devices: /device:TPU:3 before, /device:TPU:0 now
where the time goes in v1:
time: 46.1 us; the launch traced here: 45.7 us
  blocking collectives  20 us (43%)
  Pallas kernels  10.5 us (23%)
  starting transfers between devices  8.4 us (18%)
  waiting for transfers between devices  3.49 us (8%)
  local copies, waits for them, and re-layouts  3.2 us (7%)
    all_to_all x1, blocking collectives, on_device(): got = lax.all_to_all(sent, 'normal', 0, 0)  12.8 us
    pallas_call x8, Pallas kernels, call(): pl.pallas_call(kernel, name=name, out_shape=[jax.ShapeDtypeStruct(s, jnp....  10.5 us
    all_to_all x1, blocking collectives, on_device(): answer = lax.all_to_all(reply, 'normal', 0, 0)  7.22 us
    ppermute x3, starting transfers between devices, on_device(): notes.append(lax.ppermute(own, 'wrap', pairs))  4.75 us
    unnamed x8, local copies, waits for them, and re-layouts  3.2 us
    ppermute x3, waiting for transfers between devices, on_device(): notes.append(lax.ppermute(own, 'wrap', pairs))  2.74 us
    ppermute x1, starting transfers between devices, on_device(): below = lax.ppermute(up, 'normal', rises)  2.36 us
    ppermute x1, starting transfers between devices, on_device(): above = lax.ppermute(down, 'normal', falls)  1.29 us
  transfers between devices with their start and end apart: 5, of which 3 were waited for; matrix products, arithmetic and copies ran while one was open for 0% of the time, Pallas kernels for 11%

profile of v1, /device:TPU:0, one launch (start us, length us, event | category | flops | bytes accessed | tf_op | source)
XLA Modules:
  0.0 45.7 jit_solution(17519159293844888994)
XLA Ops:
  0.0 0.9 %copy-done = f32[5,4,8,128]{3,2,1,0:T(8,128)S(1)} copy-done((f32[5,4,8,128]{3,2,1,0:T(8,128)S(1)}, f32[5,4,8,128]{3,2,1,0:T(8,128)}, u32[]{:S(2)}) %copy-start) | copy-done | bytes 81944
  0.9 0.0 copy-start.1
  0.9 0.8 %copy-done.1 = f32[4,4,8,128]{3,2,1,0:T(8,128)S(1)} copy-done((f32[4,4,8,128]{3,2,1,0:T(8,128)S(1)}, f32[4,4,8,128]{3,2,1,0:T(8,128)}, u32[]{:S(2)}) %copy-start.1) | copy-done | bytes 65560
  1.7 0.8 %copy-done.2 = f32[2,4,8,128]{3,2,1,0:T(8,128)S(1)} copy-done((f32[2,4,8,128]{3,2,1,0:T(8,128)S(1)}, f32[2,4,8,128]{3,2,1,0:T(8,128)}, u32[]{:S(2)}) %copy-start.2) | copy-done | bytes 32792
  2.5 0.7 %copy-done.3 = f32[4,8,128]{2,1,0:T(8,128)S(1)} copy-done((f32[4,8,128]{2,1,0:T(8,128)S(1)}, f32[4,8,128]{2,1,0:T(8,128)}, u32[]{:S(2)}) %copy-start.3) | copy-done | bytes 16408
  3.2 2.4 %collective-permute-start = (f32[9,4,128]{2,1,0:T(4,128)S(1)}, f32[9,4,128]{2,1,0:T(4,128)S(1)}, u32[]{:S(2)}, u32[]{:S(2)}) collective-permute-start(f32[9,4,128]{2,1,0:T(4,128)S(1)} %get-tuple-element.25.up), channel_id=1, source_target_pairs={{0,1},{1,2},{2,3},{3,4},{4,5},{5,6},{6,7},{8,9},{9,10},{10,11},{11... | collective-permute-start | bytes 55304 | tf_op jit(solution)/shard_map/ppermute | solution.py:788
  5.6 1.3 %collective-permute-start.1 = (f32[7,4,128]{2,1,0:T(4,128)S(1)}, f32[7,4,128]{2,1,0:T(4,128)S(1)}, u32[]{:S(2)}, u32[]{:S(2)}) collective-permute-start(f32[7,4,128]{2,1,0:T(4,128)S(1)} %get-tuple-element.26.down), channel_id=1, source_target_pairs={{1,0},{2,1},{3,2},{4,3},{5,4},{6,5},{7,6},{9,8},{10,9},{11,10},{12... | collective-permute-start | bytes 43016 | tf_op jit(solution)/shard_map/ppermute | solution.py:789
  6.9 0.3 wall_faces.1
  7.2 2.8 %wrap.1 = (f32[2,125,8,128]{3,2,1,0:T(8,128)S(1)}, f32[125,8,128]{2,1,0:T(8,128)S(1)}, f32[6,75,8,128]{3,2,1,0:T(8,128)S(1)}, f32[2,10,8,128]{3,2,1,0:T(8,128)S(1)}, f32[4,8,128]{2,1,0:T(8,128)S(1)}) custom-call(f32[5,4,8,128]{3,2,1,0:T(8,128)S(1)} %copy-done, f32[4,4,8,128]{3,2,1,0:T(8,128)S(1)} %copy-done.1, f32[4,8,128]{2,1,0:T(8,128)S(1)} %copy-done.3, ...), custom_call_target="tpu_custom_call" | custom-call | flops 41943040 | bytes 1048576 | tf_op jit(solution)/shard_map/wrap/pallas_call | solution.py:769
  10.0 0.7 %collective-permute-done.1.above = f32[7,4,128]{2,1,0:T(4,128)S(1)} collective-permute-done((f32[7,4,128]{2,1,0:T(4,128)S(1)}, f32[7,4,128]{2,1,0:T(4,128)S(1)}, u32[]{:S(2)}, u32[]{:S(2)}) %collective-permute-start.1) | collective-permute-done | bytes 14368 | tf_op jit(solution)/shard_map/ppermute | solution.py:789
  10.8 0.0 collective-permute-done.below
  10.8 0.9 %wrap_rhs.1 = (f32[20,8,128]{2,1,0:T(8,128)S(1)}, f32[4,8,128]{2,1,0:T(8,128)S(1)}, f32[45,8,128]{2,1,0:T(8,128)S(1)}) custom-call(f32[9,4,128]{2,1,0:T(4,128)S(1)} %collective-permute-done.below, f32[7,4,128]{2,1,0:T(4,128)S(1)} %collective-permute-done.1.above, f32[9,4,128]{2,1,0:T(4,128)S(1)} %get-tuple-element.25.up, ...), custom_call_target="tpu_custom_call" | custom-call | flops 8388608 | bytes 1048576 | tf_op jit(solution)/shard_map/wrap_rhs/pallas_call | solution.py:769
  11.7 3.7 %collective-permute-start.2 = (f32[4,8,128]{2,1,0:T(8,128)S(1)}, f32[4,8,128]{2,1,0:T(8,128)S(1)}, u32[]{:S(2)}, u32[]{:S(2)}) collective-permute-start(f32[4,8,128]{2,1,0:T(8,128)S(1)} %get-tuple-element.33.refs_0_), channel_id=1, source_target_pairs={{8,0},{16,8},{24,16},{0,24},{9,1},{17,9},{25,17},{1,25},{10,2},{18... | collective-permute-start | bytes 49160 | tf_op jit(solution)/shard_map/ppermute | solution.py:824
  15.4 0.0 collective-permute-start.3
  15.4 1.0 %collective-permute-start.4 = (f32[4,8,128]{2,1,0:T(8,128)S(1)}, f32[4,8,128]{2,1,0:T(8,128)S(1)}, u32[]{:S(2)}, u32[]{:S(2)}) collective-permute-start(f32[4,8,128]{2,1,0:T(8,128)S(1)} %get-tuple-element.33.refs_0_), channel_id=1, source_target_pairs={{24,0},{0,8},{8,16},{16,24},{25,1},{1,9},{9,17},{17,25},{26,2},{2,... | collective-permute-start | bytes 49160 | tf_op jit(solution)/shard_map/ppermute | solution.py:824
  16.5 1.8 %wall.1 = (f32[2,125,8,128]{3,2,1,0:T(8,128)S(1)}, f32[125,8,128]{2,1,0:T(8,128)S(1)}, f32[2,75,8,128]{3,2,1,0:T(8,128)S(1)}, f32[125,8,128]{2,1,0:T(8,128)S(1)}, f32[8,13,4,128]{3,2,1,0:T(4,128)S(1)}) custom-call(f32[2,2,45,8,128]{4,3,2,1,0:T(8,128)S(1)} %get-tuple-element.35.refs_0_, f32[45,8,128]{2,1,0:T(8,128)S(1)} %get-tuple-element.36.refs_1_), custom_call_target="tpu_custom_call" | custom-call | flops 20971520 | bytes 1048576 | tf_op jit(solution)/shard_map/wall/pallas_call | solution.py:769
  18.2 0.0 collective-permute-done.2.refs_1_
  18.2 1.8 %collective-permute-done.3.refs_2_ = f32[4,8,128]{2,1,0:T(8,128)S(1)} collective-permute-done((f32[4,8,128]{2,1,0:T(8,128)S(1)}, f32[4,8,128]{2,1,0:T(8,128)S(1)}, u32[]{:S(2)}, u32[]{:S(2)}) %collective-permute-start.3) | collective-permute-done | bytes 16416 | tf_op jit(solution)/shard_map/ppermute | solution.py:824
  20.1 0.9 %collective-permute-done.4.refs_3_ = f32[4,8,128]{2,1,0:T(8,128)S(1)} collective-permute-done((f32[4,8,128]{2,1,0:T(8,128)S(1)}, f32[4,8,128]{2,1,0:T(8,128)S(1)}, u32[]{:S(2)}, u32[]{:S(2)}) %collective-permute-start.4) | collective-permute-done | bytes 16416 | tf_op jit(solution)/shard_map/ppermute | solution.py:824
  21.0 1.9 %cycle.1 = (f32[8,15,4,128]{3,2,1,0:T(4,128)S(1)}, f32[20,8,128]{2,1,0:T(8,128)S(1)}, f32[5,8,128]{2,1,0:T(8,128)S(1)}) custom-call(f32[4,8,128]{2,1,0:T(8,128)S(1)} %get-tuple-element.33.refs_0_, f32[4,8,128]{2,1,0:T(8,128)S(1)} %collective-permute-done.2.refs_1_, f32[4,8,128]{2,1,0:T(8,128)S(1)} %collective-permute-done.3.refs_2_, ...), custom_call_target="tpu_custom_call" | custom-call | flops 10485760 | bytes 1048576 | tf_op jit(solution)/shard_map/cycle/pallas_call | solution.py:769
  22.9 12.8 %all_to_all.10.refs_0_ = f32[8,15,4,128]{3,2,1,0:T(4,128)S(1)} all-to-all(f32[8,15,4,128]{3,2,1,0:T(4,128)S(1)} %get-tuple-element.42), channel_id=1, replica_groups=mesh['wrap'=4,'normal'=8] {'normal'}, dimensions={0} | all-to-all | bytes 491520 | tf_op jit(solution)/shard_map/all_to_all | solution.py:858
  35.7 1.8 %open.1 = f32[8,2,4,128]{3,2,1,0:T(4,128)S(1)} custom-call(f32[8,15,4,128]{3,2,1,0:T(4,128)S(1)} %all_to_all.10.refs_0_), custom_call_target="tpu_custom_call" | custom-call | flops 10485760 | bytes 1048576 | tf_op jit(solution)/shard_map/open/pallas_call | solution.py:769
  37.5 7.2 %all_to_all.11.refs_0_ = f32[8,2,4,128]{3,2,1,0:T(4,128)S(1)} all-to-all(f32[8,2,4,128]{3,2,1,0:T(4,128)S(1)} %open.1), channel_id=1, replica_groups=mesh['wrap'=4,'normal'=8] {'normal'}, dimensions={0} | all-to-all | bytes 65536 | tf_op jit(solution)/shard_map/all_to_all | solution.py:866
  44.7 0.9 %finish.1 = f32[5,4,8,128]{3,2,1,0:T(8,128)} custom-call(f32[8,2,4,128]{3,2,1,0:T(4,128)S(1)} %all_to_all.11.refs_0_, f32[2,125,8,128]{3,2,1,0:T(8,128)S(1)} %get-tuple-element.37.refs_8_.refs_1_, f32[125,8,128]{2,1,0:T(8,128)S(1)} %get-tuple-element.38.refs_9_.refs_2_, f32[2,75,8,128]{3,2,1,0:T(8,128)S(1)} %get-tuple-element.39.refs_10_.refs_3_, ...), custom_call_target="tpu_custom_call" | custom-call | flops 4194304 | bytes 1048576 | tf_op jit(solution)/shard_map/finish/pallas_call | solution.py:769
  (4 shorter events, 0.0 us)
Async XLA Ops:
  0.0 0.9 %copy-start = (f32[5,4,8,128]{3,2,1,0:T(8,128)S(1)}, f32[5,4,8,128]{3,2,1,0:T(8,128)}, u32[]{:S(2)}) copy-start(f32[5,4,8,128]{3,2,1,0:T(8,128)} %state.5) | copy-start | bytes 245764
  0.9 0.8 %copy-start.1 = (f32[4,4,8,128]{3,2,1,0:T(8,128)S(1)}, f32[4,4,8,128]{3,2,1,0:T(8,128)}, u32[]{:S(2)}) copy-start(f32[4,4,8,128]{3,2,1,0:T(8,128)} %metrics.5) | copy-start | bytes 196612
  1.7 0.8 %copy-start.2 = (f32[2,4,8,128]{3,2,1,0:T(8,128)S(1)}, f32[2,4,8,128]{3,2,1,0:T(8,128)}, u32[]{:S(2)}) copy-start(f32[2,4,8,128]{3,2,1,0:T(8,128)} %spread.5) | copy-start | bytes 98308
  2.5 0.7 %copy-start.3 = (f32[4,8,128]{2,1,0:T(8,128)S(1)}, f32[4,8,128]{2,1,0:T(8,128)}, u32[]{:S(2)}) copy-start(f32[4,8,128]{2,1,0:T(8,128)} %step.5) | copy-start | bytes 49156
  3.2 7.5 %collective-permute-start = (f32[9,4,128]{2,1,0:T(4,128)S(1)}, f32[9,4,128]{2,1,0:T(4,128)S(1)}, u32[]{:S(2)}, u32[]{:S(2)}) collective-permute-start(f32[9,4,128]{2,1,0:T(4,128)S(1)} %get-tuple-element.25.up), channel_id=1, source_target_pairs={{0,1},{1,2},{2,3},{3,4},{4,5},{5,6},{6,7},{8,9},{9,10},{10,11},{11... | collective-permute-start | bytes 55304 | tf_op jit(solution)/shard_map/ppermute | solution.py:788
  5.6 5.2 %collective-permute-start.1 = (f32[7,4,128]{2,1,0:T(4,128)S(1)}, f32[7,4,128]{2,1,0:T(4,128)S(1)}, u32[]{:S(2)}, u32[]{:S(2)}) collective-permute-start(f32[7,4,128]{2,1,0:T(4,128)S(1)} %get-tuple-element.26.down), channel_id=1, source_target_pairs={{1,0},{2,1},{3,2},{4,3},{5,4},{6,5},{7,6},{9,8},{10,9},{11,10},{12... | collective-permute-start | bytes 43016 | tf_op jit(solution)/shard_map/ppermute | solution.py:789
  11.7 6.5 %collective-permute-start.2 = (f32[4,8,128]{2,1,0:T(8,128)S(1)}, f32[4,8,128]{2,1,0:T(8,128)S(1)}, u32[]{:S(2)}, u32[]{:S(2)}) collective-permute-start(f32[4,8,128]{2,1,0:T(8,128)S(1)} %get-tuple-element.33.refs_0_), channel_id=1, source_target_pairs={{8,0},{16,8},{24,16},{0,24},{9,1},{17,9},{25,17},{1,25},{10,2},{18... | collective-permute-start | bytes 49160 | tf_op jit(solution)/shard_map/ppermute | solution.py:824
  15.4 4.6 %collective-permute-start.3 = (f32[4,8,128]{2,1,0:T(8,128)S(1)}, f32[4,8,128]{2,1,0:T(8,128)S(1)}, u32[]{:S(2)}, u32[]{:S(2)}) collective-permute-start(f32[4,8,128]{2,1,0:T(8,128)S(1)} %get-tuple-element.33.refs_0_), channel_id=1, source_target_pairs={{16,0},{24,8},{0,16},{8,24},{17,1},{25,9},{1,17},{9,25},{18,2},{26... | collective-permute-start | bytes 49160 | tf_op jit(solution)/shard_map/ppermute | solution.py:824
  15.4 5.5 %collective-permute-start.4 = (f32[4,8,128]{2,1,0:T(8,128)S(1)}, f32[4,8,128]{2,1,0:T(8,128)S(1)}, u32[]{:S(2)}, u32[]{:S(2)}) collective-permute-start(f32[4,8,128]{2,1,0:T(8,128)S(1)} %get-tuple-element.33.refs_0_), channel_id=1, source_target_pairs={{24,0},{0,8},{8,16},{16,24},{25,1},{1,9},{9,17},{17,25},{26,2},{2,... | collective-permute-start | bytes 49160 | tf_op jit(solution)/shard_map/ppermute | solution.py:824

commit v2 on v1

--- a/solution.py
+++ b/solution.py
@@ -324,10 +324,6 @@
         low, mid_l, mid_r, upp = (get_mat(work, 25 * at) for at in range(4))
     for at, m in enumerate((low, mid_l, mid_r, upp)):
         put_mat(ends, 25 * at, m)
-    inverse = mat_inv(mat_add(mid_l, mid_r))
-    put_mat(keep3, 0, inverse, (steps,))
-    put_mat(keep3, 25, mat_mul(inverse, low), (steps,))
-    put_mat(keep3, 50, mat_mul(inverse, upp), (steps,))
 
 
 def line_forward(line, rhs_e, rhs_o, keep1, keep2, keep3, zs):
@@ -356,18 +352,14 @@
         back = 4 << level
         r_l = vec_sub(r_l, mat_vec(get_mat(keep3, 25, (level,)), line.vroll(z, back)))
         r_r = vec_sub(r_r, mat_vec(get_mat(keep3, 50, (level,)), line.vroll(z, -back)))
-    put_vec(zs, 15, mat_vec(get_mat(keep3, 0, (steps,)), vec_add(r_l, r_r)))
+    put_vec(zs, 15, vec_add(r_l, r_r))
     return r_r, r_l
 
 
-def line_backward(line, first, last, keep1, keep2, keep3, zs):
-    steps = line.count.bit_length() - 1
+def line_backward(line, first, last, keep1, keep2, tail, zs):
     inner = vec_sub(
-        get_vec(zs, 15),
-        vec_add(
-            mat_vec(get_mat(keep3, 25, (steps,)), first),
-            mat_vec(get_mat(keep3, 50, (steps,)), last),
-        ),
+        mat_vec(get_mat(tail, 0), get_vec(zs, 15)),
+        vec_add(mat_vec(get_mat(tail, 25), first), mat_vec(get_mat(tail, 50), last)),
     )
     even = vec_map(lambda x, y: jnp.where(line.group == 0, y, x), inner, first)
     ahead = vec_map(
@@ -399,16 +391,43 @@
     return out
 
 
-def halo_kernel(state, metrics, step, spread, up, down):
+def tails_kernel(ends_wrap, ends_wall, after, tail_wrap, tail_wall):
+    for ends, tail in ((ends_wrap, tail_wrap), (ends_wall, tail_wall)):
+        low, mid_l, mid_r, upp = (get_mat(ends, 25 * at) for at in range(4))
+        inverse = mat_inv(mat_add(mid_l, mid_r))
+        put_mat(tail, 0, inverse)
+        put_mat(tail, 25, mat_mul(inverse, low))
+        put_mat(tail, 50, mat_mul(inverse, upp))
+
+
+def odd_device(axis):
+    return (lax.axis_index(axis) & 1) == 1
+
+
+def either(flag, a, b):
+    return jnp.where(flag, a, b)
+
+
+def split_cells(cells):
+    return cells.at[0:5], cells.at[5:9], cells.at[9], cells.at[10:12]
+
+
+def enter_kernel(cells, pair, cross):
+    state, metrics, step, spread = split_cells(cells)
+    odd = odd_device("normal")
+
+    def send(c, s, rows):
+        first, last = rows(0), rows(7)
+        pair[c, s : s + 1, :] = either(odd, first, last)
+        cross[c, s : s + 1, :] = either(odd, last, first)
+
     for s in range(4):
         for c in range(5):
-            up[c, s : s + 1, :] = state[c, s, 7:8, :]
-            down[c, s : s + 1, :] = state[c, s, 0:1, :]
+            send(c, s, lambda k: state[c, s, k : k + 1, :])
         for c in range(2):
-            up[5 + c, s : s + 1, :] = metrics[2 + c, s, 7:8, :]
-            down[5 + c, s : s + 1, :] = metrics[2 + c, s, 0:1, :]
-        up[7, s : s + 1, :] = step[s, 7:8, :]
-        up[8, s : s + 1, :] = spread[1, s, 7:8, :]
+            send(5 + c, s, lambda k: metrics[2 + c, s, k : k + 1, :])
+        send(7, s, lambda k: step[s, k : k + 1, :])
+        send(8, s, lambda k: spread[1, s, k : k + 1, :])
 
 
 def load_cells(line, state, metrics, step, spread, t, metric_at, spread_at):
@@ -426,7 +445,8 @@
     return vec_sub(line.vroll(flux_o, 2), flux_e), vec_sub(flux_e, flux_o)
 
 
-def wrap_kernel(state, metrics, step, spread, keep1, keep2, keep3, rhs, note, ends, work):
+def wrap_kernel(cells, keep1, keep2, keep3, rhs, note, ends, work):
+    state, metrics, step, spread = split_cells(cells)
     line = Line(1)
     states = []
     note[...] = jnp.zeros_like(note)
@@ -458,8 +478,10 @@
         note[k] = packed[k]
 
 
-def wall_faces_kernel(state, metrics, step, spread, coefs, rhs):
+def wall_kernel(cells, keep1, keep2, keep3, rhs, ends):
+    state, metrics, step, spread = split_cells(cells)
     line = Line(0)
+    states = []
     for t in range(2):
         cells_e, cells_o = load_cells(line, state, metrics, step, spread, t, 2, 1)
         after_e, after_o = line_faces(line, cells_e, cells_o)
@@ -468,42 +490,138 @@
             a, b = line.unpack1(rhs_e[c], rhs_o[c])
             rhs[2 * t, c] = a
             rhs[2 * t + 1, c] = b
-        for half, face in enumerate((after_e, after_o)):
-            for which in range(3):
-                at = 0
-                for i in range(5):
-                    for j in range(i, 5):
-                        coefs[t, half, 15 * which + at] = face[which][i][j]
-                        at += 1
-
-
-def get_face(ref, lead):
-    out = []
-    for which in range(3):
-        m = [[None] * 5 for _ in range(5)]
-        at = 0
-        for i in range(5):
-            for j in range(i, 5):
-                m[i][j] = m[j][i] = ref[lead + (15 * which + at,)]
-                at += 1
-        out.append(m)
-    return out + [None]
-
-
-def wrap_rhs_kernel(
-    below, above, up, down, rhs_wall, rhs_wrap, note, keep1, keep2, keep3, zs, sent, edge
-):
+        states.append(first_level(line, after_e, after_o, keep1, t))
+    line_levels(line, states, keep1, keep2, keep3, ends, None)
+
+
+def close_kernel(pair, cross, from_pair, from_cross, ends, after, flux, close, segment):
+    odd = odd_device("normal")
+    left, right = [], []
+    for c in range(9):
+        below = either(odd, from_pair[c], from_cross[c])
+        own = either(odd, cross[c], pair[c])
+        left.append(jnp.concatenate([below, own], axis=0))
+    for c in range(7):
+        above = either(odd, from_cross[c], from_pair[c])
+        own = either(odd, pair[c], cross[c])
+        right.append(jnp.concatenate([own, above], axis=0))
+    damp, lower, upper, through = face_values(left, right)
+    put_vec(flux, 0, through)
+    wall = Line(0)
+    damp_f, low_f, upp_f = (
+        mat_map(lambda x: wall.roll(x, 4), m) for m in (damp, lower, upper)
+    )
+    low, mid_l, mid_r, upp = (get_mat(ends, 25 * at) for at in range(4))
+    inverse = mat_inv(plus_eye(mat_add(mid_l, damp_f)))
+    w_low = mat_mul(inverse, low)
+    w_upp = mat_mul(inverse, upp_f)
+    put_mat(close, 0, inverse)
+    put_mat(close, 25, upp)
+    put_mat(close, 50, low_f)
+    put_mat(close, 75, w_low)
+    put_mat(close, 100, w_upp)
+    mid_r = mat_sub(mid_r, mat_mul(upp, w_low))
+    upp = mat_neg(mat_mul(upp, w_upp))
+    low = mat_neg(mat_mul(low_f, w_low))
+    mid_l = mat_sub(damp_f, mat_mul(low_f, w_upp))
+    for at, m in enumerate((mid_r, upp, low, mid_l)):
+        put_mat(segment, 25 * at, mat_map(lambda x: x[0:4], m))
+
+
+def segment_mats(ref):
+    return [get_mat(ref, 25 * at) for at in range(4)]
+
+
+def tree_bit(level):
+    return ((lax.axis_index("normal") >> level) & 1) == 1
+
+
+def tree_nodes(level):
+    nodes = []
+    for at in range(level):
+        nodes = [(at, 0)] + nodes + [(i, k + (1 << at)) for i, k in nodes]
+    return nodes
+
+
+def merge_kernel(own, other, after, node, message, *extra, level, shared, last):
+    upside = tree_bit(level)
+    mine, theirs = segment_mats(own), segment_mats(other)
+    lower = [mat_map(lambda a, b: either(upside, b, a), m, t) for m, t in zip(mine, theirs)]
+    upper = [mat_map(lambda a, b: either(upside, a, b), m, t) for m, t in zip(mine, theirs)]
+    inverse = mat_inv(mat_add(lower[3], upper[0]))
+    w_low = mat_mul(inverse, lower[2])
+    up_in = mat_mul(lower[1], inverse)
+    low_in = mat_mul(upper[2], inverse)
+    w_upp = mat_mul(inverse, upper[1])
+    for at, m in enumerate((inverse, up_in, low_in, w_low, w_upp)):
+        put_mat(node, 25 * at, m)
+    mid_r = mat_sub(lower[0], mat_mul(lower[1], w_low))
+    upp = mat_neg(mat_mul(lower[1], w_upp))
+    low = mat_neg(mat_mul(upper[2], w_low))
+    mid_l = mat_sub(upper[3], mat_mul(upper[2], w_upp))
+    at = 100
+    if last:
+        top = tree_bit(level + 1)
+        first = mat_inv(mid_r)
+        through = mat_map(lambda x: either(top, 0.0, x), mat_mul(low, first))
+        core = mat_map(
+            lambda a, b: either(top, a, b), mid_r, mat_sub(mid_l, mat_mul(through, upp))
+        )
+        put_mat(extra[0], 0, core)
+        put_mat(extra[0], 25, through)
+        put_mat(extra[0], 50, first)
+        put_mat(extra[0], 75, upp)
+        put_mat(message, 0, core)
+        put_mat(message, 25, through)
+        put_mat(
+            message,
+            50,
+            mat_map(
+                lambda a, b: either(top, a, b), up_in, mat_sub(low_in, mat_mul(through, up_in))
+            ),
+        )
+        at = 75
+    else:
+        for i, m in enumerate((mid_r, upp, low, mid_l)):
+            put_mat(message, 25 * i, m)
+        if shared is not None:
+            put_mat(message, at, up_in)
+            put_mat(message, at + 25, low_in)
+            at += 50
+    for source in (own, other):
+        for c in range(50 * (shared or 0)):
+            message[at] = source[100 + c]
+            at += 1
+
+
+def middle_kernel(own, other, inverse):
+    put_mat(inverse, 0, mat_inv(mat_add(get_mat(own, 0), get_mat(other, 0))))
+
+
+def merge_loads(upside, up_in, low_in, mine, theirs):
+    lower = [vec_map(lambda a, b: either(upside, b, a), m, t) for m, t in zip(mine, theirs)]
+    upper = [vec_map(lambda a, b: either(upside, a, b), m, t) for m, t in zip(mine, theirs)]
+    load = vec_add(lower[1], upper[0])
+    right = vec_sub(lower[0], mat_vec(up_in, load))
+    left = vec_sub(upper[1], mat_vec(low_in, load))
+    return load, (right, left)
+
+
+def in_order(position, count):
+    def pick(values, q):
+        ks = sorted({c ^ ((c + q) % count) for c in range(count)})
+        wanted = position ^ ((position + q) % count)
+        out = values[ks[0]]
+        for k in ks[1:]:
+            out = jnp.where(wanted == k, values[k], out)
+        return out
+
+    return pick
+
+
+def wrap_rhs_kernel(flux, rhs_wall, rhs_wrap, note, keep1, keep2, keep3, zs, sent):
     line, wall = Line(1), Line(0)
-    left = [jnp.concatenate([below[c], up[c]], axis=0) for c in range(9)]
-    right = [jnp.concatenate([down[c], above[c]], axis=0) for c in range(7)]
-    face = face_values(left, right)
-    for which in range(3):
-        at = 0
-        for i in range(5):
-            for j in range(i, 5):
-                edge[15 * which + at] = wall.roll(face[which][i][j], 4)
-                at += 1
-    flux = face[3]
+    through = get_vec(flux, 0)
     rhs_e, rhs_o = [], []
     for t in range(2):
         spans = []
@@ -511,8 +629,8 @@
             values = []
             for c in range(5):
                 x = rhs_wall[s, c]
-                x = jnp.where(wall.at == 0, x + wall.roll(flux[c], -s), x)
-                x = jnp.where(wall.at == 7, x - wall.roll(flux[c], 3 - s), x)
+                x = jnp.where(wall.at == 0, x + wall.roll(through[c], -s), x)
+                x = jnp.where(wall.at == 7, x - wall.roll(through[c], 3 - s), x)
                 values.append(x)
             spans.append(values)
         packed = [line.pack1(a, b) for a, b in zip(*spans)]
@@ -529,64 +647,14 @@
     sent[3] = tail
 
 
-def transpose_blocks(rows, count):
-    width = LANES // count
-    at = lax.broadcasted_iota(jnp.int32, rows[0].shape, 1)
-    block = at // width
-    bit = 1
-    while bit < count:
-        clear = (block & bit) == 0
-        new = [None] * count
-        for m in range(count):
-            if m & bit:
-                continue
-            a, b = rows[m], rows[m | bit]
-            new[m] = jnp.where(clear, a, pltpu.roll(b, bit * width, 1))
-            new[m | bit] = jnp.where(clear, pltpu.roll(a, LANES - bit * width, 1), b)
-        rows = new
-        bit *= 2
-    return rows
-
-
-def wall_kernel(coefs, edge, keep1, keep2, keep3, close, parcel, ends, *, count):
-    line = Line(0)
-    states = []
-    for t in range(2):
-        after_e = get_face(coefs, (t, 0))
-        after_o = get_face(coefs, (t, 1))
-        states.append(first_level(line, after_e, after_o, keep1, t))
-    line_levels(line, states, keep1, keep2, keep3, ends, None)
-    low, mid_l, mid_r, upp = (get_mat(ends, 25 * at) for at in range(4))
-    damp_f, low_f, upp_f, _ = get_face(edge, ())
-    inverse = mat_inv(plus_eye(mat_add(mid_l, damp_f)))
-    w_low = mat_mul(inverse, low)
-    w_upp = mat_mul(inverse, upp_f)
-    put_mat(close, 0, inverse)
-    put_mat(close, 25, upp)
-    put_mat(close, 50, low_f)
-    put_mat(close, 75, w_low)
-    put_mat(close, 100, w_upp)
-    final = [
-        mat_sub(mid_r, mat_mul(upp, w_low)),
-        mat_neg(mat_mul(upp, w_upp)),
-        mat_neg(mat_mul(low_f, w_low)),
-        mat_sub(damp_f, mat_mul(low_f, w_upp)),
+def cycle_kernel(*refs, count):
+    arrived = refs[:count]
+    (keep1, keep2, tail, zs, wkeep1, wkeep2, wkeep3, close) = refs[count : count + 8]
+    sent, wzs, closed = refs[count + 8 :]
+    pick = in_order(lax.axis_index("wrap"), count)
+    notes = [
+        [pick([ref[k] for ref in arrived], q) for k in range(4)] for q in range(count)
     ]
-    rows = [x[0:4] for m in final for r in m for x in r]
-    zero = jnp.zeros((4, LANES), jnp.float32)
-    rows += [zero] * (-len(rows) % count)
-    for k in range(len(rows) // count):
-        out = transpose_blocks(rows[k * count : (k + 1) * count], count)
-        for d in range(count):
-            parcel[d, k] = out[d]
-
-
-def cycle_kernel(
-    *refs, count, wall_count
-):
-    notes = refs[:count]
-    (keep1, keep2, keep3, zs, wkeep1, wkeep2, wkeep3, close, parcel) = refs[count : count + 9]
-    sent, wzs, closed = refs[count + 9 :]
     line = Line(1)
     period = 4 * count
     repeat = line.at % period
@@ -655,7 +723,7 @@
     spread = line.at & 3
     first = [jnp.take_along_axis(y, spread, axis=1) for y in x]
     last = [jnp.take_along_axis(y, spread, axis=1) for y in b]
-    swept = line_backward(line, first, last, keep1, keep2, keep3, zs)
+    swept = line_backward(line, first, last, keep1, keep2, tail, zs)
 
     wall = Line(0)
     rhs_e, rhs_o = [], []
@@ -663,154 +731,179 @@
         packed = [wall.pack1(p, q) for p, q in zip(swept[2 * t], swept[2 * t + 1])]
         rhs_e.append([p[0] for p in packed])
         rhs_o.append([p[1] for p in packed])
-    r_r, r_l = line_forward_wall(wall, rhs_e, rhs_o, wkeep1, wkeep2, wkeep3, wzs)
+    r_r, r_l = line_forward(wall, rhs_e, rhs_o, wkeep1, wkeep2, wkeep3, wzs)
     zb = mat_vec(get_mat(close, 0), r_l)
     put_vec(closed, 0, zb)
     out_r = vec_sub(r_r, mat_vec(get_mat(close, 25), zb))
     out_l = vec_map(lambda y: -y, mat_vec(get_mat(close, 50), zb))
-    rows = [y[0:4] for y in out_r + out_l]
-    zero = jnp.zeros((4, LANES), jnp.float32)
-    rows += [zero] * (-len(rows) % wall_count)
-    base = parcel.shape[1]
-    for k in range(base):
-        for d in range(wall_count):
-            sent[d, k] = parcel[d, k]
-    for k in range(len(rows) // wall_count):
-        out = transpose_blocks(rows[k * wall_count : (k + 1) * wall_count], wall_count)
-        for d in range(wall_count):
-            sent[d, base + k] = out[d]
-
-
-def line_forward_wall(wall, rhs_e, rhs_o, keep1, keep2, keep3, zs):
-    return line_forward(wall, rhs_e, rhs_o, keep1, keep2, keep3, zs)
-
-
-def open_kernel(got, reply, *, count):
-    width = LANES // count
-    base = -(-100 // count)
-
-    def unpack(k):
-        return transpose_blocks([got[q, k] for q in range(count)], count)
-
-    flat = [x for k in range(base) for x in unpack(k)][:100]
-    tail = [x for k in range(base, got.shape[1]) for x in unpack(k)][:10]
-
-    def mat_at(at):
-        return [[flat[at + 5 * i + j] for j in range(5)] for i in range(5)]
-
-    mid_r, upp, low, mid_l = (mat_at(25 * i) for i in range(4))
-    at = lax.broadcasted_iota(jnp.int32, (4, LANES), 1)
-    not_first = at >= width
-    not_last = at < LANES - width
-
-    def shift(x, by):
-        return pltpu.roll(x, by % LANES, 1)
-
-    def from_back(x):
-        return jnp.where(not_first, shift(x, width), 0.0)
-
-    mid = mat_add(mid_r, mat_map(from_back, mid_l))
-    back = mat_map(from_back, low)
-    ahead = mat_map(lambda x: jnp.where(not_last, x, 0.0), upp)
-    load = vec_add(tail[0:5], vec_map(from_back, tail[5:10]))
-    reach = 1
-    while reach < count:
-        by = width * reach
-        inverse = mat_inv(mid)
-        wb, wa, z = mat_mul(inverse, back), mat_mul(inverse, ahead), mat_vec(inverse, load)
-        behind = lambda m: mat_map(lambda x: shift(x, by), m)
-        beyond = lambda m: mat_map(lambda x: shift(x, -by), m)
-        mid = mat_sub(mid, mat_add(mat_mul(back, behind(wa)), mat_mul(ahead, beyond(wb))))
-        load = vec_sub(
-            load,
-            vec_add(
-                mat_vec(back, [shift(x, by) for x in z]),
-                mat_vec(ahead, [shift(x, -by) for x in z]),
-            ),
-        )
-        if 2 * reach < count:
-            back, ahead = (
-                mat_neg(mat_mul(back, behind(wb))),
-                mat_neg(mat_mul(ahead, beyond(wa))),
+    put_vec(sent, 0, [y[0:4] for y in out_r])
+    put_vec(sent, 5, [y[0:4] for y in out_l])
+
+
+def joint_rhs_kernel(own, other, joint, middle, sent):
+    mine = (get_vec(own, 0), get_vec(own, 5))
+    theirs = (get_vec(other, 0), get_vec(other, 5))
+    load, (right, left) = merge_loads(
+        tree_bit(0), get_mat(joint, 25), get_mat(joint, 50), mine, theirs
+    )
+    put_vec(middle, 0, mat_vec(get_mat(joint, 0), load))
+    put_vec(sent, 0, right)
+    put_vec(sent, 5, left)
+
+
+def finish_kernel(*refs, levels):
+    count = 1 << levels
+    arrived, refs = refs[:count], refs[count:]
+    nodes, others, refs = refs[: levels - 1], refs[levels - 1 : 2 * levels - 1], refs[2 * levels - 1 :]
+    (half, centre, joint, middle, keep1, keep2, tail, close, closed, zs, field) = refs
+    line = Line(0)
+    whole = levels - 1
+    shared = {}
+    for level in range(whole):
+        for at, (i, k) in enumerate(tree_nodes(level)):
+            shared[i, k + (1 << level)] = (others[level], 100 + 50 * at)
+    for at, (i, k) in enumerate(tree_nodes(whole)[1:]):
+        shared[i, k + (1 << whole)] = (others[whole], 75 + 50 * at)
+    loads = {k: (get_vec(ref, 0), get_vec(ref, 5)) for k, ref in enumerate(arrived)}
+    middles = []
+    top = tree_bit(levels)
+    for level in range(whole):
+        upside = tree_bit(level + 1)
+        merged = {}
+        for k in range(0, count, 2 << level):
+            mine, theirs = loads[k], loads[k + (1 << level)]
+            if level == whole - 1 and k:
+                low, upp = (
+                    [vec_map(lambda a, b: either(upside, b, a), m, t) for m, t in zip(mine, theirs)],
+                    [vec_map(lambda a, b: either(upside, a, b), m, t) for m, t in zip(mine, theirs)],
+                )
+                merged[k] = vec_sub(
+                    vec_map(lambda a, b: either(top, a, b), upp[1], low[0]),
+                    vec_add(
+                        mat_vec(get_mat(others[whole], 50), vec_add(low[1], upp[0])),
+                        mat_vec(get_mat(others[whole], 25), low[0]),
+                    ),
+                )
+                continue
+            ref, at = shared[level, k] if k else (nodes[level], 25)
+            load, merged[k] = merge_loads(
+                upside, get_mat(ref, at), get_mat(ref, at + 25), mine, theirs
             )
-        reach *= 2
-    x = mat_vec(mat_inv(mid), load)
-    nexts = [jnp.where(not_last, shift(y, -width), 0.0) for y in x]
-    rows = x + nexts
-    rows += [jnp.zeros((4, LANES), jnp.float32)] * (-len(rows) % count)
-    for k in range(len(rows) // count):
-        out = transpose_blocks(rows[k * count : (k + 1) * count], count)
-        for d in range(count):
-            reply[d, k] = out[d]
-
-
-def finish_kernel(got, keep1, keep2, keep3, close, closed, zs, field, *, count):
-    line = Line(0)
-    rows = [
-        x
-        for k in range(got.shape[1])
-        for x in transpose_blocks([got[q, k] for q in range(count)], count)
-    ]
-    twice = [jnp.concatenate([x, x], axis=0) for x in rows[:10]]
-    first, nexts = twice[0:5], twice[5:10]
+            if k == 0:
+                middles.append(mat_vec(get_mat(nodes[level], 0), load))
+        loads = merged
+    right, left = loads[0]
+    load = vec_add(
+        loads[1 << whole],
+        vec_map(
+            lambda a, b: either(top, a, b),
+            right,
+            vec_sub(left, mat_vec(get_mat(half, 25), right)),
+        ),
+    )
+    between = mat_vec(get_mat(centre, 0), load)
+    below = mat_vec(
+        get_mat(half, 50), vec_sub(right, mat_vec(get_mat(half, 75), between))
+    )
+    below, above = (
+        vec_map(lambda a, b: either(top, b, a), below, between),
+        vec_map(lambda b: either(top, 0.0, b), between),
+    )
+    path = [(tree_bit(i + 1), nodes[i], middles[i]) for i in reversed(range(whole))]
+    path.append((tree_bit(0), joint, get_vec(middle, 0)))
+    for upside, node, z in path:
+        between = vec_sub(
+            z,
+            vec_add(mat_vec(get_mat(node, 75), below), mat_vec(get_mat(node, 100), above)),
+        )
+        below, above = (
+            vec_map(lambda a, b: either(upside, b, a), below, between),
+            vec_map(lambda a, b: either(upside, b, a), between, above),
+        )
+    first, nexts = below, above
+    first = [jnp.concatenate([x, x], axis=0) for x in first]
+    nexts = [jnp.concatenate([x, x], axis=0) for x in nexts]
     last = vec_sub(
         get_vec(closed, 0),
         vec_add(mat_vec(get_mat(close, 75), first), mat_vec(get_mat(close, 100), nexts)),
     )
     last = [jnp.where(line.at < 4, x, line.roll(x, 4)) for x in last]
-    out = line_backward(line, first, last, keep1, keep2, keep3, zs)
+    out = line_backward(line, first, last, keep1, keep2, tail, zs)
     for s in range(4):
         for c in range(5):
             field[c, s] = out[s][c]
 
 
 def call(kernel, name, shapes, flops, *args, scratch=()):
-    spec = pl.BlockSpec(memory_space=pltpu.VMEM)
+    place = pl.BlockSpec(memory_space=pltpu.VMEM)
     return pl.pallas_call(
         kernel,
         name=name,
         out_shape=[jax.ShapeDtypeStruct(s, jnp.float32) for s in shapes],
-        in_specs=[spec] * len(args),
-        out_specs=[spec] * len(shapes),
-        scratch_shapes=[pltpu.VMEM(s, jnp.float32) for s in scratch],
+        in_specs=[pl.BlockSpec(memory_space=pltpu.VMEM)] * len(args),
+        out_specs=[place] * len(shapes),
+        scratch_shapes=[
+            pltpu.VMEM(s, jnp.float32) if isinstance(s, tuple) else s for s in scratch
+        ],
         compiler_params=pltpu.CompilerParams(vmem_limit_bytes=VMEM_LIMIT),
         cost_estimate=pl.CostEstimate(flops=flops, bytes_accessed=1 << 20, transcendentals=0),
     )(*args)
 
 
+def swapped(x, axis, count, by):
+    return lax.ppermute(x, axis, [(i, i ^ by) for i in range(count)])
+
+
 def on_device(state, metrics, time_step, dissipation, *, wrap_count, wall_count):
-    inputs = (state, metrics, time_step, dissipation)
-    up, down = call(
-        halo_kernel, "halo", [(9, 4, LANES), (7, 4, LANES)], 1 << 12, *inputs
-    )
-    rises = [(i, i + 1) for i in range(wall_count - 1)]
-    falls = [(i + 1, i) for i in range(wall_count - 1)]
-    below = lax.ppermute(up, "normal", rises)
-    above = lax.ppermute(down, "normal", falls)
-    keep1, keep2, keep3, rhs_wrap, note = call(
+    levels = wall_count.bit_length() - 2
+    row = (4, LANES)
+    cells = jnp.concatenate([state, metrics, time_step[None], dissipation], axis=0)
+    pair, cross = call(enter_kernel, "enter", [(9,) + row, (9,) + row], 1 << 12, cells)
+    across = [(i, i + 1) for i in range(1, wall_count - 1, 2)]
+    across += [(b, a) for a, b in across]
+    from_pair = swapped(pair, "normal", wall_count, 1)
+    from_cross = lax.ppermute(cross, "normal", across)
+    wkeep1, wkeep2, wkeep3, rhs_wall, wends = call(
+        wall_kernel,
+        "wall",
+        [(2, 125) + TILE, (125,) + TILE, (1, 75) + TILE, (4, 5) + TILE, (100,) + TILE],
+        20 << 20,
+        cells,
+    )
+    keep1, keep2, keep3, rhs_wrap, note, ends = call(
         wrap_kernel,
         "wrap",
-        [(2, 125) + TILE, (125,) + TILE, (6, 75) + TILE, (2, 10) + TILE, (4,) + TILE],
+        [
+            (2, 125) + TILE,
+            (125,) + TILE,
+            (5, 75) + TILE,
+            (2, 10) + TILE,
+            (4,) + TILE,
+            (100,) + TILE,
+        ],
         40 << 20,
-        *inputs,
-        scratch=[(100,) + TILE, (100,) + TILE],
-    )
-    coefs, rhs_wall = call(
-        wall_faces_kernel,
-        "wall_faces",
-        [(2, 2, 45) + TILE, (4, 5) + TILE],
-        8 << 20,
-        *inputs,
-    )
-    zs, own, edge = call(
+        cells,
+        scratch=[(100,) + TILE],
+    )
+    flux, close, segment = call(
+        close_kernel,
+        "close",
+        [(5,) + TILE, (125,) + TILE, (100,) + row],
+        4 << 20,
+        pair,
+        cross,
+        from_pair,
+        from_cross,
+        wends,
+        note,
+    )
+    beside = swapped(segment, "normal", wall_count, 1)
+    zs, own = call(
         wrap_rhs_kernel,
         "wrap_rhs",
-        [(20,) + TILE, (4,) + TILE, (45,) + TILE],
+        [(20,) + TILE, (4,) + TILE],
         8 << 20,
-        below,
-        above,
-        up,
-        down,
+        flux,
         rhs_wall,
         rhs_wrap,
         note,
@@ -818,61 +911,75 @@
         keep2,
         keep3,
     )
-    notes = [own]
-    for by in range(1, wrap_count):
-        pairs = [((i + by) % wrap_count, i) for i in range(wrap_count)]
-        notes.append(lax.ppermute(own, "wrap", pairs))
-    groups = -(-100 // wall_count)
-    tails = -(-10 // wall_count)
-    wkeep1, wkeep2, wkeep3, close, parcel = call(
-        lambda *refs: wall_kernel(*refs, count=wall_count),
-        "wall",
-        [
-            (2, 125) + TILE,
-            (125,) + TILE,
-            (2, 75) + TILE,
-            (125,) + TILE,
-            (wall_count, groups, 4, LANES),
-        ],
-        20 << 20,
-        coefs,
-        edge,
-        scratch=[(100,) + TILE],
+    notes = [own] + [swapped(own, "wrap", wrap_count, k) for k in range(1, wrap_count)]
+    tail, wtail = call(
+        tails_kernel, "tails", [(75,) + TILE, (75,) + TILE], 6 << 20, ends, wends, own
+    )
+    joint, message = call(
+        lambda *refs: merge_kernel(*refs, level=0, shared=None, last=False),
+        "merge",
+        [(125,) + row, (100,) + row],
+        4 << 20,
+        segment,
+        beside,
+        own,
     )
     sent, wzs, closed = call(
-        lambda *refs: cycle_kernel(*refs, count=wrap_count, wall_count=wall_count),
+        lambda *refs: cycle_kernel(*refs, count=wrap_count),
         "cycle",
-        [(wall_count, groups + tails, 4, LANES), (20,) + TILE, (5,) + TILE],
+        [(10,) + row, (20,) + TILE, (5,) + TILE],
         10 << 20,
         *notes,
         keep1,
         keep2,
-        keep3,
+        tail,
         zs,
         wkeep1,
         wkeep2,
         wkeep3,
         close,
-        parcel,
-    )
-    got = lax.all_to_all(sent, "normal", 0, 0)
-    (reply,) = call(
-        lambda *refs: open_kernel(*refs, count=wall_count),
-        "open",
-        [(wall_count, tails, 4, LANES)],
-        10 << 20,
-        got,
-    )
-    answer = lax.all_to_all(reply, "normal", 0, 0)
+    )
+    nodes, others = [], []
+    for level in range(levels - 1):
+        other = swapped(message, "normal", wall_count, 2 << level)
+        final = level == levels - 2
+        shared = len(tree_nodes(level))
+        handed = 75 + 100 * shared if final else 150 + 100 * shared
+        shapes = [(125,) + row, (handed,) + row] + ([(100,) + row] if final else [])
+        node, message, *half = call(
+            lambda *refs: merge_kernel(*refs, level=level + 1, shared=shared, last=final),
+            "merge_%d" % (level + 1),
+            shapes,
+            4 << 20,
+            message,
+            other,
+            sent,
+        )
+        nodes.append(node)
+        others.append(other)
+    other = swapped(message, "normal", wall_count, 1 << levels)
+    others.append(other)
+    (centre,) = call(middle_kernel, "middle", [(25,) + row], 1 << 16, message, other)
+    partner = swapped(sent, "normal", wall_count, 1)
+    middle, load = call(
+        joint_rhs_kernel, "joint_rhs", [(5,) + row, (10,) + row], 1 << 16, sent, partner, joint
+    )
+    loads = [load] + [swapped(load, "normal", wall_count, 2 * k) for k in range(1, 1 << levels)]
     (field,) = call(
-        lambda *refs: finish_kernel(*refs, count=wall_count),
+        lambda *refs: finish_kernel(*refs, levels=levels),
         "finish",
         [(5, 4) + TILE],
         4 << 20,
-        answer,
+        *loads,
+        *nodes,
+        *others,
+        *half,
+        centre,
+        joint,
+        middle,
         wkeep1,
         wkeep2,
-        wkeep3,
+        wtail,
         close,
         closed,
         wzs,

time: 46.1 us -> 34.2 us (0.74)
  blocking collectives: 20 us -> 0 us
  starting transfers between devices: 8.4 us -> 15.6 us
  waiting for transfers between devices: 3.49 us -> 8.23 us
  local copies, waits for them, and re-layouts: 3.2 us -> 0 us
  Pallas kernels: 10.5 us -> 9.16 us
  other arithmetic: 0 us -> 0.97 us
    all_to_all x2 -> x0, blocking collectives: 20 us -> none  [the longest x1 12.8 us: on_device(): got = lax.all_to_all(sent, 'normal', 0, 0)]
    ppermute x5 -> x12, starting transfers between devices: 8.4 us -> 15.6 us  [the longest x11 14.9 us: swapped(): return lax.ppermute(x, axis, [(i, i ^ by) for i in range(count)])]
    ppermute x5 -> x12, waiting for transfers between devices: 3.49 us -> 8.23 us  [the longest x11 8.22 us: swapped(): return lax.ppermute(x, axis, [(i, i ^ by) for i in range(count)])]
    unnamed x8 -> x0, local copies, waits for them, and re-layouts: 3.2 us -> none
    pallas_call x8 -> x12, Pallas kernels: 10.5 us -> 9.16 us  [call(): pl.pallas_call(kernel, name=name, out_shape=[jax.ShapeDtypeStruct(s, jnp....]
    concatenate x0 -> x1, other arithmetic: none -> 0.97 us  [on_device(): jnp.concatenate([state, metrics, time_step[None], dissipation], axis=0)]
  transfers between devices with their start and end apart: 5 -> 12, of which waited for: 3 -> 7; matrix products, arithmetic and copies ran while one was open for 0% -> 0% of each run, Pallas kernels for 11% -> 21%
where the time goes in v2:
time: 34.2 us; the launch traced here: 34 us
  starting transfers between devices  15.6 us (46%)
  Pallas kernels  9.16 us (27%)
  waiting for transfers between devices  8.23 us (24%)
  other arithmetic  0.97 us (3%)
    ppermute x11, starting transfers between devices, swapped(): return lax.ppermute(x, axis, [(i, i ^ by) for i in range(count)])  14.9 us
    pallas_call x12, Pallas kernels, call(): pl.pallas_call(kernel, name=name, out_shape=[jax.ShapeDtypeStruct(s, jnp....  9.16 us
    ppermute x11, waiting for transfers between devices, swapped(): return lax.ppermute(x, axis, [(i, i ^ by) for i in range(count)])  8.22 us
    concatenate x1, other arithmetic, on_device(): jnp.concatenate([state, metrics, time_step[None], dissipation], axis=0)  0.97 us
  transfers between devices with their start and end apart: 12, of which 7 were waited for; matrix products, arithmetic and copies ran while one was open for 0% of the time, Pallas kernels for 21%

profile of v2, /device:TPU:0, one launch (start us, length us, event | category | flops | bytes accessed | tf_op | source)
XLA Modules:
  0.0 34.0 jit_solution(8780260239711968068)
XLA Ops:
  0.0 1.0 %pad_maximum_fusion.cells = f32[12,4,8,128]{3,2,1,0:T(8,128)S(1)} fusion(f32[2,4,8,128]{3,2,1,0:T(8,128)} %param.7, f32[1,4,8,128]{3,2,1,0:T(8,128)} %bitcast.1, f32[4,4,8,128]{3,2,1,0:T(8,128)} %param.5, f32[5,4,8,128]{3,2,1,0:T(8,128)} %param.4), kind=kLoop, calls=%fused_computation | loop fusion | flops 147456 | bytes 393216 | tf_op jit(solution)/shard_map/concatenate | solution.py:860
  1.0 0.5 %collective-permute-start = (f32[9,4,128]{2,1,0:T(4,128)S(1)}, f32[9,4,128]{2,1,0:T(4,128)S(1)}, u32[]{:S(2)}, u32[]{:S(2)}) collective-permute-start(f32[9,4,128]{2,1,0:T(4,128)S(1)} %get-tuple-element.35.pair), channel_id=1, source_target_pairs={{0,1},{1,0},{2,3},{3,2},{4,5},{5,4},{6,7},{7,6},{8,9},{9,8},{10,11... | collective-permute-start | bytes 55304 | tf_op jit(solution)/shard_map/ppermute | solution.py:854
  1.5 0.7 %collective-permute-start.1 = (f32[9,4,128]{2,1,0:T(4,128)S(1)}, f32[9,4,128]{2,1,0:T(4,128)S(1)}, u32[]{:S(2)}, u32[]{:S(2)}) collective-permute-start(f32[9,4,128]{2,1,0:T(4,128)S(1)} %get-tuple-element.36.cross), channel_id=1, source_target_pairs={{1,2},{3,4},{5,6},{2,1},{4,3},{6,5},{9,10},{11,12},{13,14},{10,9},... | collective-permute-start | bytes 55304 | tf_op jit(solution)/shard_map/ppermute | solution.py:865
  2.2 1.4 %wall.1 = (f32[2,125,8,128]{3,2,1,0:T(8,128)S(1)}, f32[125,8,128]{2,1,0:T(8,128)S(1)}, f32[1,75,8,128]{3,2,1,0:T(8,128)S(1)}, f32[4,5,8,128]{3,2,1,0:T(8,128)S(1)}, f32[100,8,128]{2,1,0:T(8,128)S(1)}) custom-call(f32[12,4,8,128]{3,2,1,0:T(8,128)S(1)} %pad_maximum_fusion.cells), custom_call_target="tpu_custom_call" | custom-call | flops 20971520 | bytes 1048576 | tf_op jit(solution)/shard_map/wall/pallas_call | solution.py:839
  3.6 2.8 %wrap.1 = (f32[2,125,8,128]{3,2,1,0:T(8,128)S(1)}, f32[125,8,128]{2,1,0:T(8,128)S(1)}, f32[5,75,8,128]{3,2,1,0:T(8,128)S(1)}, f32[2,10,8,128]{3,2,1,0:T(8,128)S(...) custom-call(f32[12,4,8,128]{3,2,1,0:T(8,128)S(1)} %pad_maximum_fusion.cells), custom_call_target="tpu_custom_call" | custom-call | flops 41943040 | bytes 1048576 | tf_op jit(solution)/shard_map/wrap/pallas_call | solution.py:839
  6.5 0.3 %close.1 = (f32[5,8,128]{2,1,0:T(8,128)S(1)}, f32[125,8,128]{2,1,0:T(8,128)S(1)}, f32[100,4,128]{2,1,0:T(4,128)S(1)}) custom-call(f32[9,4,128]{2,1,0:T(4,128)S(1)} %get-tuple-element.35.pair, f32[9,4,128]{2,1,0:T(4,128)S(1)} %get-tuple-element.36.cross, f32[9,4,128]{2,1,0:T(4,128)S(1)} %collective-permute-done.from_pair, ...), custom_call_target="tpu_custom_call" | custom-call | flops 4194304 | bytes 1048576 | tf_op jit(solution)/shard_map/close/pallas_call | solution.py:839
  6.8 3.9 %collective-permute-start.6 = (f32[100,4,128]{2,1,0:T(4,128)S(1)}, f32[100,4,128]{2,1,0:T(4,128)S(1)}, u32[]{:S(2)}, u32[]{:S(2)}) collective-permute-start(f32[100,4,128]{2,1,0:T(4,128)S(1)} %get-tuple-element.54.refs_0_), channel_id=1, source_target_pairs={{0,1},{1,0},{2,3},{3,2},{4,5},{5,4},{6,7},{7,6},{8,9},{9,8},{10,11... | collective-permute-start | bytes 614408 | tf_op jit(solution)/shard_map/ppermute | solution.py:854
  10.7 0.8 %wrap_rhs.1 = (f32[20,8,128]{2,1,0:T(8,128)S(1)}, f32[4,8,128]{2,1,0:T(8,128)S(1)}) custom-call(f32[5,8,128]{2,1,0:T(8,128)S(1)} %get-tuple-element.39.flux, f32[4,5,8,128]{3,2,1,0:T(8,128)S(1)} %get-tuple-element.40.rhs_wall, f32[2,10,8,128]{3,2,1,0:T(8,128)S(1)} %get-tuple-element.41.rhs_wrap, f32[4,8,128]{2,1,0:T(8,128)S(1)} %get-tuple-element.38.after.note, ...), custom_call_target="tpu_custom_call" | custom-call | flops 8388608 | bytes 1048576 | tf_op jit(solution)/shard_map/wrap_rhs/pallas_call | solution.py:839
  11.8 0.4 %merge.1 = (f32[125,4,128]{2,1,0:T(4,128)S(1)}, f32[100,4,128]{2,1,0:T(4,128)S(1)}) custom-call(f32[100,4,128]{2,1,0:T(4,128)S(1)} %get-tuple-element.54.refs_0_, f32[100,4,128]{2,1,0:T(4,128)S(1)} %collective-permute-done.6.refs_1_, f32[4,8,128]{2,1,0:T(8,128)S(1)} %get-tuple-element.45.after.refs_0_.refs_2_), custom_call_target="tpu_custom_call" | custom-call | flops 4194304 | bytes 1048576 | tf_op jit(solution)/shard_map/merge/pallas_call | solution.py:839
  12.2 1.6 %collective-permute-start.10 = (f32[100,4,128]{2,1,0:T(4,128)S(1)}, f32[100,4,128]{2,1,0:T(4,128)S(1)}, u32[]{:S(2)}, u32[]{:S(2)}) collective-permute-start(f32[100,4,128]{2,1,0:T(4,128)S(1)} %get-tuple-element.57.refs_0_), channel_id=1, source_target_pairs={{0,2},{1,3},{2,0},{3,1},{4,6},{5,7},{6,4},{7,5},{8,10},{9,11},{10,... | collective-permute-start | bytes 614408 | tf_op jit(solution)/shard_map/ppermute | solution.py:854
  13.8 3.6 %collective-permute-start.4 = (f32[4,8,128]{2,1,0:T(8,128)S(1)}, f32[4,8,128]{2,1,0:T(8,128)S(1)}, u32[]{:S(2)}, u32[]{:S(2)}) collective-permute-start(f32[4,8,128]{2,1,0:T(8,128)S(1)} %get-tuple-element.45.after.refs_0_.refs_2_), channel_id=1, source_target_pairs={{0,24},{8,16},{16,8},{24,0},{1,25},{9,17},{17,9},{25,1},{2,26},{10... | collective-permute-start | bytes 49160 | tf_op jit(solution)/shard_map/ppermute | solution.py:854
  17.4 0.8 %collective-permute-start.2 = (f32[4,8,128]{2,1,0:T(8,128)S(1)}, f32[4,8,128]{2,1,0:T(8,128)S(1)}, u32[]{:S(2)}, u32[]{:S(2)}) collective-permute-start(f32[4,8,128]{2,1,0:T(8,128)S(1)} %get-tuple-element.45.after.refs_0_.refs_2_), channel_id=1, source_target_pairs={{0,8},{8,0},{16,24},{24,16},{1,9},{9,1},{17,25},{25,17},{2,10},{10... | collective-permute-start | bytes 49160 | tf_op jit(solution)/shard_map/ppermute | solution.py:854
  18.4 0.9 %collective-permute-done.4.refs_3_ = f32[4,8,128]{2,1,0:T(8,128)S(1)} collective-permute-done((f32[4,8,128]{2,1,0:T(8,128)S(1)}, f32[4,8,128]{2,1,0:T(8,128)S(1)}, u32[]{:S(2)}, u32[]{:S(2)}) %collective-permute-start.4) | collective-permute-done | bytes 16416 | tf_op jit(solution)/shard_map/ppermute | solution.py:854
  19.3 2.7 %collective-permute-done.3.refs_2_ = f32[4,8,128]{2,1,0:T(8,128)S(1)} collective-permute-done((f32[4,8,128]{2,1,0:T(8,128)S(1)}, f32[4,8,128]{2,1,0:T(8,128)S(1)}, u32[]{:S(2)}, u32[]{:S(2)}) %collective-permute-start.3) | collective-permute-done | bytes 16416 | tf_op jit(solution)/shard_map/ppermute | solution.py:854
  22.0 1.7 %cycle.1 = (f32[10,4,128]{2,1,0:T(4,128)S(1)}, f32[20,8,128]{2,1,0:T(8,128)S(1)}, f32[5,8,128]{2,1,0:T(8,128)S(1)}) custom-call(f32[4,8,128]{2,1,0:T(8,128)S(1)} %get-tuple-element.45.after.refs_0_.refs_2_, f32[4,8,128]{2,1,0:T(8,128)S(1)} %collective-permute-done.2.refs_1_, f32[4,8,128]{2,1,0:T(8,128)S(1)} %collective-permute-done.3.refs_2_, ...), custom_call_target="tpu_custom_call" | custom-call | flops 10485760 | bytes 1048576 | tf_op jit(solution)/shard_map/cycle/pallas_call | solution.py:839
  23.7 0.5 %merge_1.1 = (f32[125,4,128]{2,1,0:T(4,128)S(1)}, f32[75,4,128]{2,1,0:T(4,128)S(1)}, f32[100,4,128]{2,1,0:T(4,128)S(1)}) custom-call(f32[100,4,128]{2,1,0:T(4,128)S(1)} %get-tuple-element.57.refs_0_, f32[100,4,128]{2,1,0:T(4,128)S(1)} %collective-permute-done.10.refs_1_.refs_5_, f32[10,4,128]{2,1,0:T(4,128)S(1)} %get-tuple-element.53.own.refs_2_), custom_call_target="tpu_custom_call" | custom-call | flops 4194304 | bytes 1048576 | tf_op jit(solution)/shard_map/merge_1/pallas_call | solution.py:839
  24.3 1.0 %collective-permute-start.11 = (f32[75,4,128]{2,1,0:T(4,128)S(1)}, f32[75,4,128]{2,1,0:T(4,128)S(1)}, u32[]{:S(2)}, u32[]{:S(2)}) collective-permute-start(f32[75,4,128]{2,1,0:T(4,128)S(1)} %get-tuple-element.59.own), channel_id=1, source_target_pairs={{0,4},{1,5},{2,6},{3,7},{4,0},{5,1},{6,2},{7,3},{8,12},{9,13},{10,... | collective-permute-start | bytes 460808 | tf_op jit(solution)/shard_map/ppermute | solution.py:854
  25.2 1.2 %collective-permute-done.5.other = f32[10,4,128]{2,1,0:T(4,128)S(1)} collective-permute-done((f32[10,4,128]{2,1,0:T(4,128)S(1)}, f32[10,4,128]{2,1,0:T(4,128)S(1)}, u32[]{:S(2)}, u32[]{:S(2)}) %collective-permute-start.5) | collective-permute-done | bytes 20512 | tf_op jit(solution)/shard_map/ppermute | solution.py:854
  26.5 1.2 %collective-permute-start.9 = (f32[10,4,128]{2,1,0:T(4,128)S(1)}, f32[10,4,128]{2,1,0:T(4,128)S(1)}, u32[]{:S(2)}, u32[]{:S(2)}) collective-permute-start(f32[10,4,128]{2,1,0:T(4,128)S(1)} %get-tuple-element.56.refs_0_), channel_id=1, source_target_pairs={{0,6},{1,7},{2,4},{3,5},{4,2},{5,3},{6,0},{7,1},{8,14},{9,15},{10,... | collective-permute-start | bytes 61448 | tf_op jit(solution)/shard_map/ppermute | solution.py:854
  27.6 1.8 %collective-permute-start.8 = (f32[10,4,128]{2,1,0:T(4,128)S(1)}, f32[10,4,128]{2,1,0:T(4,128)S(1)}, u32[]{:S(2)}, u32[]{:S(2)}) collective-permute-start(f32[10,4,128]{2,1,0:T(4,128)S(1)} %get-tuple-element.56.refs_0_), channel_id=1, source_target_pairs={{0,4},{1,5},{2,6},{3,7},{4,0},{5,1},{6,2},{7,3},{8,12},{9,13},{10,... | collective-permute-start | bytes 61448 | tf_op jit(solution)/shard_map/ppermute | solution.py:854
  29.4 0.6 %collective-permute-start.7 = (f32[10,4,128]{2,1,0:T(4,128)S(1)}, f32[10,4,128]{2,1,0:T(4,128)S(1)}, u32[]{:S(2)}, u32[]{:S(2)}) collective-permute-start(f32[10,4,128]{2,1,0:T(4,128)S(1)} %get-tuple-element.56.refs_0_), channel_id=1, source_target_pairs={{0,2},{1,3},{2,0},{3,1},{4,6},{5,7},{6,4},{7,5},{8,10},{9,11},{10,... | collective-permute-start | bytes 61448 | tf_op jit(solution)/shard_map/ppermute | solution.py:854
  30.1 1.1 %collective-permute-done.9.refs_3_ = f32[10,4,128]{2,1,0:T(4,128)S(1)} collective-permute-done((f32[10,4,128]{2,1,0:T(4,128)S(1)}, f32[10,4,128]{2,1,0:T(4,128)S(1)}, u32[]{:S(2)}, u32[]{:S(2)}) %collective-permute-start.9) | collective-permute-done | bytes 20512 | tf_op jit(solution)/shard_map/ppermute | solution.py:854
  31.4 1.8 %collective-permute-done.7.refs_1_ = f32[10,4,128]{2,1,0:T(4,128)S(1)} collective-permute-done((f32[10,4,128]{2,1,0:T(4,128)S(1)}, f32[10,4,128]{2,1,0:T(4,128)S(1)}, u32[]{:S(2)}, u32[]{:S(2)}) %collective-permute-start.7) | collective-permute-done | bytes 20512 | tf_op jit(solution)/shard_map/ppermute | solution.py:854
  33.2 0.8 %finish.1 = f32[5,4,8,128]{3,2,1,0:T(8,128)} custom-call(f32[10,4,128]{2,1,0:T(4,128)S(1)} %get-tuple-element.56.refs_0_, f32[10,4,128]{2,1,0:T(4,128)S(1)} %collective-permute-done.7.refs_1_, f32[10,4,128]{2,1,0:T(4,128)S(1)} %collective-permute-done.8.refs_2_, f32[10,4,128]{2,1,0:T(4,128)S(1)} %collective-permute-done.9.refs_3_, ...), custom_call_target="tpu_custom_call" | custom-call | flops 4194304 | bytes 1048576 | tf_op jit(solution)/shard_map/finish/pallas_call | solution.py:839
  (13 shorter events, 0.8 us)
Async XLA Ops:
  1.0 5.4 %collective-permute-start = (f32[9,4,128]{2,1,0:T(4,128)S(1)}, f32[9,4,128]{2,1,0:T(4,128)S(1)}, u32[]{:S(2)}, u32[]{:S(2)}) collective-permute-start(f32[9,4,128]{2,1,0:T(4,128)S(1)} %get-tuple-element.35.pair), channel_id=1, source_target_pairs={{0,1},{1,0},{2,3},{3,2},{4,5},{5,4},{6,7},{7,6},{8,9},{9,8},{10,11... | collective-permute-start | bytes 55304 | tf_op jit(solution)/shard_map/ppermute | solution.py:854
  1.5 4.9 %collective-permute-start.1 = (f32[9,4,128]{2,1,0:T(4,128)S(1)}, f32[9,4,128]{2,1,0:T(4,128)S(1)}, u32[]{:S(2)}, u32[]{:S(2)}) collective-permute-start(f32[9,4,128]{2,1,0:T(4,128)S(1)} %get-tuple-element.36.cross), channel_id=1, source_target_pairs={{1,2},{3,4},{5,6},{2,1},{4,3},{6,5},{9,10},{11,12},{13,14},{10,9},... | collective-permute-start | bytes 55304 | tf_op jit(solution)/shard_map/ppermute | solution.py:865
  6.8 5.0 %collective-permute-start.6 = (f32[100,4,128]{2,1,0:T(4,128)S(1)}, f32[100,4,128]{2,1,0:T(4,128)S(1)}, u32[]{:S(2)}, u32[]{:S(2)}) collective-permute-start(f32[100,4,128]{2,1,0:T(4,128)S(1)} %get-tuple-element.54.refs_0_), channel_id=1, source_target_pairs={{0,1},{1,0},{2,3},{3,2},{4,5},{5,4},{6,7},{7,6},{8,9},{9,8},{10,11... | collective-permute-start | bytes 614408 | tf_op jit(solution)/shard_map/ppermute | solution.py:854
  12.2 11.5 %collective-permute-start.10 = (f32[100,4,128]{2,1,0:T(4,128)S(1)}, f32[100,4,128]{2,1,0:T(4,128)S(1)}, u32[]{:S(2)}, u32[]{:S(2)}) collective-permute-start(f32[100,4,128]{2,1,0:T(4,128)S(1)} %get-tuple-element.57.refs_0_), channel_id=1, source_target_pairs={{0,2},{1,3},{2,0},{3,1},{4,6},{5,7},{6,4},{7,5},{8,10},{9,11},{10,... | collective-permute-start | bytes 614408 | tf_op jit(solution)/shard_map/ppermute | solution.py:854
  13.8 5.5 %collective-permute-start.4 = (f32[4,8,128]{2,1,0:T(8,128)S(1)}, f32[4,8,128]{2,1,0:T(8,128)S(1)}, u32[]{:S(2)}, u32[]{:S(2)}) collective-permute-start(f32[4,8,128]{2,1,0:T(8,128)S(1)} %get-tuple-element.45.after.refs_0_.refs_2_), channel_id=1, source_target_pairs={{0,24},{8,16},{16,8},{24,0},{1,25},{9,17},{17,9},{25,1},{2,26},{10... | collective-permute-start | bytes 49160 | tf_op jit(solution)/shard_map/ppermute | solution.py:854
  17.4 4.6 %collective-permute-start.3 = (f32[4,8,128]{2,1,0:T(8,128)S(1)}, f32[4,8,128]{2,1,0:T(8,128)S(1)}, u32[]{:S(2)}, u32[]{:S(2)}) collective-permute-start(f32[4,8,128]{2,1,0:T(8,128)S(1)} %get-tuple-element.45.after.refs_0_.refs_2_), channel_id=1, source_target_pairs={{0,16},{8,24},{16,0},{24,8},{1,17},{9,25},{17,1},{25,9},{2,18},{10... | collective-permute-start | bytes 49160 | tf_op jit(solution)/shard_map/ppermute | solution.py:854
  17.4 4.6 %collective-permute-start.2 = (f32[4,8,128]{2,1,0:T(8,128)S(1)}, f32[4,8,128]{2,1,0:T(8,128)S(1)}, u32[]{:S(2)}, u32[]{:S(2)}) collective-permute-start(f32[4,8,128]{2,1,0:T(8,128)S(1)} %get-tuple-element.45.after.refs_0_.refs_2_), channel_id=1, source_target_pairs={{0,8},{8,0},{16,24},{24,16},{1,9},{9,1},{17,25},{25,17},{2,10},{10... | collective-permute-start | bytes 49160 | tf_op jit(solution)/shard_map/ppermute | solution.py:854
  24.3 5.7 %collective-permute-start.11 = (f32[75,4,128]{2,1,0:T(4,128)S(1)}, f32[75,4,128]{2,1,0:T(4,128)S(1)}, u32[]{:S(2)}, u32[]{:S(2)}) collective-permute-start(f32[75,4,128]{2,1,0:T(4,128)S(1)} %get-tuple-element.59.own), channel_id=1, source_target_pairs={{0,4},{1,5},{2,6},{3,7},{4,0},{5,1},{6,2},{7,3},{8,12},{9,13},{10,... | collective-permute-start | bytes 460808 | tf_op jit(solution)/shard_map/ppermute | solution.py:854
  25.2 1.2 %collective-permute-start.5 = (f32[10,4,128]{2,1,0:T(4,128)S(1)}, f32[10,4,128]{2,1,0:T(4,128)S(1)}, u32[]{:S(2)}, u32[]{:S(2)}) collective-permute-start(f32[10,4,128]{2,1,0:T(4,128)S(1)} %get-tuple-element.53.own.refs_2_), channel_id=1, source_target_pairs={{0,1},{1,0},{2,3},{3,2},{4,5},{5,4},{6,7},{7,6},{8,9},{9,8},{10,11... | collective-permute-start | bytes 61448 | tf_op jit(solution)/shard_map/ppermute | solution.py:854
  26.5 4.7 %collective-permute-start.9 = (f32[10,4,128]{2,1,0:T(4,128)S(1)}, f32[10,4,128]{2,1,0:T(4,128)S(1)}, u32[]{:S(2)}, u32[]{:S(2)}) collective-permute-start(f32[10,4,128]{2,1,0:T(4,128)S(1)} %get-tuple-element.56.refs_0_), channel_id=1, source_target_pairs={{0,6},{1,7},{2,4},{3,5},{4,2},{5,3},{6,0},{7,1},{8,14},{9,15},{10,... | collective-permute-start | bytes 61448 | tf_op jit(solution)/shard_map/ppermute | solution.py:854
  27.6 3.8 %collective-permute-start.8 = (f32[10,4,128]{2,1,0:T(4,128)S(1)}, f32[10,4,128]{2,1,0:T(4,128)S(1)}, u32[]{:S(2)}, u32[]{:S(2)}) collective-permute-start(f32[10,4,128]{2,1,0:T(4,128)S(1)} %get-tuple-element.56.refs_0_), channel_id=1, source_target_pairs={{0,4},{1,5},{2,6},{3,7},{4,0},{5,1},{6,2},{7,3},{8,12},{9,13},{10,... | collective-permute-start | bytes 61448 | tf_op jit(solution)/shard_map/ppermute | solution.py:854
  29.4 3.8 %collective-permute-start.7 = (f32[10,4,128]{2,1,0:T(4,128)S(1)}, f32[10,4,128]{2,1,0:T(4,128)S(1)}, u32[]{:S(2)}, u32[]{:S(2)}) collective-permute-start(f32[10,4,128]{2,1,0:T(4,128)S(1)} %get-tuple-element.56.refs_0_), channel_id=1, source_target_pairs={{0,2},{1,3},{2,0},{3,1},{4,6},{5,7},{6,4},{7,5},{8,10},{9,11},{10,... | collective-permute-start | bytes 61448 | tf_op jit(solution)/shard_map/ppermute | solution.py:854

commit v3 on v2

--- a/solution.py
+++ b/solution.py
@@ -478,10 +478,31 @@
         note[k] = packed[k]
 
 
-def wall_kernel(cells, keep1, keep2, keep3, rhs, ends):
+def put_face(ref, lead, face):
+    for which in range(3):
+        at = 0
+        for i in range(5):
+            for j in range(i, 5):
+                ref[lead + (15 * which + at,)] = face[which][i][j]
+                at += 1
+
+
+def get_face(ref, lead):
+    out = []
+    for which in range(3):
+        m = [[None] * 5 for _ in range(5)]
+        at = 0
+        for i in range(5):
+            for j in range(i, 5):
+                m[i][j] = m[j][i] = ref[lead + (15 * which + at,)]
+                at += 1
+        out.append(m)
+    return out + [None]
+
+
+def wall_faces_kernel(cells, coefs, rhs):
     state, metrics, step, spread = split_cells(cells)
     line = Line(0)
-    states = []
     for t in range(2):
         cells_e, cells_o = load_cells(line, state, metrics, step, spread, t, 2, 1)
         after_e, after_o = line_faces(line, cells_e, cells_o)
@@ -490,11 +511,11 @@
             a, b = line.unpack1(rhs_e[c], rhs_o[c])
             rhs[2 * t, c] = a
             rhs[2 * t + 1, c] = b
-        states.append(first_level(line, after_e, after_o, keep1, t))
-    line_levels(line, states, keep1, keep2, keep3, ends, None)
-
-
-def close_kernel(pair, cross, from_pair, from_cross, ends, after, flux, close, segment):
+        for half, face in enumerate((after_e, after_o)):
+            put_face(coefs, (t, half), face)
+
+
+def edge_faces(pair, cross, from_pair, from_cross):
     odd = odd_device("normal")
     left, right = [], []
     for c in range(9):
@@ -505,12 +526,17 @@
         above = either(odd, from_cross[c], from_pair[c])
         own = either(odd, pair[c], cross[c])
         right.append(jnp.concatenate([own, above], axis=0))
-    damp, lower, upper, through = face_values(left, right)
-    put_vec(flux, 0, through)
-    wall = Line(0)
-    damp_f, low_f, upp_f = (
-        mat_map(lambda x: wall.roll(x, 4), m) for m in (damp, lower, upper)
-    )
+    return face_values(left, right)
+
+
+def wall_kernel(coefs, edge, keep1, keep2, keep3, ends, close, segment):
+    line = Line(0)
+    states = []
+    for t in range(2):
+        after_e, after_o = get_face(coefs, (t, 0)), get_face(coefs, (t, 1))
+        states.append(first_level(line, after_e, after_o, keep1, t))
+    line_levels(line, states, keep1, keep2, keep3, ends, None)
+    damp_f, low_f, upp_f, _ = get_face(edge, ())
     low, mid_l, mid_r, upp = (get_mat(ends, 25 * at) for at in range(4))
     inverse = mat_inv(plus_eye(mat_add(mid_l, damp_f)))
     w_low = mat_mul(inverse, low)
@@ -536,18 +562,15 @@
     return ((lax.axis_index("normal") >> level) & 1) == 1
 
 
-def tree_nodes(level):
-    nodes = []
-    for at in range(level):
-        nodes = [(at, 0)] + nodes + [(i, k + (1 << at)) for i, k in nodes]
-    return nodes
-
-
-def merge_kernel(own, other, after, node, message, *extra, level, shared, last):
-    upside = tree_bit(level)
-    mine, theirs = segment_mats(own), segment_mats(other)
-    lower = [mat_map(lambda a, b: either(upside, b, a), m, t) for m, t in zip(mine, theirs)]
-    upper = [mat_map(lambda a, b: either(upside, a, b), m, t) for m, t in zip(mine, theirs)]
+def merge_kernel(*refs, level, last):
+    node, result = refs[-2:]
+    if level == 0:
+        lower, upper = segment_mats(refs[0].at[0]), segment_mats(refs[0].at[1])
+    else:
+        upside = tree_bit(level)
+        mine, theirs = segment_mats(refs[0]), segment_mats(refs[1])
+        lower = [mat_map(lambda a, b: either(upside, b, a), m, t) for m, t in zip(mine, theirs)]
+        upper = [mat_map(lambda a, b: either(upside, a, b), m, t) for m, t in zip(mine, theirs)]
     inverse = mat_inv(mat_add(lower[3], upper[0]))
     w_low = mat_mul(inverse, lower[2])
     up_in = mat_mul(lower[1], inverse)
@@ -559,43 +582,18 @@
     upp = mat_neg(mat_mul(lower[1], w_upp))
     low = mat_neg(mat_mul(upper[2], w_low))
     mid_l = mat_sub(upper[3], mat_mul(upper[2], w_upp))
-    at = 100
     if last:
         top = tree_bit(level + 1)
         first = mat_inv(mid_r)
-        through = mat_map(lambda x: either(top, 0.0, x), mat_mul(low, first))
+        through = mat_mul(low, first)
         core = mat_map(
             lambda a, b: either(top, a, b), mid_r, mat_sub(mid_l, mat_mul(through, upp))
         )
-        put_mat(extra[0], 0, core)
-        put_mat(extra[0], 25, through)
-        put_mat(extra[0], 50, first)
-        put_mat(extra[0], 75, upp)
-        put_mat(message, 0, core)
-        put_mat(message, 25, through)
-        put_mat(
-            message,
-            50,
-            mat_map(
-                lambda a, b: either(top, a, b), up_in, mat_sub(low_in, mat_mul(through, up_in))
-            ),
-        )
-        at = 75
+        parts = (core, through, first, upp)
     else:
-        for i, m in enumerate((mid_r, upp, low, mid_l)):
-            put_mat(message, 25 * i, m)
-        if shared is not None:
-            put_mat(message, at, up_in)
-            put_mat(message, at + 25, low_in)
-            at += 50
-    for source in (own, other):
-        for c in range(50 * (shared or 0)):
-            message[at] = source[100 + c]
-            at += 1
-
-
-def middle_kernel(own, other, inverse):
-    put_mat(inverse, 0, mat_inv(mat_add(get_mat(own, 0), get_mat(other, 0))))
+        parts = (mid_r, upp, low, mid_l)
+    for at, m in enumerate(parts):
+        put_mat(result, 25 * at, m)
 
 
 def merge_loads(upside, up_in, low_in, mine, theirs):
@@ -619,9 +617,13 @@
     return pick
 
 
-def wrap_rhs_kernel(flux, rhs_wall, rhs_wrap, note, keep1, keep2, keep3, zs, sent):
+def wrap_rhs_kernel(
+    pair, cross, from_pair, from_cross, rhs_wall, rhs_wrap, note, keep1, keep2, keep3, zs, sent, edge
+):
     line, wall = Line(1), Line(0)
-    through = get_vec(flux, 0)
+    face = edge_faces(pair, cross, from_pair, from_cross)
+    through = face[3]
+    put_face(edge, (), [mat_map(lambda x: wall.roll(x, 4), m) for m in face[:3]])
     rhs_e, rhs_o = [], []
     for t in range(2):
         spans = []
@@ -740,82 +742,70 @@
     put_vec(sent, 5, [y[0:4] for y in out_l])
 
 
-def joint_rhs_kernel(own, other, joint, middle, sent):
+def joint_rhs_kernel(own, other, node, *refs, level, last):
     mine = (get_vec(own, 0), get_vec(own, 5))
     theirs = (get_vec(other, 0), get_vec(other, 5))
     load, (right, left) = merge_loads(
-        tree_bit(0), get_mat(joint, 25), get_mat(joint, 50), mine, theirs
-    )
-    put_vec(middle, 0, mat_vec(get_mat(joint, 0), load))
-    put_vec(sent, 0, right)
-    put_vec(sent, 5, left)
-
-
-def finish_kernel(*refs, levels):
-    count = 1 << levels
-    arrived, refs = refs[:count], refs[count:]
-    nodes, others, refs = refs[: levels - 1], refs[levels - 1 : 2 * levels - 1], refs[2 * levels - 1 :]
-    (half, centre, joint, middle, keep1, keep2, tail, close, closed, zs, field) = refs
+        tree_bit(level), get_mat(node, 25), get_mat(node, 50), mine, theirs
+    )
+    if not last:
+        middle, sent = refs
+        put_vec(middle, 0, mat_vec(get_mat(node, 0), load))
+        put_vec(sent, 0, right)
+        put_vec(sent, 5, left)
+        return
+    half, middle, sent = refs
+    put_vec(middle, 0, mat_vec(get_mat(node, 0), load))
+    put_vec(middle, 5, right)
+    top = tree_bit(level + 1)
+    closed = vec_sub(left, mat_vec(get_mat(half, 25), right))
+    for c in range(25):
+        sent[c] = half[c]
+    put_vec(sent, 25, vec_map(lambda a, b: either(top, a, b), right, closed))
+
+
+def mat_solve(matrix, load):
+    a = [list(row) + [x] for row, x in zip(matrix, load)]
+    for k in range(5):
+        over = 1.0 / a[k][k]
+        for j in range(k + 1, 6):
+            a[k][j] = a[k][j] * over
+        for i in range(k + 1, 5):
+            for j in range(k + 1, 6):
+                a[i][j] = a[i][j] - a[i][k] * a[k][j]
+    x = [None] * 5
+    for i in reversed(range(5)):
+        total = a[i][5]
+        for j in range(i + 1, 5):
+            total = total - a[i][j] * x[j]
+        x[i] = total
+    return x
+
+
+def finish_kernel(own, other, half, *refs, levels):
+    nodes, middles = refs[: levels - 1], refs[levels - 1 : 2 * levels - 2]
+    (keep1, keep2, tail, close, closed, zs, field) = refs[2 * levels - 2 :]
     line = Line(0)
-    whole = levels - 1
-    shared = {}
-    for level in range(whole):
-        for at, (i, k) in enumerate(tree_nodes(level)):
-            shared[i, k + (1 << level)] = (others[level], 100 + 50 * at)
-    for at, (i, k) in enumerate(tree_nodes(whole)[1:]):
-        shared[i, k + (1 << whole)] = (others[whole], 75 + 50 * at)
-    loads = {k: (get_vec(ref, 0), get_vec(ref, 5)) for k, ref in enumerate(arrived)}
-    middles = []
-    top = tree_bit(levels)
-    for level in range(whole):
-        upside = tree_bit(level + 1)
-        merged = {}
-        for k in range(0, count, 2 << level):
-            mine, theirs = loads[k], loads[k + (1 << level)]
-            if level == whole - 1 and k:
-                low, upp = (
-                    [vec_map(lambda a, b: either(upside, b, a), m, t) for m, t in zip(mine, theirs)],
-                    [vec_map(lambda a, b: either(upside, a, b), m, t) for m, t in zip(mine, theirs)],
-                )
-                merged[k] = vec_sub(
-                    vec_map(lambda a, b: either(top, a, b), upp[1], low[0]),
-                    vec_add(
-                        mat_vec(get_mat(others[whole], 50), vec_add(low[1], upp[0])),
-                        mat_vec(get_mat(others[whole], 25), low[0]),
-                    ),
-                )
-                continue
-            ref, at = shared[level, k] if k else (nodes[level], 25)
-            load, merged[k] = merge_loads(
-                upside, get_mat(ref, at), get_mat(ref, at + 25), mine, theirs
-            )
-            if k == 0:
-                middles.append(mat_vec(get_mat(nodes[level], 0), load))
-        loads = merged
-    right, left = loads[0]
-    load = vec_add(
-        loads[1 << whole],
-        vec_map(
-            lambda a, b: either(top, a, b),
-            right,
-            vec_sub(left, mat_vec(get_mat(half, 25), right)),
-        ),
-    )
-    between = mat_vec(get_mat(centre, 0), load)
+    between = mat_solve(
+        mat_add(get_mat(own, 0), get_mat(other, 0)),
+        vec_add(get_vec(own, 25), get_vec(other, 25)),
+    )
     below = mat_vec(
-        get_mat(half, 50), vec_sub(right, mat_vec(get_mat(half, 75), between))
-    )
+        get_mat(half, 50),
+        vec_sub(get_vec(middles[-1], 5), mat_vec(get_mat(half, 75), between)),
+    )
+    top = tree_bit(levels - 1)
     below, above = (
         vec_map(lambda a, b: either(top, b, a), below, between),
         vec_map(lambda b: either(top, 0.0, b), between),
     )
-    path = [(tree_bit(i + 1), nodes[i], middles[i]) for i in reversed(range(whole))]
-    path.append((tree_bit(0), joint, get_vec(middle, 0)))
-    for upside, node, z in path:
+    for level in reversed(range(levels - 1)):
+        node = nodes[level]
         between = vec_sub(
-            z,
+            get_vec(middles[level], 0),
             vec_add(mat_vec(get_mat(node, 75), below), mat_vec(get_mat(node, 100), above)),
         )
+        upside = tree_bit(level)
         below, above = (
             vec_map(lambda a, b: either(upside, b, a), below, between),
             vec_map(lambda a, b: either(upside, b, a), between, above),
@@ -855,7 +845,7 @@
 
 
 def on_device(state, metrics, time_step, dissipation, *, wrap_count, wall_count):
-    levels = wall_count.bit_length() - 2
+    levels = wall_count.bit_length() - 1
     row = (4, LANES)
     cells = jnp.concatenate([state, metrics, time_step[None], dissipation], axis=0)
     pair, cross = call(enter_kernel, "enter", [(9,) + row, (9,) + row], 1 << 12, cells)
@@ -863,12 +853,8 @@
     across += [(b, a) for a, b in across]
     from_pair = swapped(pair, "normal", wall_count, 1)
     from_cross = lax.ppermute(cross, "normal", across)
-    wkeep1, wkeep2, wkeep3, rhs_wall, wends = call(
-        wall_kernel,
-        "wall",
-        [(2, 125) + TILE, (125,) + TILE, (1, 75) + TILE, (4, 5) + TILE, (100,) + TILE],
-        20 << 20,
-        cells,
+    coefs, rhs_wall = call(
+        wall_faces_kernel, "wall_faces", [(2, 2, 45) + TILE, (4, 5) + TILE], 8 << 20, cells
     )
     keep1, keep2, keep3, rhs_wrap, note, ends = call(
         wrap_kernel,
@@ -885,25 +871,15 @@
         cells,
         scratch=[(100,) + TILE],
     )
-    flux, close, segment = call(
-        close_kernel,
-        "close",
-        [(5,) + TILE, (125,) + TILE, (100,) + row],
-        4 << 20,
+    zs, own, edge = call(
+        wrap_rhs_kernel,
+        "wrap_rhs",
+        [(20,) + TILE, (4,) + TILE, (45,) + TILE],
+        8 << 20,
         pair,
         cross,
         from_pair,
         from_cross,
-        wends,
-        note,
-    )
-    beside = swapped(segment, "normal", wall_count, 1)
-    zs, own = call(
-        wrap_rhs_kernel,
-        "wrap_rhs",
-        [(20,) + TILE, (4,) + TILE],
-        8 << 20,
-        flux,
         rhs_wall,
         rhs_wrap,
         note,
@@ -912,17 +888,28 @@
         keep3,
     )
     notes = [own] + [swapped(own, "wrap", wrap_count, k) for k in range(1, wrap_count)]
+    wkeep1, wkeep2, wkeep3, wends, close, segment = call(
+        wall_kernel,
+        "wall",
+        [
+            (2, 125) + TILE,
+            (125,) + TILE,
+            (1, 75) + TILE,
+            (100,) + TILE,
+            (125,) + TILE,
+            (100,) + row,
+        ],
+        20 << 20,
+        coefs,
+        edge,
+    )
+    joined = [
+        lax.all_gather(
+            segment, "normal", axis_index_groups=[[i, i + 1] for i in range(0, wall_count, 2)]
+        )
+    ]
     tail, wtail = call(
         tails_kernel, "tails", [(75,) + TILE, (75,) + TILE], 6 << 20, ends, wends, own
-    )
-    joint, message = call(
-        lambda *refs: merge_kernel(*refs, level=0, shared=None, last=False),
-        "merge",
-        [(125,) + row, (100,) + row],
-        4 << 20,
-        segment,
-        beside,
-        own,
     )
     sent, wzs, closed = call(
         lambda *refs: cycle_kernel(*refs, count=wrap_count),
@@ -939,44 +926,46 @@
         wkeep3,
         close,
     )
-    nodes, others = [], []
+    nodes = []
     for level in range(levels - 1):
-        other = swapped(message, "normal", wall_count, 2 << level)
-        final = level == levels - 2
-        shared = len(tree_nodes(level))
-        handed = 75 + 100 * shared if final else 150 + 100 * shared
-        shapes = [(125,) + row, (handed,) + row] + ([(100,) + row] if final else [])
-        node, message, *half = call(
-            lambda *refs: merge_kernel(*refs, level=level + 1, shared=shared, last=final),
-            "merge_%d" % (level + 1),
-            shapes,
+        last = level == levels - 2
+        node, result = call(
+            lambda *refs: merge_kernel(*refs, level=level, last=last),
+            "merge_%d" % level,
+            [(125,) + row, (100,) + row],
             4 << 20,
-            message,
-            other,
+            *joined,
+            *(notes[1:] if level == 0 else []),
+        )
+        nodes.append(node)
+        if not last:
+            joined = [result, swapped(result, "normal", wall_count, 2 << level)]
+    middles = []
+    for level in range(levels - 1):
+        last = level == levels - 2
+        partner = swapped(sent, "normal", wall_count, 1 << level)
+        middle, sent = call(
+            lambda *refs: joint_rhs_kernel(*refs, level=level, last=last),
+            "joint_rhs_%d" % level,
+            [(10 if last else 5,) + row, (30 if last else 10,) + row],
+            1 << 16,
             sent,
-        )
-        nodes.append(node)
-        others.append(other)
-    other = swapped(message, "normal", wall_count, 1 << levels)
-    others.append(other)
-    (centre,) = call(middle_kernel, "middle", [(25,) + row], 1 << 16, message, other)
-    partner = swapped(sent, "normal", wall_count, 1)
-    middle, load = call(
-        joint_rhs_kernel, "joint_rhs", [(5,) + row, (10,) + row], 1 << 16, sent, partner, joint
-    )
-    loads = [load] + [swapped(load, "normal", wall_count, 2 * k) for k in range(1, 1 << levels)]
+            partner,
+            nodes[level],
+            *([result] if last else []),
+        )
+        middles.append(middle)
+    partner = swapped(sent, "normal", wall_count, 1 << (levels - 1))
     (field,) = call(
         lambda *refs: finish_kernel(*refs, levels=levels),
         "finish",
         [(5, 4) + TILE],
         4 << 20,
-        *loads,
+        sent,
+        partner,
+        result,
         *nodes,
-        *others,
-        *half,
-        centre,
-        joint,
-        middle,
+        *middles,
         wkeep1,
         wkeep2,
         wtail,

time: 34.2 us -> 31.7 us (0.927)
  starting transfers between devices: 15.6 us -> 10.3 us
  blocking collectives: 0 us -> 4.02 us
  waiting for transfers between devices: 8.23 us -> 7.09 us
    ppermute x11 -> x8, starting transfers between devices: 14.9 us -> 9.65 us  [swapped(): return lax.ppermute(x, axis, [(i, i ^ by) for i in range(count)])]
    all_gather x0 -> x1, blocking collectives: none -> 4.02 us  [on_device(): lax.all_gather(segment, 'normal', axis_index_groups=[[i, i + 1] for i in...]
    ppermute x11 -> x8, waiting for transfers between devices: 8.22 us -> 7.09 us  [swapped(): return lax.ppermute(x, axis, [(i, i ^ by) for i in range(count)])]
  transfers between devices with their start and end apart: 12 -> 9, of which waited for: 7 -> 4; matrix products, arithmetic and copies ran while one was open for 0% -> 0% of each run, Pallas kernels for 21% -> 22%
where the time goes in v3:
time: 31.7 us; the launch traced here: 31.6 us
  starting transfers between devices  10.3 us (32%)
  Pallas kernels  9.09 us (29%)
  waiting for transfers between devices  7.09 us (22%)
  blocking collectives  4.02 us (13%)
  other arithmetic  0.97 us (3%)
    ppermute x8, starting transfers between devices, swapped(): return lax.ppermute(x, axis, [(i, i ^ by) for i in range(count)])  9.65 us
    pallas_call x12, Pallas kernels, call(): pl.pallas_call(kernel, name=name, out_shape=[jax.ShapeDtypeStruct(s, jnp....  9.09 us
    ppermute x8, waiting for transfers between devices, swapped(): return lax.ppermute(x, axis, [(i, i ^ by) for i in range(count)])  7.09 us
    all_gather x1, blocking collectives, on_device(): lax.all_gather(segment, 'normal', axis_index_groups=[[i, i + 1] for i in...  4.02 us
    concatenate x1, other arithmetic, on_device(): jnp.concatenate([state, metrics, time_step[None], dissipation], axis=0)  0.97 us
    ppermute x1, starting transfers between devices, on_device(): from_cross = lax.ppermute(cross, 'normal', across)  0.65 us
  transfers between devices with their start and end apart: 9, of which 4 were waited for; matrix products, arithmetic and copies ran while one was open for 0% of the time, Pallas kernels for 22%

profile of v3, /device:TPU:0, one launch (start us, length us, event | category | flops | bytes accessed | tf_op | source)
XLA Modules:
  0.0 31.6 jit_solution(1023216233073257761)
XLA Ops:
  0.0 1.0 %pad_maximum_fusion.cells = f32[12,4,8,128]{3,2,1,0:T(8,128)S(1)} fusion(f32[2,4,8,128]{3,2,1,0:T(8,128)} %param.7, f32[1,4,8,128]{3,2,1,0:T(8,128)} %bitcast.3, f32[4,4,8,128]{3,2,1,0:T(8,128)} %param.5, f32[5,4,8,128]{3,2,1,0:T(8,128)} %param.4), kind=kLoop, calls=%fused_computation | loop fusion | flops 147456 | bytes 393216 | tf_op jit(solution)/shard_map/concatenate | solution.py:850
  1.0 0.5 %collective-permute-start = (f32[9,4,128]{2,1,0:T(4,128)S(1)}, f32[9,4,128]{2,1,0:T(4,128)S(1)}, u32[]{:S(2)}, u32[]{:S(2)}) collective-permute-start(f32[9,4,128]{2,1,0:T(4,128)S(1)} %get-tuple-element.37.pair), channel_id=1, source_target_pairs={{0,1},{1,0},{2,3},{3,2},{4,5},{5,4},{6,7},{7,6},{8,9},{9,8},{10,11... | collective-permute-start | bytes 55304 | tf_op jit(solution)/shard_map/ppermute | solution.py:844
  1.5 0.7 %collective-permute-start.1 = (f32[9,4,128]{2,1,0:T(4,128)S(1)}, f32[9,4,128]{2,1,0:T(4,128)S(1)}, u32[]{:S(2)}, u32[]{:S(2)}) collective-permute-start(f32[9,4,128]{2,1,0:T(4,128)S(1)} %get-tuple-element.38.cross), channel_id=1, source_target_pairs={{1,2},{3,4},{5,6},{2,1},{4,3},{6,5},{9,10},{11,12},{13,14},{10,9},... | collective-permute-start | bytes 55304 | tf_op jit(solution)/shard_map/ppermute | solution.py:855
  2.2 0.3 wall_faces.1
  2.5 2.8 %wrap.1 = (f32[2,125,8,128]{3,2,1,0:T(8,128)S(1)}, f32[125,8,128]{2,1,0:T(8,128)S(1)}, f32[5,75,8,128]{3,2,1,0:T(8,128)S(1)}, f32[2,10,8,128]{3,2,1,0:T(8,128)S(...) custom-call(f32[12,4,8,128]{3,2,1,0:T(8,128)S(1)} %pad_maximum_fusion.cells), custom_call_target="tpu_custom_call" | custom-call | flops 41943040 | bytes 1048576 | tf_op jit(solution)/shard_map/wrap/pallas_call | solution.py:829
  5.3 0.0 collective-permute-done.1.from_cross
  5.4 0.9 %wrap_rhs.1 = (f32[20,8,128]{2,1,0:T(8,128)S(1)}, f32[4,8,128]{2,1,0:T(8,128)S(1)}, f32[45,8,128]{2,1,0:T(8,128)S(1)}) custom-call(f32[9,4,128]{2,1,0:T(4,128)S(1)} %get-tuple-element.37.pair, f32[9,4,128]{2,1,0:T(4,128)S(1)} %get-tuple-element.38.cross, f32[9,4,128]{2,1,0:T(4,128)S(1)} %collective-permute-done.from_pair, ...), custom_call_target="tpu_custom_call" | custom-call | flops 8388608 | bytes 1048576 | tf_op jit(solution)/shard_map/wrap_rhs/pallas_call | solution.py:829
  6.3 4.7 %collective-permute-start.4 = (f32[4,8,128]{2,1,0:T(8,128)S(1)}, f32[4,8,128]{2,1,0:T(8,128)S(1)}, u32[]{:S(2)}, u32[]{:S(2)}) collective-permute-start(f32[4,8,128]{2,1,0:T(8,128)S(1)} %get-tuple-element.45.after.refs_0_), channel_id=1, source_target_pairs={{0,24},{8,16},{16,8},{24,0},{1,25},{9,17},{17,9},{25,1},{2,26},{10... | collective-permute-start | bytes 49160 | tf_op jit(solution)/shard_map/ppermute | solution.py:844
  10.9 0.6 %collective-permute-start.2 = (f32[4,8,128]{2,1,0:T(8,128)S(1)}, f32[4,8,128]{2,1,0:T(8,128)S(1)}, u32[]{:S(2)}, u32[]{:S(2)}) collective-permute-start(f32[4,8,128]{2,1,0:T(8,128)S(1)} %get-tuple-element.45.after.refs_0_), channel_id=1, source_target_pairs={{0,8},{8,0},{16,24},{24,16},{1,9},{9,1},{17,25},{25,17},{2,10},{10... | collective-permute-start | bytes 49160 | tf_op jit(solution)/shard_map/ppermute | solution.py:844
  11.6 1.4 %wall.1 = (f32[2,125,8,128]{3,2,1,0:T(8,128)S(1)}, f32[125,8,128]{2,1,0:T(8,128)S(1)}, f32[1,75,8,128]{3,2,1,0:T(8,128)S(1)}, f32[100,8,128]{2,1,0:T(8,128)S(1)}...) custom-call(f32[2,2,45,8,128]{4,3,2,1,0:T(8,128)S(1)} %get-tuple-element.47.coefs, ...), custom_call_target="tpu_custom_call" | custom-call | flops 20971520 | bytes 1048576 | tf_op jit(solution)/shard_map/wall/pallas_call | solution.py:829
  13.0 4.0 %all-gather = f32[200,4,128]{2,1,0:T(4,128)S(1)} all-gather(f32[100,4,128]{2,1,0:T(4,128)S(1)} %get-tuple-element.57), channel_id=2, replica_groups={{0,1},{2,3},{4,5},{6,7},{8,9},{10,11},{12,13},{14,15},{16,17},{18,19},{..., dimensions={0}, use_global_device_ids=true | all-gather | bytes 614400 | tf_op jit(solution)/shard_map/all_gather | solution.py:907
  17.0 0.3 merge_0.1
  17.3 2.0 %collective-permute-start.7 = (f32[100,4,128]{2,1,0:T(4,128)S(1)}, f32[100,4,128]{2,1,0:T(4,128)S(1)}, u32[]{:S(2)}, u32[]{:S(2)}) collective-permute-start(f32[100,4,128]{2,1,0:T(4,128)S(1)} %get-tuple-element.60.refs_0_), channel_id=1, source_target_pairs={{0,2},{1,3},{2,0},{3,1},{4,6},{5,7},{6,4},{7,5},{8,10},{9,11},{10,... | collective-permute-start | bytes 614408 | tf_op jit(solution)/shard_map/ppermute | solution.py:844
  19.3 0.2 tails.1
  19.5 1.7 %cycle.1 = (f32[10,4,128]{2,1,0:T(4,128)S(1)}, f32[20,8,128]{2,1,0:T(8,128)S(1)}, f32[5,8,128]{2,1,0:T(8,128)S(1)}) custom-call(f32[4,8,128]{2,1,0:T(8,128)S(1)} %get-tuple-element.45.after.refs_0_, f32[4,8,128]{2,1,0:T(8,128)S(1)} %collective-permute-done.2.refs_1_, f32[4,8,128]{2,1,0:T(8,128)S(1)} %collective-permute-done.3.refs_2_, ...), custom_call_target="tpu_custom_call" | custom-call | flops 10485760 | bytes 1048576 | tf_op jit(solution)/shard_map/cycle/pallas_call | solution.py:829
  21.3 0.1 collective-permute-start.5
  21.3 1.2 %collective-permute-done.5.refs_1_ = f32[10,4,128]{2,1,0:T(4,128)S(1)} collective-permute-done((f32[10,4,128]{2,1,0:T(4,128)S(1)}, f32[10,4,128]{2,1,0:T(4,128)S(1)}, u32[]{:S(2)}, u32[]{:S(2)}) %collective-permute-start.5) | collective-permute-done | bytes 20512 | tf_op jit(solution)/shard_map/ppermute | solution.py:844
  22.5 0.2 collective-permute-start.6
  22.7 2.0 %collective-permute-done.7.refs_1_ = f32[100,4,128]{2,1,0:T(4,128)S(1)} collective-permute-done((f32[100,4,128]{2,1,0:T(4,128)S(1)}, f32[100,4,128]{2,1,0:T(4,128)S(1)}, u32[]{:S(2)}, u32[]{:S(2)}) %collective-permute-start.7) | collective-permute-done | bytes 204832 | tf_op jit(solution)/shard_map/ppermute | solution.py:844
  24.7 0.5 %merge_1.1 = (f32[125,4,128]{2,1,0:T(4,128)S(1)}, f32[100,4,128]{2,1,0:T(4,128)S(1)}) custom-call(f32[100,4,128]{2,1,0:T(4,128)S(1)} %get-tuple-element.60.refs_0_, f32[100,4,128]{2,1,0:T(4,128)S(1)} %collective-permute-done.7.refs_1_), custom_call_target="tpu_custom_call" | custom-call | flops 4194304 | bytes 1048576 | tf_op jit(solution)/shard_map/merge_1/pallas_call | solution.py:829
  25.2 1.2 %collective-permute-done.6.refs_1_ = f32[10,4,128]{2,1,0:T(4,128)S(1)} collective-permute-done((f32[10,4,128]{2,1,0:T(4,128)S(1)}, f32[10,4,128]{2,1,0:T(4,128)S(1)}, u32[]{:S(2)}, u32[]{:S(2)}) %collective-permute-start.6) | collective-permute-done | bytes 20512 | tf_op jit(solution)/shard_map/ppermute | solution.py:844
  26.4 1.6 %collective-permute-start.8 = (f32[30,4,128]{2,1,0:T(4,128)S(1)}, f32[30,4,128]{2,1,0:T(4,128)S(1)}, u32[]{:S(2)}, u32[]{:S(2)}) collective-permute-start(f32[30,4,128]{2,1,0:T(4,128)S(1)} %get-tuple-element.63.refs_0_), channel_id=1, source_target_pairs={{0,4},{1,5},{2,6},{3,7},{4,0},{5,1},{6,2},{7,3},{8,12},{9,13},{10,... | collective-permute-start | bytes 184328 | tf_op jit(solution)/shard_map/ppermute | solution.py:844
  28.0 2.7 %collective-permute-done.8.refs_1_ = f32[30,4,128]{2,1,0:T(4,128)S(1)} collective-permute-done((f32[30,4,128]{2,1,0:T(4,128)S(1)}, f32[30,4,128]{2,1,0:T(4,128)S(1)}, u32[]{:S(2)}, u32[]{:S(2)}) %collective-permute-start.8) | collective-permute-done | bytes 61472 | tf_op jit(solution)/shard_map/ppermute | solution.py:844
  30.7 0.8 %finish.1 = f32[5,4,8,128]{3,2,1,0:T(8,128)} custom-call(f32[30,4,128]{2,1,0:T(4,128)S(1)} %get-tuple-element.63.refs_0_, f32[30,4,128]{2,1,0:T(4,128)S(1)} %collective-permute-done.8.refs_1_, f32[100,4,128]{2,1,0:T(4,128)S(1)} %get-tuple-element.62.refs_3_.refs_2_, f32[125,4,128]{2,1,0:T(4,128)S(1)} %get-tuple-element.58.refs_2_.refs_3_, ...), custom_call_target="tpu_custom_call" | custom-call | flops 4194304 | bytes 1048576 | tf_op jit(solution)/shard_map/finish/pallas_call | solution.py:829
  (8 shorter events, 0.1 us)
Async XLA Ops:
  1.0 4.3 %collective-permute-start = (f32[9,4,128]{2,1,0:T(4,128)S(1)}, f32[9,4,128]{2,1,0:T(4,128)S(1)}, u32[]{:S(2)}, u32[]{:S(2)}) collective-permute-start(f32[9,4,128]{2,1,0:T(4,128)S(1)} %get-tuple-element.37.pair), channel_id=1, source_target_pairs={{0,1},{1,0},{2,3},{3,2},{4,5},{5,4},{6,7},{7,6},{8,9},{9,8},{10,11... | collective-permute-start | bytes 55304 | tf_op jit(solution)/shard_map/ppermute | solution.py:844
  1.5 3.8 %collective-permute-start.1 = (f32[9,4,128]{2,1,0:T(4,128)S(1)}, f32[9,4,128]{2,1,0:T(4,128)S(1)}, u32[]{:S(2)}, u32[]{:S(2)}) collective-permute-start(f32[9,4,128]{2,1,0:T(4,128)S(1)} %get-tuple-element.38.cross), channel_id=1, source_target_pairs={{1,2},{3,4},{5,6},{2,1},{4,3},{6,5},{9,10},{11,12},{13,14},{10,9},... | collective-permute-start | bytes 55304 | tf_op jit(solution)/shard_map/ppermute | solution.py:855
  6.3 10.7 %collective-permute-start.4 = (f32[4,8,128]{2,1,0:T(8,128)S(1)}, f32[4,8,128]{2,1,0:T(8,128)S(1)}, u32[]{:S(2)}, u32[]{:S(2)}) collective-permute-start(f32[4,8,128]{2,1,0:T(8,128)S(1)} %get-tuple-element.45.after.refs_0_), channel_id=1, source_target_pairs={{0,24},{8,16},{16,8},{24,0},{1,25},{9,17},{17,9},{25,1},{2,26},{10... | collective-permute-start | bytes 49160 | tf_op jit(solution)/shard_map/ppermute | solution.py:844
  10.9 6.0 %collective-permute-start.3 = (f32[4,8,128]{2,1,0:T(8,128)S(1)}, f32[4,8,128]{2,1,0:T(8,128)S(1)}, u32[]{:S(2)}, u32[]{:S(2)}) collective-permute-start(f32[4,8,128]{2,1,0:T(8,128)S(1)} %get-tuple-element.45.after.refs_0_), channel_id=1, source_target_pairs={{0,16},{8,24},{16,0},{24,8},{1,17},{9,25},{17,1},{25,9},{2,18},{10... | collective-permute-start | bytes 49160 | tf_op jit(solution)/shard_map/ppermute | solution.py:844
  10.9 6.0 %collective-permute-start.2 = (f32[4,8,128]{2,1,0:T(8,128)S(1)}, f32[4,8,128]{2,1,0:T(8,128)S(1)}, u32[]{:S(2)}, u32[]{:S(2)}) collective-permute-start(f32[4,8,128]{2,1,0:T(8,128)S(1)} %get-tuple-element.45.after.refs_0_), channel_id=1, source_target_pairs={{0,8},{8,0},{16,24},{24,16},{1,9},{9,1},{17,25},{25,17},{2,10},{10... | collective-permute-start | bytes 49160 | tf_op jit(solution)/shard_map/ppermute | solution.py:844
  17.3 7.4 %collective-permute-start.7 = (f32[100,4,128]{2,1,0:T(4,128)S(1)}, f32[100,4,128]{2,1,0:T(4,128)S(1)}, u32[]{:S(2)}, u32[]{:S(2)}) collective-permute-start(f32[100,4,128]{2,1,0:T(4,128)S(1)} %get-tuple-element.60.refs_0_), channel_id=1, source_target_pairs={{0,2},{1,3},{2,0},{3,1},{4,6},{5,7},{6,4},{7,5},{8,10},{9,11},{10,... | collective-permute-start | bytes 614408 | tf_op jit(solution)/shard_map/ppermute | solution.py:844
  21.3 1.3 %collective-permute-start.5 = (f32[10,4,128]{2,1,0:T(4,128)S(1)}, f32[10,4,128]{2,1,0:T(4,128)S(1)}, u32[]{:S(2)}, u32[]{:S(2)}) collective-permute-start(f32[10,4,128]{2,1,0:T(4,128)S(1)} %get-tuple-element.56.refs_0_), channel_id=1, source_target_pairs={{0,1},{1,0},{2,3},{3,2},{4,5},{5,4},{6,7},{7,6},{8,9},{9,8},{10,11... | collective-permute-start | bytes 61448 | tf_op jit(solution)/shard_map/ppermute | solution.py:844
  22.5 3.8 %collective-permute-start.6 = (f32[10,4,128]{2,1,0:T(4,128)S(1)}, f32[10,4,128]{2,1,0:T(4,128)S(1)}, u32[]{:S(2)}, u32[]{:S(2)}) collective-permute-start(f32[10,4,128]{2,1,0:T(4,128)S(1)} %get-tuple-element.59.refs_0_), channel_id=1, source_target_pairs={{0,2},{1,3},{2,0},{3,1},{4,6},{5,7},{6,4},{7,5},{8,10},{9,11},{10,... | collective-permute-start | bytes 61448 | tf_op jit(solution)/shard_map/ppermute | solution.py:844
  26.4 4.3 %collective-permute-start.8 = (f32[30,4,128]{2,1,0:T(4,128)S(1)}, f32[30,4,128]{2,1,0:T(4,128)S(1)}, u32[]{:S(2)}, u32[]{:S(2)}) collective-permute-start(f32[30,4,128]{2,1,0:T(4,128)S(1)} %get-tuple-element.63.refs_0_), channel_id=1, source_target_pairs={{0,4},{1,5},{2,6},{3,7},{4,0},{5,1},{6,2},{7,3},{8,12},{9,13},{10,... | collective-permute-start | bytes 184328 | tf_op jit(solution)/shard_map/ppermute | solution.py:844

commit v4 on v3

--- a/solution.py
+++ b/solution.py
@@ -391,13 +391,12 @@
     return out
 
 
-def tails_kernel(ends_wrap, ends_wall, after, tail_wrap, tail_wall):
-    for ends, tail in ((ends_wrap, tail_wrap), (ends_wall, tail_wall)):
-        low, mid_l, mid_r, upp = (get_mat(ends, 25 * at) for at in range(4))
-        inverse = mat_inv(mat_add(mid_l, mid_r))
-        put_mat(tail, 0, inverse)
-        put_mat(tail, 25, mat_mul(inverse, low))
-        put_mat(tail, 50, mat_mul(inverse, upp))
+def tail_kernel(ends, after, tail):
+    low, mid_l, mid_r, upp = (get_mat(ends, 25 * at) for at in range(4))
+    inverse = mat_inv(mat_add(mid_l, mid_r))
+    put_mat(tail, 0, inverse)
+    put_mat(tail, 25, mat_mul(inverse, low))
+    put_mat(tail, 50, mat_mul(inverse, upp))
 
 
 def odd_device(axis):
@@ -887,7 +886,9 @@
         keep2,
         keep3,
     )
-    notes = [own] + [swapped(own, "wrap", wrap_count, k) for k in range(1, wrap_count)]
+    notes = [own] + [None] * (wrap_count - 1)
+    for k in [1, 3, 2] + list(range(4, wrap_count)):
+        notes[k] = swapped(own, "wrap", wrap_count, k)
     wkeep1, wkeep2, wkeep3, wends, close, segment = call(
         wall_kernel,
         "wall",
@@ -908,9 +909,7 @@
             segment, "normal", axis_index_groups=[[i, i + 1] for i in range(0, wall_count, 2)]
         )
     ]
-    tail, wtail = call(
-        tails_kernel, "tails", [(75,) + TILE, (75,) + TILE], 6 << 20, ends, wends, own
-    )
+    (tail,) = call(tail_kernel, "tail", [(75,) + TILE], 3 << 20, ends, own)
     sent, wzs, closed = call(
         lambda *refs: cycle_kernel(*refs, count=wrap_count),
         "cycle",
@@ -955,6 +954,7 @@
             *([result] if last else []),
         )
         middles.append(middle)
+    (wtail,) = call(tail_kernel, "wall_tail", [(75,) + TILE], 3 << 20, wends, sent)
     partner = swapped(sent, "normal", wall_count, 1 << (levels - 1))
     (field,) = call(
         lambda *refs: finish_kernel(*refs, levels=levels),

time: 31.7 us -> 31.7 us (level)
    pallas_call x12 -> x13, Pallas kernels: 9.09 us -> 9.14 us  [call(): pl.pallas_call(kernel, name=name, out_shape=[jax.ShapeDtypeStruct(s, jnp....]
where the time goes in v4:
time: 31.7 us; the launch traced here: 31.5 us
  starting transfers between devices  10.3 us (32%)
  Pallas kernels  9.14 us (29%)
  waiting for transfers between devices  6.94 us (22%)
  blocking collectives  4.02 us (13%)
  other arithmetic  0.97 us (3%)
    ppermute x8, starting transfers between devices, swapped(): return lax.ppermute(x, axis, [(i, i ^ by) for i in range(count)])  9.65 us
    pallas_call x13, Pallas kernels, call(): pl.pallas_call(kernel, name=name, out_shape=[jax.ShapeDtypeStruct(s, jnp....  9.14 us
    ppermute x8, waiting for transfers between devices, swapped(): return lax.ppermute(x, axis, [(i, i ^ by) for i in range(count)])  6.94 us
    all_gather x1, blocking collectives, on_device(): lax.all_gather(segment, 'normal', axis_index_groups=[[i, i + 1] for i in...  4.02 us
    concatenate x1, other arithmetic, on_device(): jnp.concatenate([state, metrics, time_step[None], dissipation], axis=0)  0.97 us
    ppermute x1, starting transfers between devices, on_device(): from_cross = lax.ppermute(cross, 'normal', across)  0.65 us
  transfers between devices with their start and end apart: 9, of which 4 were waited for; matrix products, arithmetic and copies ran while one was open for 0% of the time, Pallas kernels for 22%

profile of v4, /device:TPU:0, one launch (start us, length us, event | category | flops | bytes accessed | tf_op | source)
XLA Modules:
  0.0 31.5 jit_solution(3787468377141863256)
XLA Ops:
  0.0 1.0 %pad_maximum_fusion.cells = f32[12,4,8,128]{3,2,1,0:T(8,128)S(1)} fusion(f32[2,4,8,128]{3,2,1,0:T(8,128)} %param.7, f32[1,4,8,128]{3,2,1,0:T(8,128)} %bitcast.3, f32[4,4,8,128]{3,2,1,0:T(8,128)} %param.5, f32[5,4,8,128]{3,2,1,0:T(8,128)} %param.4), kind=kLoop, calls=%fused_computation | loop fusion | flops 147456 | bytes 393216 | tf_op jit(solution)/shard_map/concatenate | solution.py:849
  1.0 0.5 %collective-permute-start = (f32[9,4,128]{2,1,0:T(4,128)S(1)}, f32[9,4,128]{2,1,0:T(4,128)S(1)}, u32[]{:S(2)}, u32[]{:S(2)}) collective-permute-start(f32[9,4,128]{2,1,0:T(4,128)S(1)} %get-tuple-element.35.pair), channel_id=1, source_target_pairs={{0,1},{1,0},{2,3},{3,2},{4,5},{5,4},{6,7},{7,6},{8,9},{9,8},{10,11... | collective-permute-start | bytes 55304 | tf_op jit(solution)/shard_map/ppermute | solution.py:843
  1.5 0.7 %collective-permute-start.1 = (f32[9,4,128]{2,1,0:T(4,128)S(1)}, f32[9,4,128]{2,1,0:T(4,128)S(1)}, u32[]{:S(2)}, u32[]{:S(2)}) collective-permute-start(f32[9,4,128]{2,1,0:T(4,128)S(1)} %get-tuple-element.36.cross), channel_id=1, source_target_pairs={{1,2},{3,4},{5,6},{2,1},{4,3},{6,5},{9,10},{11,12},{13,14},{10,9},... | collective-permute-start | bytes 55304 | tf_op jit(solution)/shard_map/ppermute | solution.py:854
  2.2 0.3 wall_faces.1
  2.5 2.8 %wrap.1 = (f32[2,125,8,128]{3,2,1,0:T(8,128)S(1)}, f32[125,8,128]{2,1,0:T(8,128)S(1)}, f32[5,75,8,128]{3,2,1,0:T(8,128)S(1)}, f32[2,10,8,128]{3,2,1,0:T(8,128)S(...) custom-call(f32[12,4,8,128]{3,2,1,0:T(8,128)S(1)} %pad_maximum_fusion.cells), custom_call_target="tpu_custom_call" | custom-call | flops 41943040 | bytes 1048576 | tf_op jit(solution)/shard_map/wrap/pallas_call | solution.py:828
  5.4 0.9 %wrap_rhs.1 = (f32[20,8,128]{2,1,0:T(8,128)S(1)}, f32[4,8,128]{2,1,0:T(8,128)S(1)}, f32[45,8,128]{2,1,0:T(8,128)S(1)}) custom-call(f32[9,4,128]{2,1,0:T(4,128)S(1)} %get-tuple-element.35.pair, f32[9,4,128]{2,1,0:T(4,128)S(1)} %get-tuple-element.36.cross, f32[9,4,128]{2,1,0:T(4,128)S(1)} %collective-permute-done.from_pair, ...), custom_call_target="tpu_custom_call" | custom-call | flops 8388608 | bytes 1048576 | tf_op jit(solution)/shard_map/wrap_rhs/pallas_call | solution.py:828
  6.3 4.7 %collective-permute-start.4 = (f32[4,8,128]{2,1,0:T(8,128)S(1)}, f32[4,8,128]{2,1,0:T(8,128)S(1)}, u32[]{:S(2)}, u32[]{:S(2)}) collective-permute-start(f32[4,8,128]{2,1,0:T(8,128)S(1)} %get-tuple-element.43.after.refs_0_), channel_id=1, source_target_pairs={{0,24},{8,16},{16,8},{24,0},{1,25},{9,17},{17,9},{25,1},{2,26},{10... | collective-permute-start | bytes 49160 | tf_op jit(solution)/shard_map/ppermute | solution.py:843
  10.9 0.6 %collective-permute-start.2 = (f32[4,8,128]{2,1,0:T(8,128)S(1)}, f32[4,8,128]{2,1,0:T(8,128)S(1)}, u32[]{:S(2)}, u32[]{:S(2)}) collective-permute-start(f32[4,8,128]{2,1,0:T(8,128)S(1)} %get-tuple-element.43.after.refs_0_), channel_id=1, source_target_pairs={{0,8},{8,0},{16,24},{24,16},{1,9},{9,1},{17,25},{25,17},{2,10},{10... | collective-permute-start | bytes 49160 | tf_op jit(solution)/shard_map/ppermute | solution.py:843
  11.6 1.4 %wall.1 = (f32[2,125,8,128]{3,2,1,0:T(8,128)S(1)}, f32[125,8,128]{2,1,0:T(8,128)S(1)}, f32[1,75,8,128]{3,2,1,0:T(8,128)S(1)}, f32[100,8,128]{2,1,0:T(8,128)S(1)}...) custom-call(f32[2,2,45,8,128]{4,3,2,1,0:T(8,128)S(1)} %get-tuple-element.46.coefs, ...), custom_call_target="tpu_custom_call" | custom-call | flops 20971520 | bytes 1048576 | tf_op jit(solution)/shard_map/wall/pallas_call | solution.py:828
  13.0 4.0 %all-gather = f32[200,4,128]{2,1,0:T(4,128)S(1)} all-gather(f32[100,4,128]{2,1,0:T(4,128)S(1)} %get-tuple-element.53), channel_id=2, replica_groups={{0,1},{2,3},{4,5},{6,7},{8,9},{10,11},{12,13},{14,15},{16,17},{18,19},{..., dimensions={0}, use_global_device_ids=true | all-gather | bytes 614400 | tf_op jit(solution)/shard_map/all_gather | solution.py:908
  17.0 0.3 merge_0.1
  17.3 2.0 %collective-permute-start.7 = (f32[100,4,128]{2,1,0:T(4,128)S(1)}, f32[100,4,128]{2,1,0:T(4,128)S(1)}, u32[]{:S(2)}, u32[]{:S(2)}) collective-permute-start(f32[100,4,128]{2,1,0:T(4,128)S(1)} %get-tuple-element.56.refs_0_), channel_id=1, source_target_pairs={{0,2},{1,3},{2,0},{3,1},{4,6},{5,7},{6,4},{7,5},{8,10},{9,11},{10,... | collective-permute-start | bytes 614408 | tf_op jit(solution)/shard_map/ppermute | solution.py:843
  19.3 0.1 tail.1.refs_6_
  19.4 1.7 %cycle.1 = (f32[10,4,128]{2,1,0:T(4,128)S(1)}, f32[20,8,128]{2,1,0:T(8,128)S(1)}, f32[5,8,128]{2,1,0:T(8,128)S(1)}) custom-call(f32[4,8,128]{2,1,0:T(8,128)S(1)} %get-tuple-element.43.after.refs_0_, f32[4,8,128]{2,1,0:T(8,128)S(1)} %collective-permute-done.2.refs_1_, f32[4,8,128]{2,1,0:T(8,128)S(1)} %collective-permute-done.3.refs_2_, ...), custom_call_target="tpu_custom_call" | custom-call | flops 10485760 | bytes 1048576 | tf_op jit(solution)/shard_map/cycle/pallas_call | solution.py:828
  21.2 0.1 collective-permute-start.5
  21.2 1.2 %collective-permute-done.5.refs_1_ = f32[10,4,128]{2,1,0:T(4,128)S(1)} collective-permute-done((f32[10,4,128]{2,1,0:T(4,128)S(1)}, f32[10,4,128]{2,1,0:T(4,128)S(1)}, u32[]{:S(2)}, u32[]{:S(2)}) %collective-permute-start.5) | collective-permute-done | bytes 20512 | tf_op jit(solution)/shard_map/ppermute | solution.py:843
  22.5 0.2 collective-permute-start.6
  22.6 2.1 %collective-permute-done.7.refs_1_ = f32[100,4,128]{2,1,0:T(4,128)S(1)} collective-permute-done((f32[100,4,128]{2,1,0:T(4,128)S(1)}, f32[100,4,128]{2,1,0:T(4,128)S(1)}, u32[]{:S(2)}, u32[]{:S(2)}) %collective-permute-start.7) | collective-permute-done | bytes 204832 | tf_op jit(solution)/shard_map/ppermute | solution.py:843
  24.8 0.5 %merge_1.1 = (f32[125,4,128]{2,1,0:T(4,128)S(1)}, f32[100,4,128]{2,1,0:T(4,128)S(1)}) custom-call(f32[100,4,128]{2,1,0:T(4,128)S(1)} %get-tuple-element.56.refs_0_, f32[100,4,128]{2,1,0:T(4,128)S(1)} %collective-permute-done.7.refs_1_), custom_call_target="tpu_custom_call" | custom-call | flops 4194304 | bytes 1048576 | tf_op jit(solution)/shard_map/merge_1/pallas_call | solution.py:828
  25.3 1.1 %collective-permute-done.6.refs_1_ = f32[10,4,128]{2,1,0:T(4,128)S(1)} collective-permute-done((f32[10,4,128]{2,1,0:T(4,128)S(1)}, f32[10,4,128]{2,1,0:T(4,128)S(1)}, u32[]{:S(2)}, u32[]{:S(2)}) %collective-permute-start.6) | collective-permute-done | bytes 20512 | tf_op jit(solution)/shard_map/ppermute | solution.py:843
  26.4 1.6 %collective-permute-start.8 = (f32[30,4,128]{2,1,0:T(4,128)S(1)}, f32[30,4,128]{2,1,0:T(4,128)S(1)}, u32[]{:S(2)}, u32[]{:S(2)}) collective-permute-start(f32[30,4,128]{2,1,0:T(4,128)S(1)} %get-tuple-element.59.after.refs_0_), channel_id=1, source_target_pairs={{0,4},{1,5},{2,6},{3,7},{4,0},{5,1},{6,2},{7,3},{8,12},{9,13},{10,... | collective-permute-start | bytes 184328 | tf_op jit(solution)/shard_map/ppermute | solution.py:843
  27.9 0.1 wall_tail.1.refs_9_
  28.1 2.6 %collective-permute-done.8.refs_1_ = f32[30,4,128]{2,1,0:T(4,128)S(1)} collective-permute-done((f32[30,4,128]{2,1,0:T(4,128)S(1)}, f32[30,4,128]{2,1,0:T(4,128)S(1)}, u32[]{:S(2)}, u32[]{:S(2)}) %collective-permute-start.8) | collective-permute-done | bytes 61472 | tf_op jit(solution)/shard_map/ppermute | solution.py:843
  30.6 0.8 %finish.1 = f32[5,4,8,128]{3,2,1,0:T(8,128)} custom-call(f32[30,4,128]{2,1,0:T(4,128)S(1)} %get-tuple-element.59.after.refs_0_, f32[30,4,128]{2,1,0:T(4,128)S(1)} %collective-permute-done.8.refs_1_, f32[100,4,128]{2,1,0:T(4,128)S(1)} %get-tuple-element.58.refs_3_.refs_2_, f32[125,4,128]{2,1,0:T(4,128)S(1)} %get-tuple-element.54.refs_2_.refs_3_, ...), custom_call_target="tpu_custom_call" | custom-call | flops 4194304 | bytes 1048576 | tf_op jit(solution)/shard_map/finish/pallas_call | solution.py:828
  (9 shorter events, 0.1 us)
Async XLA Ops:
  1.0 4.3 %collective-permute-start = (f32[9,4,128]{2,1,0:T(4,128)S(1)}, f32[9,4,128]{2,1,0:T(4,128)S(1)}, u32[]{:S(2)}, u32[]{:S(2)}) collective-permute-start(f32[9,4,128]{2,1,0:T(4,128)S(1)} %get-tuple-element.35.pair), channel_id=1, source_target_pairs={{0,1},{1,0},{2,3},{3,2},{4,5},{5,4},{6,7},{7,6},{8,9},{9,8},{10,11... | collective-permute-start | bytes 55304 | tf_op jit(solution)/shard_map/ppermute | solution.py:843
  1.5 3.8 %collective-permute-start.1 = (f32[9,4,128]{2,1,0:T(4,128)S(1)}, f32[9,4,128]{2,1,0:T(4,128)S(1)}, u32[]{:S(2)}, u32[]{:S(2)}) collective-permute-start(f32[9,4,128]{2,1,0:T(4,128)S(1)} %get-tuple-element.36.cross), channel_id=1, source_target_pairs={{1,2},{3,4},{5,6},{2,1},{4,3},{6,5},{9,10},{11,12},{13,14},{10,9},... | collective-permute-start | bytes 55304 | tf_op jit(solution)/shard_map/ppermute | solution.py:854
  6.3 10.7 %collective-permute-start.4 = (f32[4,8,128]{2,1,0:T(8,128)S(1)}, f32[4,8,128]{2,1,0:T(8,128)S(1)}, u32[]{:S(2)}, u32[]{:S(2)}) collective-permute-start(f32[4,8,128]{2,1,0:T(8,128)S(1)} %get-tuple-element.43.after.refs_0_), channel_id=1, source_target_pairs={{0,24},{8,16},{16,8},{24,0},{1,25},{9,17},{17,9},{25,1},{2,26},{10... | collective-permute-start | bytes 49160 | tf_op jit(solution)/shard_map/ppermute | solution.py:843
  10.9 6.1 %collective-permute-start.3 = (f32[4,8,128]{2,1,0:T(8,128)S(1)}, f32[4,8,128]{2,1,0:T(8,128)S(1)}, u32[]{:S(2)}, u32[]{:S(2)}) collective-permute-start(f32[4,8,128]{2,1,0:T(8,128)S(1)} %get-tuple-element.43.after.refs_0_), channel_id=1, source_target_pairs={{0,16},{8,24},{16,0},{24,8},{1,17},{9,25},{17,1},{25,9},{2,18},{10... | collective-permute-start | bytes 49160 | tf_op jit(solution)/shard_map/ppermute | solution.py:843
  10.9 6.1 %collective-permute-start.2 = (f32[4,8,128]{2,1,0:T(8,128)S(1)}, f32[4,8,128]{2,1,0:T(8,128)S(1)}, u32[]{:S(2)}, u32[]{:S(2)}) collective-permute-start(f32[4,8,128]{2,1,0:T(8,128)S(1)} %get-tuple-element.43.after.refs_0_), channel_id=1, source_target_pairs={{0,8},{8,0},{16,24},{24,16},{1,9},{9,1},{17,25},{25,17},{2,10},{10... | collective-permute-start | bytes 49160 | tf_op jit(solution)/shard_map/ppermute | solution.py:843
  17.3 7.4 %collective-permute-start.7 = (f32[100,4,128]{2,1,0:T(4,128)S(1)}, f32[100,4,128]{2,1,0:T(4,128)S(1)}, u32[]{:S(2)}, u32[]{:S(2)}) collective-permute-start(f32[100,4,128]{2,1,0:T(4,128)S(1)} %get-tuple-element.56.refs_0_), channel_id=1, source_target_pairs={{0,2},{1,3},{2,0},{3,1},{4,6},{5,7},{6,4},{7,5},{8,10},{9,11},{10,... | collective-permute-start | bytes 614408 | tf_op jit(solution)/shard_map/ppermute | solution.py:843
  21.2 1.3 %collective-permute-start.5 = (f32[10,4,128]{2,1,0:T(4,128)S(1)}, f32[10,4,128]{2,1,0:T(4,128)S(1)}, u32[]{:S(2)}, u32[]{:S(2)}) collective-permute-start(f32[10,4,128]{2,1,0:T(4,128)S(1)} %get-tuple-element.52.refs_0_), channel_id=1, source_target_pairs={{0,1},{1,0},{2,3},{3,2},{4,5},{5,4},{6,7},{7,6},{8,9},{9,8},{10,11... | collective-permute-start | bytes 61448 | tf_op jit(solution)/shard_map/ppermute | solution.py:843
  22.5 3.8 %collective-permute-start.6 = (f32[10,4,128]{2,1,0:T(4,128)S(1)}, f32[10,4,128]{2,1,0:T(4,128)S(1)}, u32[]{:S(2)}, u32[]{:S(2)}) collective-permute-start(f32[10,4,128]{2,1,0:T(4,128)S(1)} %get-tuple-element.55.refs_0_), channel_id=1, source_target_pairs={{0,2},{1,3},{2,0},{3,1},{4,6},{5,7},{6,4},{7,5},{8,10},{9,11},{10,... | collective-permute-start | bytes 61448 | tf_op jit(solution)/shard_map/ppermute | solution.py:843
  26.4 4.3 %collective-permute-start.8 = (f32[30,4,128]{2,1,0:T(4,128)S(1)}, f32[30,4,128]{2,1,0:T(4,128)S(1)}, u32[]{:S(2)}, u32[]{:S(2)}) collective-permute-start(f32[30,4,128]{2,1,0:T(4,128)S(1)} %get-tuple-element.59.after.refs_0_), channel_id=1, source_target_pairs={{0,4},{1,5},{2,6},{3,7},{4,0},{5,1},{6,2},{7,3},{8,12},{9,13},{10,... | collective-permute-start | bytes 184328 | tf_op jit(solution)/shard_map/ppermute | solution.py:843

commit v5 on v4

--- a/solution.py
+++ b/solution.py
@@ -372,7 +372,6 @@
         ),
     )
     pairs = [line.unpack2(x, y) for x, y in zip(even, odd)]
-    out = []
     for t in range(2):
         even = [p[t] for p in pairs]
         ends = line.vroll(last, 2) if t == 0 else last
@@ -386,9 +385,7 @@
         )
         odd = vec_map(lambda x, y: jnp.where(line.inner, x, y), odd, ends)
         spans = [line.unpack1(x, y) for x, y in zip(even, odd)]
-        out.append([s[0] for s in spans])
-        out.append([s[1] for s in spans])
-    return out
+        yield [s[0] for s in spans], [s[1] for s in spans]
 
 
 def tail_kernel(ends, after, tail):
@@ -724,7 +721,7 @@
     spread = line.at & 3
     first = [jnp.take_along_axis(y, spread, axis=1) for y in x]
     last = [jnp.take_along_axis(y, spread, axis=1) for y in b]
-    swept = line_backward(line, first, last, keep1, keep2, tail, zs)
+    swept = [x for pair in line_backward(line, first, last, keep1, keep2, tail, zs) for x in pair]
 
     wall = Line(0)
     rhs_e, rhs_o = [], []
@@ -783,7 +780,7 @@
 
 def finish_kernel(own, other, half, *refs, levels):
     nodes, middles = refs[: levels - 1], refs[levels - 1 : 2 * levels - 2]
-    (keep1, keep2, tail, close, closed, zs, field) = refs[2 * levels - 2 :]
+    (keep1, keep2, tail, close, closed, zs, field, held, sems) = refs[2 * levels - 2 :]
     line = Line(0)
     between = mat_solve(
         mat_add(get_mat(own, 0), get_mat(other, 0)),
@@ -817,20 +814,26 @@
         vec_add(mat_vec(get_mat(close, 75), first), mat_vec(get_mat(close, 100), nexts)),
     )
     last = [jnp.where(line.at < 4, x, line.roll(x, 4)) for x in last]
-    out = line_backward(line, first, last, keep1, keep2, tail, zs)
-    for s in range(4):
-        for c in range(5):
-            field[c, s] = out[s][c]
-
-
-def call(kernel, name, shapes, flops, *args, scratch=()):
-    place = pl.BlockSpec(memory_space=pltpu.VMEM)
+    copies = []
+    for t, pair in enumerate(line_backward(line, first, last, keep1, keep2, tail, zs)):
+        for s in range(2):
+            for c in range(5):
+                held[t, c, s] = pair[s][c]
+        copies.append(
+            pltpu.make_async_copy(held.at[t], field.at[:, 2 * t : 2 * t + 2], sems.at[t])
+        )
+        copies[-1].start()
+    for copy in copies:
+        copy.wait()
+
+
+def call(kernel, name, shapes, flops, *args, scratch=(), output=pltpu.VMEM):
     return pl.pallas_call(
         kernel,
         name=name,
         out_shape=[jax.ShapeDtypeStruct(s, jnp.float32) for s in shapes],
         in_specs=[pl.BlockSpec(memory_space=pltpu.VMEM)] * len(args),
-        out_specs=[place] * len(shapes),
+        out_specs=[pl.BlockSpec(memory_space=output)] * len(shapes),
         scratch_shapes=[
             pltpu.VMEM(s, jnp.float32) if isinstance(s, tuple) else s for s in scratch
         ],
@@ -972,6 +975,8 @@
         close,
         closed,
         wzs,
+        scratch=[(2, 5, 2) + TILE, pltpu.SemaphoreType.DMA((2,))],
+        output=pltpu.HBM,
     )
     return field
 

time: 31.7 us -> 31.6 us (level)
  no operation moved by 1% of the time
where the time goes in v5:
time: 31.6 us; the launch traced here: 31.5 us
  starting transfers between devices  10.3 us (33%)
  Pallas kernels  9.14 us (29%)
  waiting for transfers between devices  6.94 us (22%)
  blocking collectives  4.02 us (13%)
  other arithmetic  0.97 us (3%)
    ppermute x8, starting transfers between devices, swapped(): return lax.ppermute(x, axis, [(i, i ^ by) for i in range(count)])  9.65 us
    pallas_call x13, Pallas kernels, call(): pl.pallas_call(kernel, name=name, out_shape=[jax.ShapeDtypeStruct(s, jnp....  9.14 us
    ppermute x8, waiting for transfers between devices, swapped(): return lax.ppermute(x, axis, [(i, i ^ by) for i in range(count)])  6.94 us
    all_gather x1, blocking collectives, on_device(): lax.all_gather(segment, 'normal', axis_index_groups=[[i, i + 1] for i in...  4.02 us
    concatenate x1, other arithmetic, on_device(): jnp.concatenate([state, metrics, time_step[None], dissipation], axis=0)  0.97 us
    ppermute x1, starting transfers between devices, on_device(): from_cross = lax.ppermute(cross, 'normal', across)  0.65 us
  transfers between devices with their start and end apart: 9, of which 4 were waited for; matrix products, arithmetic and copies ran while one was open for 0% of the time, Pallas kernels for 22%

profile of v5, /device:TPU:0, one launch (start us, length us, event | category | flops | bytes accessed | tf_op | source)
XLA Modules:
  0.0 31.5 jit_solution(4764512841191336150)
XLA Ops:
  0.0 1.0 %pad_maximum_fusion.cells = f32[12,4,8,128]{3,2,1,0:T(8,128)S(1)} fusion(f32[2,4,8,128]{3,2,1,0:T(8,128)} %param.7, f32[1,4,8,128]{3,2,1,0:T(8,128)} %bitcast.3, f32[4,4,8,128]{3,2,1,0:T(8,128)} %param.5, f32[5,4,8,128]{3,2,1,0:T(8,128)} %param.4), kind=kLoop, calls=%fused_computation | loop fusion | flops 147456 | bytes 393216 | tf_op jit(solution)/shard_map/concatenate | solution.py:852
  1.0 0.5 %collective-permute-start = (f32[9,4,128]{2,1,0:T(4,128)S(1)}, f32[9,4,128]{2,1,0:T(4,128)S(1)}, u32[]{:S(2)}, u32[]{:S(2)}) collective-permute-start(f32[9,4,128]{2,1,0:T(4,128)S(1)} %get-tuple-element.35.pair), channel_id=1, source_target_pairs={{0,1},{1,0},{2,3},{3,2},{4,5},{5,4},{6,7},{7,6},{8,9},{9,8},{10,11... | collective-permute-start | bytes 55304 | tf_op jit(solution)/shard_map/ppermute | solution.py:846
  1.5 0.7 %collective-permute-start.1 = (f32[9,4,128]{2,1,0:T(4,128)S(1)}, f32[9,4,128]{2,1,0:T(4,128)S(1)}, u32[]{:S(2)}, u32[]{:S(2)}) collective-permute-start(f32[9,4,128]{2,1,0:T(4,128)S(1)} %get-tuple-element.36.cross), channel_id=1, source_target_pairs={{1,2},{3,4},{5,6},{2,1},{4,3},{6,5},{9,10},{11,12},{13,14},{10,9},... | collective-permute-start | bytes 55304 | tf_op jit(solution)/shard_map/ppermute | solution.py:857
  2.2 0.3 wall_faces.1
  2.5 2.8 %wrap.1 = (f32[2,125,8,128]{3,2,1,0:T(8,128)S(1)}, f32[125,8,128]{2,1,0:T(8,128)S(1)}, f32[5,75,8,128]{3,2,1,0:T(8,128)S(1)}, f32[2,10,8,128]{3,2,1,0:T(8,128)S(...) custom-call(f32[12,4,8,128]{3,2,1,0:T(8,128)S(1)} %pad_maximum_fusion.cells), custom_call_target="tpu_custom_call" | custom-call | flops 41943040 | bytes 1048576 | tf_op jit(solution)/shard_map/wrap/pallas_call | solution.py:831
  5.4 0.9 %wrap_rhs.1 = (f32[20,8,128]{2,1,0:T(8,128)S(1)}, f32[4,8,128]{2,1,0:T(8,128)S(1)}, f32[45,8,128]{2,1,0:T(8,128)S(1)}) custom-call(f32[9,4,128]{2,1,0:T(4,128)S(1)} %get-tuple-element.35.pair, f32[9,4,128]{2,1,0:T(4,128)S(1)} %get-tuple-element.36.cross, f32[9,4,128]{2,1,0:T(4,128)S(1)} %collective-permute-done.from_pair, ...), custom_call_target="tpu_custom_call" | custom-call | flops 8388608 | bytes 1048576 | tf_op jit(solution)/shard_map/wrap_rhs/pallas_call | solution.py:831
  6.3 4.7 %collective-permute-start.4 = (f32[4,8,128]{2,1,0:T(8,128)S(1)}, f32[4,8,128]{2,1,0:T(8,128)S(1)}, u32[]{:S(2)}, u32[]{:S(2)}) collective-permute-start(f32[4,8,128]{2,1,0:T(8,128)S(1)} %get-tuple-element.43.after.refs_0_), channel_id=1, source_target_pairs={{0,24},{8,16},{16,8},{24,0},{1,25},{9,17},{17,9},{25,1},{2,26},{10... | collective-permute-start | bytes 49160 | tf_op jit(solution)/shard_map/ppermute | solution.py:846
  10.9 0.6 %collective-permute-start.2 = (f32[4,8,128]{2,1,0:T(8,128)S(1)}, f32[4,8,128]{2,1,0:T(8,128)S(1)}, u32[]{:S(2)}, u32[]{:S(2)}) collective-permute-start(f32[4,8,128]{2,1,0:T(8,128)S(1)} %get-tuple-element.43.after.refs_0_), channel_id=1, source_target_pairs={{0,8},{8,0},{16,24},{24,16},{1,9},{9,1},{17,25},{25,17},{2,10},{10... | collective-permute-start | bytes 49160 | tf_op jit(solution)/shard_map/ppermute | solution.py:846
  11.6 1.4 %wall.1 = (f32[2,125,8,128]{3,2,1,0:T(8,128)S(1)}, f32[125,8,128]{2,1,0:T(8,128)S(1)}, f32[1,75,8,128]{3,2,1,0:T(8,128)S(1)}, f32[100,8,128]{2,1,0:T(8,128)S(1)}...) custom-call(f32[2,2,45,8,128]{4,3,2,1,0:T(8,128)S(1)} %get-tuple-element.46.coefs, ...), custom_call_target="tpu_custom_call" | custom-call | flops 20971520 | bytes 1048576 | tf_op jit(solution)/shard_map/wall/pallas_call | solution.py:831
  13.0 4.0 %all-gather = f32[200,4,128]{2,1,0:T(4,128)S(1)} all-gather(f32[100,4,128]{2,1,0:T(4,128)S(1)} %get-tuple-element.53), channel_id=2, replica_groups={{0,1},{2,3},{4,5},{6,7},{8,9},{10,11},{12,13},{14,15},{16,17},{18,19},{..., dimensions={0}, use_global_device_ids=true | all-gather | bytes 614400 | tf_op jit(solution)/shard_map/all_gather | solution.py:911
  17.0 0.3 merge_0.1
  17.3 2.0 %collective-permute-start.7 = (f32[100,4,128]{2,1,0:T(4,128)S(1)}, f32[100,4,128]{2,1,0:T(4,128)S(1)}, u32[]{:S(2)}, u32[]{:S(2)}) collective-permute-start(f32[100,4,128]{2,1,0:T(4,128)S(1)} %get-tuple-element.56.refs_0_), channel_id=1, source_target_pairs={{0,2},{1,3},{2,0},{3,1},{4,6},{5,7},{6,4},{7,5},{8,10},{9,11},{10,... | collective-permute-start | bytes 614408 | tf_op jit(solution)/shard_map/ppermute | solution.py:846
  19.3 0.1 tail.1.refs_6_
  19.4 1.7 %cycle.1 = (f32[10,4,128]{2,1,0:T(4,128)S(1)}, f32[20,8,128]{2,1,0:T(8,128)S(1)}, f32[5,8,128]{2,1,0:T(8,128)S(1)}) custom-call(f32[4,8,128]{2,1,0:T(8,128)S(1)} %get-tuple-element.43.after.refs_0_, f32[4,8,128]{2,1,0:T(8,128)S(1)} %collective-permute-done.2.refs_1_, f32[4,8,128]{2,1,0:T(8,128)S(1)} %collective-permute-done.3.refs_2_, ...), custom_call_target="tpu_custom_call" | custom-call | flops 10485760 | bytes 1048576 | tf_op jit(solution)/shard_map/cycle/pallas_call | solution.py:831
  21.2 0.1 collective-permute-start.5
  21.2 1.2 %collective-permute-done.5.refs_1_ = f32[10,4,128]{2,1,0:T(4,128)S(1)} collective-permute-done((f32[10,4,128]{2,1,0:T(4,128)S(1)}, f32[10,4,128]{2,1,0:T(4,128)S(1)}, u32[]{:S(2)}, u32[]{:S(2)}) %collective-permute-start.5) | collective-permute-done | bytes 20512 | tf_op jit(solution)/shard_map/ppermute | solution.py:846
  22.5 0.2 collective-permute-start.6
  22.6 2.1 %collective-permute-done.7.refs_1_ = f32[100,4,128]{2,1,0:T(4,128)S(1)} collective-permute-done((f32[100,4,128]{2,1,0:T(4,128)S(1)}, f32[100,4,128]{2,1,0:T(4,128)S(1)}, u32[]{:S(2)}, u32[]{:S(2)}) %collective-permute-start.7) | collective-permute-done | bytes 204832 | tf_op jit(solution)/shard_map/ppermute | solution.py:846
  24.8 0.5 %merge_1.1 = (f32[125,4,128]{2,1,0:T(4,128)S(1)}, f32[100,4,128]{2,1,0:T(4,128)S(1)}) custom-call(f32[100,4,128]{2,1,0:T(4,128)S(1)} %get-tuple-element.56.refs_0_, f32[100,4,128]{2,1,0:T(4,128)S(1)} %collective-permute-done.7.refs_1_), custom_call_target="tpu_custom_call" | custom-call | flops 4194304 | bytes 1048576 | tf_op jit(solution)/shard_map/merge_1/pallas_call | solution.py:831
  25.3 1.1 %collective-permute-done.6.refs_1_ = f32[10,4,128]{2,1,0:T(4,128)S(1)} collective-permute-done((f32[10,4,128]{2,1,0:T(4,128)S(1)}, f32[10,4,128]{2,1,0:T(4,128)S(1)}, u32[]{:S(2)}, u32[]{:S(2)}) %collective-permute-start.6) | collective-permute-done | bytes 20512 | tf_op jit(solution)/shard_map/ppermute | solution.py:846
  26.4 1.6 %collective-permute-start.8 = (f32[30,4,128]{2,1,0:T(4,128)S(1)}, f32[30,4,128]{2,1,0:T(4,128)S(1)}, u32[]{:S(2)}, u32[]{:S(2)}) collective-permute-start(f32[30,4,128]{2,1,0:T(4,128)S(1)} %get-tuple-element.59.after.refs_0_), channel_id=1, source_target_pairs={{0,4},{1,5},{2,6},{3,7},{4,0},{5,1},{6,2},{7,3},{8,12},{9,13},{10,... | collective-permute-start | bytes 184328 | tf_op jit(solution)/shard_map/ppermute | solution.py:846
  27.9 0.1 wall_tail.1.refs_9_
  28.1 2.6 %collective-permute-done.8.refs_1_ = f32[30,4,128]{2,1,0:T(4,128)S(1)} collective-permute-done((f32[30,4,128]{2,1,0:T(4,128)S(1)}, f32[30,4,128]{2,1,0:T(4,128)S(1)}, u32[]{:S(2)}, u32[]{:S(2)}) %collective-permute-start.8) | collective-permute-done | bytes 61472 | tf_op jit(solution)/shard_map/ppermute | solution.py:846
  30.6 0.8 %finish.1 = f32[5,4,8,128]{3,2,1,0:T(8,128)} custom-call(f32[30,4,128]{2,1,0:T(4,128)S(1)} %get-tuple-element.59.after.refs_0_, f32[30,4,128]{2,1,0:T(4,128)S(1)} %collective-permute-done.8.refs_1_, f32[100,4,128]{2,1,0:T(4,128)S(1)} %get-tuple-element.58.refs_3_.refs_2_, f32[125,4,128]{2,1,0:T(4,128)S(1)} %get-tuple-element.54.refs_2_.refs_3_, ...), custom_call_target="tpu_custom_call" | custom-call | flops 4194304 | bytes 1048576 | tf_op jit(solution)/shard_map/finish/pallas_call | solution.py:831
  (9 shorter events, 0.1 us)
Async XLA Ops:
  1.0 4.3 %collective-permute-start = (f32[9,4,128]{2,1,0:T(4,128)S(1)}, f32[9,4,128]{2,1,0:T(4,128)S(1)}, u32[]{:S(2)}, u32[]{:S(2)}) collective-permute-start(f32[9,4,128]{2,1,0:T(4,128)S(1)} %get-tuple-element.35.pair), channel_id=1, source_target_pairs={{0,1},{1,0},{2,3},{3,2},{4,5},{5,4},{6,7},{7,6},{8,9},{9,8},{10,11... | collective-permute-start | bytes 55304 | tf_op jit(solution)/shard_map/ppermute | solution.py:846
  1.5 3.8 %collective-permute-start.1 = (f32[9,4,128]{2,1,0:T(4,128)S(1)}, f32[9,4,128]{2,1,0:T(4,128)S(1)}, u32[]{:S(2)}, u32[]{:S(2)}) collective-permute-start(f32[9,4,128]{2,1,0:T(4,128)S(1)} %get-tuple-element.36.cross), channel_id=1, source_target_pairs={{1,2},{3,4},{5,6},{2,1},{4,3},{6,5},{9,10},{11,12},{13,14},{10,9},... | collective-permute-start | bytes 55304 | tf_op jit(solution)/shard_map/ppermute | solution.py:857
  6.3 10.7 %collective-permute-start.4 = (f32[4,8,128]{2,1,0:T(8,128)S(1)}, f32[4,8,128]{2,1,0:T(8,128)S(1)}, u32[]{:S(2)}, u32[]{:S(2)}) collective-permute-start(f32[4,8,128]{2,1,0:T(8,128)S(1)} %get-tuple-element.43.after.refs_0_), channel_id=1, source_target_pairs={{0,24},{8,16},{16,8},{24,0},{1,25},{9,17},{17,9},{25,1},{2,26},{10... | collective-permute-start | bytes 49160 | tf_op jit(solution)/shard_map/ppermute | solution.py:846
  10.9 6.1 %collective-permute-start.3 = (f32[4,8,128]{2,1,0:T(8,128)S(1)}, f32[4,8,128]{2,1,0:T(8,128)S(1)}, u32[]{:S(2)}, u32[]{:S(2)}) collective-permute-start(f32[4,8,128]{2,1,0:T(8,128)S(1)} %get-tuple-element.43.after.refs_0_), channel_id=1, source_target_pairs={{0,16},{8,24},{16,0},{24,8},{1,17},{9,25},{17,1},{25,9},{2,18},{10... | collective-permute-start | bytes 49160 | tf_op jit(solution)/shard_map/ppermute | solution.py:846
  10.9 6.1 %collective-permute-start.2 = (f32[4,8,128]{2,1,0:T(8,128)S(1)}, f32[4,8,128]{2,1,0:T(8,128)S(1)}, u32[]{:S(2)}, u32[]{:S(2)}) collective-permute-start(f32[4,8,128]{2,1,0:T(8,128)S(1)} %get-tuple-element.43.after.refs_0_), channel_id=1, source_target_pairs={{0,8},{8,0},{16,24},{24,16},{1,9},{9,1},{17,25},{25,17},{2,10},{10... | collective-permute-start | bytes 49160 | tf_op jit(solution)/shard_map/ppermute | solution.py:846
  17.3 7.4 %collective-permute-start.7 = (f32[100,4,128]{2,1,0:T(4,128)S(1)}, f32[100,4,128]{2,1,0:T(4,128)S(1)}, u32[]{:S(2)}, u32[]{:S(2)}) collective-permute-start(f32[100,4,128]{2,1,0:T(4,128)S(1)} %get-tuple-element.56.refs_0_), channel_id=1, source_target_pairs={{0,2},{1,3},{2,0},{3,1},{4,6},{5,7},{6,4},{7,5},{8,10},{9,11},{10,... | collective-permute-start | bytes 614408 | tf_op jit(solution)/shard_map/ppermute | solution.py:846
  21.2 1.3 %collective-permute-start.5 = (f32[10,4,128]{2,1,0:T(4,128)S(1)}, f32[10,4,128]{2,1,0:T(4,128)S(1)}, u32[]{:S(2)}, u32[]{:S(2)}) collective-permute-start(f32[10,4,128]{2,1,0:T(4,128)S(1)} %get-tuple-element.52.refs_0_), channel_id=1, source_target_pairs={{0,1},{1,0},{2,3},{3,2},{4,5},{5,4},{6,7},{7,6},{8,9},{9,8},{10,11... | collective-permute-start | bytes 61448 | tf_op jit(solution)/shard_map/ppermute | solution.py:846
  22.5 3.8 %collective-permute-start.6 = (f32[10,4,128]{2,1,0:T(4,128)S(1)}, f32[10,4,128]{2,1,0:T(4,128)S(1)}, u32[]{:S(2)}, u32[]{:S(2)}) collective-permute-start(f32[10,4,128]{2,1,0:T(4,128)S(1)} %get-tuple-element.55.refs_0_), channel_id=1, source_target_pairs={{0,2},{1,3},{2,0},{3,1},{4,6},{5,7},{6,4},{7,5},{8,10},{9,11},{10,... | collective-permute-start | bytes 61448 | tf_op jit(solution)/shard_map/ppermute | solution.py:846
  26.4 4.3 %collective-permute-start.8 = (f32[30,4,128]{2,1,0:T(4,128)S(1)}, f32[30,4,128]{2,1,0:T(4,128)S(1)}, u32[]{:S(2)}, u32[]{:S(2)}) collective-permute-start(f32[30,4,128]{2,1,0:T(4,128)S(1)} %get-tuple-element.59.after.refs_0_), channel_id=1, source_target_pairs={{0,4},{1,5},{2,6},{3,7},{4,0},{5,1},{6,2},{7,3},{8,12},{9,13},{10,... | collective-permute-start | bytes 184328 | tf_op jit(solution)/shard_map/ppermute | solution.py:846
